TPU v7x, 512 devices: a whole 4x4x16 slice. The times are simulated.
512 devices in a mesh: queue: 32 (over y_hi, z), mp: 16 (over x, y_lo, core).
Axes of the slice: x: 4, y: 4 (y_hi: 2, y_lo: 2; y = y_hi * 2 + y_lo), z: 16, core: 2. Of those that a mesh axis runs over, the one named last changes fastest.
Arguments:
- latents: bfloat16 [32, 768, 1152], P('queue', 'mp'), may hold values from -6 to 6
- fresh_noise: bfloat16 [768, 1152], P('mp'), may hold values from -6 to 6
- levels: int32 [32], P('queue'), may hold values from 0 to 31, each once
- modulation: float32 [32, 6, 1152], replicated, may hold values from -1 to 11, as said below
- head_map: int32 [16], P('mp'), may hold values from 0 to 15, each once
- window: int32 [16], replicated, may hold values from 1 to 2, as said below
- qkv_weight: bfloat16 [1152, 3456], P(None, 'mp'), may hold values from -0.1875 to 0.1875
- out_weight: bfloat16 [1152, 1152], P('mp'), may hold values from -0.1875 to 0.1875
- fc1_weight: bfloat16 [1152, 4608], P(None, 'mp'), may hold values from -0.1875 to 0.1875
- fc2_weight: bfloat16 [4608, 1152], P('mp'), may hold values from -0.09375 to 0.09375
Outputs:
- queue_next: bfloat16 [32, 768, 1152], P('queue', 'mp')
Inputs may be any that keep to these rules, and one draw needn't show every extreme that they name: `window`: every head's half-width lies in 1..2 and some head has exactly 2. `modulation`: shift entries in -1..1, gates in 0.3..1.5, scale entries in -0.5..11.
All inputs are finite; a program needn't handle non-finite values.
Results may differ from a plain program's by a relative error of at most 0.025.
Values may be sent and summed in bfloat16 or wider, within the bound.
No kernel may reach another device: no remote copies, remote signals or barrier semaphores. Data moves between devices by JAX's collectives and lax.ppermute only.
A program may use at most 64 MiB of HBM per device.

v0:
```python
import jax
import jax.numpy as jnp
from jax import lax
from jax.sharding import PartitionSpec as P

WMAX = 2


def shifted(value, axis, steps):
    count = lax.axis_size(axis)
    first, last = (max(0, -steps), min(count, count - steps))
    return lax.ppermute(value, axis, [(source, source + steps) for source in range(first, last)])


def modulate(values, shift, scale):
    floats = values.astype(jnp.float32)
    center = jnp.mean(floats, axis=-1, keepdims=True)
    spread = jnp.mean((floats - center) ** 2, axis=-1, keepdims=True)
    return ((floats - center) * lax.rsqrt(spread + 1e-06) * (1.0 + scale) + shift).astype(
        jnp.bfloat16
    )


def fetch_frame(payload, distance):
    return shifted(payload, "queue", distance)


def per_device(
    latents,
    fresh_noise,
    levels,
    modulation,
    head_map,
    window,
    qkv_weight,
    out_weight,
    fc1_weight,
    fc2_weight,
):
    local_tokens = latents[0]
    level_count = modulation.shape[0]
    head_total = window.shape[0]
    local_heads = head_map.shape[0]
    head_size = qkv_weight.shape[1] // (3 * local_heads)
    picked = jnp.sum(
        jnp.where(jnp.arange(level_count)[:, None, None] == levels[0], modulation, 0.0), axis=0
    )
    half_width = jnp.sum(
        jnp.where(head_map[:, None] == jnp.arange(head_total)[None, :], window[None, :], 0), axis=1
    )
    queue_pos = lax.axis_index("queue")
    queue_len = lax.axis_size("queue")
    normed = modulate(local_tokens, picked[0], picked[1])
    qkv = jnp.dot(
        lax.all_gather(normed, "mp", axis=0, tiled=True),
        qkv_weight,
        preferred_element_type=jnp.float32,
    ).astype(jnp.bfloat16)
    frame_tokens = qkv.shape[0]
    split = qkv.reshape(frame_tokens, local_heads, 3, head_size)
    query = split[:, :, 0].astype(jnp.float32)
    keyval = jnp.stack([split[:, :, 1], split[:, :, 2]]).reshape(
        2, frame_tokens, local_heads * head_size
    )
    arrived = {0: keyval}
    for distance in range(1, WMAX + 1):
        arrived[-distance] = fetch_frame(keyval, distance)
        arrived[distance] = fetch_frame(keyval, -distance)
    scores = []
    valids = []
    value_list = []
    for offset in range(-WMAX, WMAX + 1):
        payload = (
            arrived[offset].reshape(2, frame_tokens, local_heads, head_size).astype(jnp.float32)
        )
        scores.append(jnp.sum(query * payload[0], axis=-1) / jnp.sqrt(jnp.float32(head_size)))
        target = queue_pos + offset
        inside = (target >= 0) & (target < queue_len)
        valids.append(
            jnp.broadcast_to(
                (inside & (abs(offset) <= half_width))[None, :], (frame_tokens, local_heads)
            )
        )
        value_list.append(payload[1])
    scores = jnp.stack(scores)
    valids = jnp.stack(valids)
    masked = jnp.where(valids, scores, jnp.float32(-1e30))
    top = jnp.max(masked, axis=0, keepdims=True)
    expo = jnp.where(valids, jnp.exp(masked - top), jnp.float32(0.0))
    probs = expo / jnp.sum(expo, axis=0, keepdims=True)
    attended = jnp.sum(probs[..., None] * jnp.stack(value_list), axis=0).astype(jnp.bfloat16)
    attended = attended.reshape(frame_tokens, local_heads * head_size)
    block = attended
    attn = lax.psum_scatter(
        jnp.dot(block, out_weight, preferred_element_type=jnp.float32).astype(jnp.bfloat16),
        "mp",
        scatter_dimension=0,
        tiled=True,
    ).astype(jnp.float32)
    resid = (local_tokens.astype(jnp.float32) + picked[2] * attn).astype(jnp.bfloat16)
    normed_two = modulate(resid, picked[3], picked[4])
    hidden = jax.nn.gelu(
        jnp.dot(
            lax.all_gather(normed_two, "mp", axis=0, tiled=True),
            fc1_weight,
            preferred_element_type=jnp.float32,
        ),
        approximate=True,
    ).astype(jnp.bfloat16)
    block = hidden
    mlp = lax.psum_scatter(
        jnp.dot(block, fc2_weight, preferred_element_type=jnp.float32).astype(jnp.bfloat16),
        "mp",
        scatter_dimension=0,
        tiled=True,
    ).astype(jnp.float32)
    block_out = (resid.astype(jnp.float32) + picked[5] * mlp).astype(jnp.bfloat16)
    moved = shifted(block_out, "queue", 1)
    return jnp.where(queue_pos == 0, fresh_noise, moved)[None]


def solution(mesh):
    in_specs = (
        P("queue", "mp", None),
        P("mp", None),
        P("queue"),
        P(),
        P("mp"),
        P(),
        P(None, "mp"),
        P("mp", None),
        P(None, "mp"),
        P("mp", None),
    )
    out_specs = P("queue", "mp", None)
    return jax.shard_map(
        per_device, mesh=mesh, in_specs=in_specs, out_specs=out_specs, check_vma=False
    )
```

profile of v0, /device:TPU:16, one launch (start us, length us, event | category | flops | bytes accessed | tf_op | source)
XLA Modules:
  0.0 294.3 jit_solution(7334173166625640876)
XLA Ops:
  6.5 0.0 copy-start
  6.5 0.0 all-gather.3.cloned.1.call-start
  7.3 1.0 convert_reduce_fusion.1
  8.3 1.1 fusion.23
  9.4 1.4 select_reduce_fusion
  10.8 0.1 slice_reduce_fusion.1
  10.9 0.0 copy-done.1
  10.9 0.8 fusion.26
  11.7 0.0 all-gather.3.cloned.1.call-update
  11.7 0.0 reduce-scatter.3.cloned.1.call-start
  11.7 45.2 %all-gather.3.cloned.1.call-done = bf16[768,1152]{1,0:T(8,128)(2,1)} async-done(((bf16[48,1152]{1,0:T(8,128)(2,1)}), bf16[768,1152]{1,0:T(8,128)(2,1)}) %all-gather.3.cloned.1.call-update) | async-done | bytes 1769488 | tf_op jit(solution)/shard_map/all_gather | solution.py:55
  56.9 0.0 copy-done.5
  56.9 2.2 convolution_convert_fusion.2
  59.2 0.0 copy-start.6
  59.3 6.9 %collective-permute-start.3 = (bf16[2,768,72]{1,2,0:T(8,128)(2,1)S(1)}, bf16[2,768,72]{1,2,0:T(8,128)(2,1)S(1)}, u32[]{:S(2)}, u32[]{:S(2)}) collective-permute-start(bf16[2,768,72]{1,2,0:T(8,128)(2,1)S(1)} %get-tuple-element.21), channel_id=1, source_target_pairs={{32,0},{48,16},{64,32},{80,48},{96,64},{112,80},{128,96},{144,112}... | collective-permute-start | bytes 663560 | tf_op jit(solution)/shard_map/ppermute | solution.py:12
  66.2 3.3 %collective-permute-start.2 = (bf16[2,768,72]{1,2,0:T(8,128)(2,1)S(1)}, bf16[2,768,72]{1,2,0:T(8,128)(2,1)S(1)}, u32[]{:S(2)}, u32[]{:S(2)}) collective-permute-start(bf16[2,768,72]{1,2,0:T(8,128)(2,1)S(1)} %get-tuple-element.21), channel_id=1, source_target_pairs={{16,0},{32,16},{48,32},{64,48},{80,64},{96,80},{112,96},{128,112},... | collective-permute-start | bytes 663560 | tf_op jit(solution)/shard_map/ppermute | solution.py:12
  69.5 2.6 collective-permute-start.1
  72.0 2.0 collective-permute-start
  74.7 0.0 copy-done.6
  74.7 0.7 fusion.46
  77.8 0.0 collective-permute-done.3
  77.8 2.9 collective-permute-done.2
  80.8 7.3 %collective-permute-done.1 = bf16[2,768,72]{1,2,0:T(8,128)(2,1)S(1)} collective-permute-done((bf16[2,768,72]{1,2,0:T(8,128)(2,1)S(1)}, bf16[2,768,72]{1,2,0:T(8,128)(2,1)S(1)}, u32[]{:S(2)}, u32[]{:S(2)}) %collective-permute-start.1) | collective-permute-done | bytes 221216 | tf_op jit(solution)/shard_map/ppermute | solution.py:12
  88.1 0.0 collective-permute-done
  88.1 0.1 fusion.33
  88.5 0.1 fusion.42
  88.6 0.0 copy-start.2
  88.7 0.1 multiply_reduce_fusion
  88.8 0.7 copy-done.2
  89.5 1.9 convolution_convert_fusion
  91.4 0.0 reduce-scatter.3.cloned.1.call-update
  91.4 0.0 all-gather.5.cloned.1.call-start
  91.5 66.4 %reduce-scatter.3.cloned.1.call-done = bf16[48,1152]{1,0:T(8,128)(2,1)} async-done(((bf16[768,1152]{1,0:T(8,128)(2,1)}), bf16[48,1152]{1,0:T(8,128)(2,1)}) %reduce-scatter.3.cloned.1.call-update) | async-done | bytes 110608 | tf_op jit(solution)/shard_map/reduce_scatter | solution.py:94
  157.8 1.0 convert_reduce_fusion
  158.9 0.2 fusion.19
  159.1 0.8 fusion.22
  159.9 0.0 all-gather.5.cloned.1.call-update
  159.9 0.0 reduce-scatter.5.cloned.1.call-start
  159.9 40.0 %all-gather.5.cloned.1.call-done = bf16[768,1152]{1,0:T(8,128)(2,1)} async-done(((bf16[48,1152]{1,0:T(8,128)(2,1)}), bf16[768,1152]{1,0:T(8,128)(2,1)}) %all-gather.5.cloned.1.call-update) | async-done | bytes 1769488 | tf_op jit(solution)/shard_map/all_gather | solution.py:104
  200.0 0.0 copy-done
  200.0 0.0 copy-done.4
  200.0 4.9 %convolution_convert_fusion.1 = bf16[768,1152]{1,0:T(8,128)(2,1)} fusion(bf16[288,1152]{1,0:T(8,128)(2,1)S(1)} %copy-done, bf16[768,1152]{1,0:T(8,128)(2,1)} %all-gather.5.cloned.1.call-done, bf16[1152,288]{0,1:T(8,128)(2,1)S(1)} %copy-done.4), kind=kOutput, calls=%fused_computation.1 | convolution fusion | flops 1022091264 | bytes 4866048 | tf_op jit(solution)/shard_map/dot_general | solution.py:112
  204.9 0.0 reduce-scatter.5.cloned.1.call-update
  204.9 71.0 %reduce-scatter.5.cloned.1.call-done = bf16[48,1152]{1,0:T(8,128)(2,1)} async-done(((bf16[768,1152]{1,0:T(8,128)(2,1)}), bf16[48,1152]{1,0:T(8,128)(2,1)}) %reduce-scatter.5.cloned.1.call-update) | async-done | bytes 110608 | tf_op jit(solution)/shard_map/reduce_scatter | solution.py:111
  275.9 0.9 fusion.28
  276.9 3.5 %collective-permute-start.4 = (bf16[48,1152]{1,0:T(8,128)(2,1)S(1)}, bf16[48,1152]{1,0:T(8,128)(2,1)S(1)}, u32[]{:S(2)}, u32[]{:S(2)}) collective-permute-start(bf16[48,1152]{1,0:T(8,128)(2,1)S(1)} %fusion.28), channel_id=1, source_target_pairs={{0,16},{16,32},{32,48},{48,64},{64,80},{80,96},{96,112},{112,128},... | collective-permute-start | bytes 331784 | tf_op jit(solution)/shard_map/ppermute | solution.py:12
  280.3 6.8 %collective-permute-done.4 = bf16[48,1152]{1,0:T(8,128)(2,1)S(1)} collective-permute-done((bf16[48,1152]{1,0:T(8,128)(2,1)S(1)}, bf16[48,1152]{1,0:T(8,128)(2,1)S(1)}, u32[]{:S(2)}, u32[]{:S(2)}) %collective-permute-start.4) | collective-permute-done | bytes 110624 | tf_op jit(solution)/shard_map/ppermute | solution.py:12
  287.1 0.7 select_bitcast_fusion
  (49 shorter events, 0.7 us)
Async XLA Ops:
  6.5 193.4 %copy-start = (bf16[288,1152]{1,0:T(8,128)(2,1)S(1)}, bf16[288,1152]{1,0:T(8,128)(2,1)}, u32[]{:S(2)}) copy-start(bf16[288,1152]{1,0:T(8,128)(2,1)} %param.19) | copy-start | bytes 1990660
  6.5 4.4 %copy-start.1 = (bf16[1,48,1152]{2,1,0:T(8,128)(2,1)S(1)}, bf16[1,48,1152]{2,1,0:T(8,128)(2,1)}, u32[]{:S(2)}) copy-start(bf16[1,48,1152]{2,1,0:T(8,128)(2,1)} %param.10) | copy-start | bytes 331780
  6.5 50.4 %copy-start.5 = (bf16[1152,216]{0,1:T(8,128)(2,1)S(1)}, bf16[1152,216]{0,1:T(8,128)(2,1)}, u32[]{:S(2)}) copy-start(bf16[1152,216]{0,1:T(8,128)(2,1)} %param.16) | copy-start | bytes 1492996
  6.5 50.4 %all-gather.3.cloned.1.call-start = ((), (), s32[]{:S(2)}) async-start(), calls=%async_computation.2 | async-start | bytes 1880064 | tf_op jit(solution)/shard_map/all_gather | solution.py:55
  11.7 146.2 %reduce-scatter.3.cloned.1.call-start = ((), (), s32[]{:S(2)}) async-start(), calls=%async_computation.3 | async-start | bytes 1880064 | tf_op jit(solution)/shard_map/reduce_scatter | solution.py:94
  59.2 15.5 %copy-start.6 = (s32[16]{0:T(128)S(1)}, s32[16]{0:T(128)}, u32[]{:S(2)}) copy-start(s32[16]{0:T(128)} %param.15) | copy-start | bytes 196
  59.3 18.5 %collective-permute-start.3 = (bf16[2,768,72]{1,2,0:T(8,128)(2,1)S(1)}, bf16[2,768,72]{1,2,0:T(8,128)(2,1)S(1)}, u32[]{:S(2)}, u32[]{:S(2)}) collective-permute-start(bf16[2,768,72]{1,2,0:T(8,128)(2,1)S(1)} %get-tuple-element.21), channel_id=1, source_target_pairs={{32,0},{48,16},{64,32},{80,48},{96,64},{112,80},{128,96},{144,112}... | collective-permute-start | bytes 663560 | tf_op jit(solution)/shard_map/ppermute | solution.py:12
  66.2 14.6 %collective-permute-start.2 = (bf16[2,768,72]{1,2,0:T(8,128)(2,1)S(1)}, bf16[2,768,72]{1,2,0:T(8,128)(2,1)S(1)}, u32[]{:S(2)}, u32[]{:S(2)}) collective-permute-start(bf16[2,768,72]{1,2,0:T(8,128)(2,1)S(1)} %get-tuple-element.21), channel_id=1, source_target_pairs={{16,0},{32,16},{48,32},{64,48},{80,64},{96,80},{112,96},{128,112},... | collective-permute-start | bytes 663560 | tf_op jit(solution)/shard_map/ppermute | solution.py:12
  69.5 18.6 %collective-permute-start.1 = (bf16[2,768,72]{1,2,0:T(8,128)(2,1)S(1)}, bf16[2,768,72]{1,2,0:T(8,128)(2,1)S(1)}, u32[]{:S(2)}, u32[]{:S(2)}) collective-permute-start(bf16[2,768,72]{1,2,0:T(8,128)(2,1)S(1)} %get-tuple-element.21), channel_id=1, source_target_pairs={{0,16},{16,32},{32,48},{48,64},{64,80},{80,96},{96,112},{112,128},... | collective-permute-start | bytes 663560 | tf_op jit(solution)/shard_map/ppermute | solution.py:12
  72.0 16.1 %collective-permute-start = (bf16[2,768,72]{1,2,0:T(8,128)(2,1)S(1)}, bf16[2,768,72]{1,2,0:T(8,128)(2,1)S(1)}, u32[]{:S(2)}, u32[]{:S(2)}) collective-permute-start(bf16[2,768,72]{1,2,0:T(8,128)(2,1)S(1)} %get-tuple-element.21), channel_id=1, source_target_pairs={{0,32},{16,48},{32,64},{48,80},{64,96},{80,112},{96,128},{112,144}... | collective-permute-start | bytes 663560 | tf_op jit(solution)/shard_map/ppermute | solution.py:12
  88.6 0.9 copy-start.2
  91.4 108.6 %copy-start.4 = (bf16[1152,288]{0,1:T(8,128)(2,1)S(1)}, bf16[1152,288]{0,1:T(8,128)(2,1)}, u32[]{:S(2)}) copy-start(bf16[1152,288]{0,1:T(8,128)(2,1)} %param.18) | copy-start | bytes 1990660
  91.4 108.5 %all-gather.5.cloned.1.call-start = ((), (), s32[]{:S(2)}) async-start(), calls=%async_computation.4 | async-start | bytes 1880064 | tf_op jit(solution)/shard_map/all_gather | solution.py:104
  159.9 116.0 %reduce-scatter.5.cloned.1.call-start = ((), (), s32[]{:S(2)}) async-start(), calls=%async_computation.5 | async-start | bytes 1880064 | tf_op jit(solution)/shard_map/reduce_scatter | solution.py:111
  204.9 82.2 %copy-start.3 = (bf16[48,1152]{1,0:T(8,128)(2,1)S(1)}, bf16[48,1152]{1,0:T(8,128)(2,1)}, u32[]{:S(2)}) copy-start(bf16[48,1152]{1,0:T(8,128)(2,1)} %param.11) | copy-start | bytes 331780
  276.9 10.3 %collective-permute-start.4 = (bf16[48,1152]{1,0:T(8,128)(2,1)S(1)}, bf16[48,1152]{1,0:T(8,128)(2,1)S(1)}, u32[]{:S(2)}, u32[]{:S(2)}) collective-permute-start(bf16[48,1152]{1,0:T(8,128)(2,1)S(1)} %fusion.28), channel_id=1, source_target_pairs={{0,16},{16,32},{32,48},{48,64},{64,80},{80,96},{96,112},{112,128},... | collective-permute-start | bytes 331784 | tf_op jit(solution)/shard_map/ppermute | solution.py:12
Sparse Core Ops, SparseCore 0:
  11.8 45.0 all-gather.2
  91.5 66.2 reduce-scatter.2
  160.2 39.7 all-gather.4
  205.0 70.8 reduce-scatter.4
where the time goes:
time: 295 us; the launch traced here: 294 us
  waiting for transfers between devices  240 us (81%)
  starting transfers between devices  18.3 us (6%)
  between operations  17 us (6%)
  other arithmetic  9.16 us (3%)
  matrix products  9.05 us (3%)
    reduce_scatter x1, waiting for transfers between devices, per_device(): lax.psum_scatter(jnp.dot(block, fc2_weight, preferred_element_type=jnp.fl...  71 us
    reduce_scatter x1, waiting for transfers between devices, per_device(): lax.psum_scatter(jnp.dot(block, out_weight, preferred_element_type=jnp.fl...  66.4 us
    all_gather x1, waiting for transfers between devices, per_device(): lax.all_gather(normed, 'mp', axis=0, tiled=True)  45.2 us
    all_gather x1, waiting for transfers between devices, per_device(): lax.all_gather(normed_two, 'mp', axis=0, tiled=True)  40 us
    ppermute x5, starting transfers between devices, shifted(): lax.ppermute(value, axis, [(source, source + steps) for source in range(f...  18.2 us
    ppermute x5, waiting for transfers between devices, shifted(): lax.ppermute(value, axis, [(source, source + steps) for source in range(f...  17 us
  transfers between devices with their start and end apart: 9, of which 7 were waited for; matrix products, arithmetic and copies ran while one was open for 0% of the time, Pallas kernels for 0%

commit v1 on v0

v1 whole, which is shorter than its diff:
```python
import jax
import jax.numpy as jnp
from jax import lax
from jax.experimental import pallas as pl
from jax.experimental.pallas import tpu as pltpu
from jax.sharding import Mesh
from jax.sharding import PartitionSpec as P

WMAX = 2
VMEM_LIMIT = 48 * 1024 * 1024
BF16, F32 = jnp.bfloat16, jnp.float32
SLOTS = ("yhi", "z")
SWAP = [(0, 1), (1, 0)]
FAR_Y = [(0, 3), (3, 0), (1, 2), (2, 1)]
PARAMS = pltpu.CompilerParams(vmem_limit_bytes=VMEM_LIMIT)


def normalise(floats, shift, scale):
    center = jnp.mean(floats, axis=-1, keepdims=True)
    spread = jnp.mean((floats - center) ** 2, axis=-1, keepdims=True)
    return ((floats - center) * lax.rsqrt(spread + 1e-06) * (1.0 + scale) + shift).astype(BF16)


def halves(value):
    high = value.astype(BF16)
    return high, (value - high.astype(F32)).astype(BF16)


def dot2(value, indicator):
    high, low = halves(value)
    return jnp.dot(high, indicator, preferred_element_type=F32) + jnp.dot(
        low, indicator, preferred_element_type=F32
    )


def qkv_kernel(head, width, tok_ref, mod_ref, w0, w1, w2, w3, q_ref, kv_ref, half_ref):
    normed = normalise(tok_ref[...].astype(F32), mod_ref[0:1, :], mod_ref[1:2, :])
    queries, keys, values = [], [], []
    lane = lax.broadcasted_iota(jnp.int32, half_ref.shape, 1)
    half = jnp.zeros(half_ref.shape, F32)
    for slot, weight in enumerate((w0, w1, w2, w3)):
        part = jnp.dot(normed, weight[0:width, :], preferred_element_type=F32)
        queries.append(part[:, :head])
        keys.append(part[:, head : 2 * head])
        values.append(part[:, 2 * head :])
        half = jnp.where(lane == slot, weight[width : width + 16, 0:128].astype(F32), half)
    q_ref[...] = jnp.concatenate(queries, axis=1).astype(BF16)
    kv_ref[...] = jnp.concatenate(keys + values, axis=1).astype(BF16)
    half_ref[...] = half


def attention_kernel(head, frames, frame_ref, half_ref, q_ref, k0, k1, k2, k3, k4, out_ref):
    rows, cols = q_ref.shape
    col = lax.broadcasted_iota(jnp.int32, (cols, 128), 0)
    lane = lax.broadcasted_iota(jnp.int32, (cols, 128), 1)
    gather = ((col >= lane * head) & (col < (lane + 1) * head)).astype(F32).astype(BF16)
    col = lax.broadcasted_iota(jnp.int32, (128, cols), 1)
    lane = lax.broadcasted_iota(jnp.int32, (128, cols), 0)
    spread = ((col >= lane * head) & (col < (lane + 1) * head)).astype(F32).astype(BF16)
    query = q_ref[...].astype(F32)
    half = half_ref[0:1, :]
    frame = frame_ref[0]
    keyvals = (k0, k1, k2, k3, k4)
    masked, valids = [], []
    for index, ref in enumerate(keyvals):
        offset = index - WMAX
        score = dot2(query * ref[:, :cols].astype(F32), gather) / (float(head) ** 0.5)
        target = frame + offset
        inside = ((target >= 0) & (target < frames)).astype(F32)
        valid = (inside * (half >= abs(offset)).astype(F32)) > 0.5
        valids.append(valid)
        masked.append(jnp.where(valid, score, -1e30))
    top = masked[0]
    for value in masked[1:]:
        top = jnp.maximum(top, value)
    expo = [jnp.where(valid, jnp.exp(value - top), 0.0) for valid, value in zip(valids, masked)]
    total = expo[0]
    for value in expo[1:]:
        total = total + value
    out = jnp.zeros((rows, cols), F32)
    for value, ref in zip(expo, keyvals):
        out = out + dot2(value / total, spread) * ref[:, cols:].astype(F32)
    out_ref[...] = out.astype(BF16)


def mlp_kernel(
    head, hidden, ylo_ref, att_ref, tok_ref, mod_ref, oa_ref, ob_ref, m0, m1, m2, m3, resid_ref, part_ref
):
    groups = att_ref.shape[0]
    ylo = ylo_ref[0]
    rows = tok_ref.shape[0]
    attn = jnp.zeros(tok_ref.shape, F32)
    for group in range(groups):
        for far in range(2):
            line = ylo if far == 0 else 1 - ylo
            for core, ref in enumerate((oa_ref, ob_ref)):
                slot = far * 2 + core
                block = att_ref[group, :, slot * head : (slot + 1) * head]
                attn = attn + jnp.dot(block, ref[group, line], preferred_element_type=F32)
    resid = (tok_ref[...].astype(F32) + mod_ref[2:3, :] * attn).astype(BF16)
    resid_ref[...] = resid
    normed = normalise(resid.astype(F32), mod_ref[3:4, :], mod_ref[4:5, :])
    total = jnp.zeros(tok_ref.shape, F32)
    for ref in (m0, m1, m2, m3):
        wide = lax.dot_general(
            normed, ref[hidden:, :], (((1,), (1,)), ((), ())), preferred_element_type=F32
        )
        active = jax.nn.gelu(wide, approximate=True).astype(BF16)
        total = total + jnp.dot(active, ref[:hidden, :], preferred_element_type=F32)
    part_ref[...] = total.astype(BF16)


def call(kernel, outs, smem, *args):
    specs = [pl.BlockSpec(memory_space=pltpu.SMEM)] * smem
    specs += [pl.BlockSpec(memory_space=pltpu.VMEM)] * (len(args) - smem)
    return pl.pallas_call(
        kernel,
        out_shape=outs,
        in_specs=specs,
        out_specs=jax.tree.map(lambda _: pl.BlockSpec(memory_space=pltpu.VMEM), outs),
        compiler_params=PARAMS,
    )(*args)


def per_device(
    latents,
    fresh_noise,
    levels,
    modulation,
    head_map,
    window,
    qkv_weight,
    out_weight,
    fc1_weight,
    fc2_weight,
):
    tokens, width = latents.shape[1:]
    level_count = modulation.shape[0]
    head = out_weight.shape[0]
    hidden = fc2_weight.shape[0]
    slots = lax.axis_size(SLOTS)
    slot = lax.axis_index(SLOTS)
    ylo = lax.axis_index("ylo").astype(jnp.int32)
    across = lax.axis_index("x")
    around = lax.axis_size("x")

    def slid(value, steps):
        return lax.ppermute(value, SLOTS, [(s, (s + steps) % slots) for s in range(slots)])

    half = jnp.sum(jnp.where(jnp.arange(window.shape[0]) == head_map[0], window, 0))
    own_w = jnp.concatenate(
        [qkv_weight, jnp.broadcast_to(half.astype(BF16), (16, qkv_weight.shape[1]))], axis=0
    )
    near_w = lax.ppermute(own_w, "ylo", SWAP)
    core_w = lax.ppermute(own_w, "core", SWAP)
    payload = jnp.concatenate(
        [latents[0], jnp.broadcast_to(levels.astype(BF16)[:, None], (16, width))], axis=0
    )
    moved = slid(payload, 1)
    far_w = lax.ppermute(core_w, ("yhi", "ylo"), FAR_Y)
    out_a = lax.all_gather(out_weight, ("x", "ylo"), axis=0, tiled=False).reshape(
        around, 2, head, width
    )
    own_m = jnp.concatenate([fc2_weight, fc1_weight.T], axis=0)
    core_m = lax.ppermute(own_m, "core", SWAP)

    tok = lax.all_gather(moved[:tokens], "x", axis=0, tiled=True)
    level = moved[tokens, 0].astype(jnp.int32)
    picked = jnp.sum(
        jnp.where(jnp.arange(level_count)[:, None, None] == level, modulation, 0.0), axis=0
    )
    rows = tok.shape[0]
    cols = 4 * head
    query, keyval, halfs = call(
        lambda *refs: qkv_kernel(head, width, *refs),
        (
            jax.ShapeDtypeStruct((rows, cols), BF16),
            jax.ShapeDtypeStruct((rows, 2 * cols), BF16),
            jax.ShapeDtypeStruct((16, 128), F32),
        ),
        0,
        tok,
        picked,
        own_w,
        core_w,
        near_w,
        far_w,
    )
    near_m = lax.ppermute(own_m, "ylo", SWAP)
    far_m = lax.ppermute(core_m, ("yhi", "ylo"), FAR_Y)
    arrived = [slid(keyval, 2), slid(keyval, 1), keyval, slid(keyval, -1), slid(keyval, -2)]
    out_b = lax.ppermute(out_a, "core", SWAP)
    frame = jnp.where(slot == 0, slots - 1, slot - 1).astype(jnp.int32)
    attended = call(
        lambda *refs: attention_kernel(head, slots, *refs),
        jax.ShapeDtypeStruct((rows, cols), BF16),
        1,
        frame[None],
        halfs,
        query,
        *arrived,
    )
    att = lax.all_gather(attended, "x", axis=0, tiled=False)
    resid, part = call(
        lambda *refs: mlp_kernel(head, hidden, *refs),
        (jax.ShapeDtypeStruct((rows, width), BF16), jax.ShapeDtypeStruct((rows, width), BF16)),
        1,
        ylo[None],
        att,
        tok,
        picked,
        out_a,
        out_b,
        own_m,
        core_m,
        near_m,
        far_m,
    )
    parts = lax.all_to_all(part, "x", 0, 0, tiled=True).reshape(around, tokens, width)
    mlp = jnp.sum(parts.astype(F32), axis=0)
    mine = lax.dynamic_slice_in_dim(resid, across * tokens, tokens, 0)
    block_out = (mine.astype(F32) + picked[5] * mlp).astype(BF16)
    return jnp.where(slot == 0, fresh_noise, block_out)[None]


def solution(mesh):
    split = Mesh(mesh.devices.reshape(2, 16, 4, 2, 2), ("yhi", "z", "x", "ylo", "core"))
    mp = ("x", "ylo", "core")
    in_specs = (
        P(SLOTS, mp, None),
        P(mp, None),
        P(SLOTS),
        P(),
        P(mp),
        P(),
        P(None, mp),
        P(mp, None),
        P(None, mp),
        P(mp, None),
    )
    return jax.shard_map(
        per_device, mesh=split, in_specs=in_specs, out_specs=P(SLOTS, mp, None), check_vma=False
    )
```

time: 295 us -> 195 us (0.66)
  the two profiles are of different devices: /device:TPU:16 before, /device:TPU:2 now
where the time goes in v1:
time: 195 us; the launch traced here: 194 us
  waiting for transfers between devices  86.7 us (44%)
  starting transfers between devices  38.2 us (20%)
  blocking collectives  26.3 us (13%)
  between operations  16.2 us (8%)
  local copies, waits for them, and re-layouts  12.3 us (6%)
  Pallas kernels  11 us (6%)
  other arithmetic  3.03 us (2%)
    all_gather x1, waiting for transfers between devices, per_device(): lax.all_gather(out_weight, ('x', 'ylo'), axis=0, tiled=False)  46.2 us
    ppermute x5, waiting for transfers between devices, slid(): lax.ppermute(value, SLOTS, [(s, (s + steps) % slots) for s in range(slots)])  33.6 us
    ppermute x5, starting transfers between devices, slid(): lax.ppermute(value, SLOTS, [(s, (s + steps) % slots) for s in range(slots)])  13.5 us
    all_gather x1, blocking collectives, per_device(): tok = lax.all_gather(moved[:tokens], 'x', axis=0, tiled=True)  13.2 us
    all_gather x1, blocking collectives, per_device(): att = lax.all_gather(attended, 'x', axis=0, tiled=False)  13.1 us
    pallas_call x3, Pallas kernels, call(): pl.pallas_call(kernel, out_shape=outs, in_specs=specs, out_specs=jax.tree...  11 us
    all_to_all x1, waiting for transfers between devices, per_device(): lax.all_to_all(part, 'x', 0, 0, tiled=True).reshape(around, tokens, width)  6.16 us
    all_to_all x1, starting transfers between devices, per_device(): lax.all_to_all(part, 'x', 0, 0, tiled=True).reshape(around, tokens, width)  4.63 us
  transfers between devices with their start and end apart: 14, of which 7 were waited for; matrix products, arithmetic and copies ran while one was open for 6% of the time, Pallas kernels for 1%

profile of v1, /device:TPU:2, one launch (start us, length us, event | category | flops | bytes accessed | tf_op | source)
XLA Modules:
  0.0 193.8 jit_solution(14264922792128812637)
XLA Ops:
  6.5 0.7 all-gather.4.cloned.1.call-update
  7.3 1.4 pad_maximum_fusion.refs_6_
  8.7 1.9 collective-permute-start.9
  10.7 0.2 copy.12
  11.6 0.6 fusion.2
  12.8 0.1 concatenate.10.refs_2_
  12.9 0.0 copy-start.3
  12.9 1.0 copy.13
  13.9 2.4 %collective-permute-start.1 = (bf16[1168,216]{0,1:T(8,128)(2,1)}, bf16[1168,216]{0,1:T(8,128)(2,1)S(1)}, u32[]{:S(2)}, u32[]{:S(2)}) collective-permute-start(bf16[1168,216]{0,1:T(8,128)(2,1)} %copy.13), channel_id=1, source_target_pairs={{0,1},{1,0},{2,3},{3,2},{4,5},{5,4},{6,7},{7,6},{8,9},{9,8},{10,11... | collective-permute-start | bytes 1513736 | tf_op jit(solution)/shard_map/ppermute | solution.py:155
  16.3 3.5 %collective-permute-start.10 = (bf16[576,1152]{1,0:T(8,128)(2,1)S(1)}, bf16[576,1152]{1,0:T(8,128)(2,1)}, u32[]{:S(2)}, u32[]{:S(2)}) collective-permute-start(bf16[576,1152]{1,0:T(8,128)(2,1)S(1)} %pad_maximum_fusion.refs_6_), channel_id=1, source_target_pairs={{0,2},{2,0},{1,3},{3,1},{4,6},{6,4},{5,7},{7,5},{8,10},{10,8},{9,1... | collective-permute-start | bytes 3981320 | tf_op jit(solution)/shard_map/ppermute | solution.py:189
  19.8 4.1 %collective-permute-start.11 = (bf16[576,1152]{1,0:T(8,128)(2,1)}, bf16[576,1152]{1,0:T(8,128)(2,1)}, u32[]{:S(2)}, u32[]{:S(2)}) collective-permute-start(bf16[576,1152]{1,0:T(8,128)(2,1)} %collective-permute-done.9.refs_7_), channel_id=1, source_target_pairs={{0,258},{258,0},{2,256},{256,2},{1,259},{259,1},{3,257},{257,3},{4... | collective-permute-start | bytes 3981320 | tf_op jit(solution)/shard_map/ppermute | solution.py:190
  23.9 46.2 %all-gather.4.cloned.1.call-done = bf16[576,1152]{1,0:T(8,128)(2,1)} async-done(((bf16[72,1152]{1,0:T(8,128)(2,1)}), bf16[576,1152]{1,0:T(8,128)(2,1)}) %all-gather.4.cloned.1.call-update) | async-done | bytes 1327120 | tf_op jit(solution)/shard_map/all_gather | solution.py:161
  70.1 2.0 %collective-permute-start.8 = (bf16[4,2,72,1152]{3,2,1,0:T(8,128)(2,1)}, bf16[4,2,72,1152]{3,2,1,0:T(8,128)(2,1)}, u32[]{:S(2)}, u32[]{:S(2)}) collective-permute-start(bf16[4,2,72,1152]{3,2,1,0:T(8,128)(2,1)} %bitcast.15), channel_id=1, source_target_pairs={{0,1},{1,0},{2,3},{3,2},{4,5},{5,4},{6,7},{7,6},{8,9},{9,8},{10,11... | collective-permute-start | bytes 3981320 | tf_op jit(solution)/shard_map/ppermute | solution.py:192
  72.7 0.9 concatenate.9
  73.7 3.5 %collective-permute-start = (bf16[64,1152]{1,0:T(8,128)(2,1)S(1)}, bf16[64,1152]{1,0:T(8,128)(2,1)}, u32[]{:S(2)}, u32[]{:S(2)}) collective-permute-start(bf16[64,1152]{1,0:T(8,128)(2,1)S(1)} %concatenate.9), channel_id=1, source_target_pairs={{0,16},{16,32},{32,48},{48,64},{64,80},{80,96},{96,112},{112,128},... | collective-permute-start | bytes 442376 | tf_op jit(solution)/shard_map/ppermute | solution.py:148
  77.1 9.2 %collective-permute-done = bf16[64,1152]{1,0:T(8,128)(2,1)} collective-permute-done((bf16[64,1152]{1,0:T(8,128)(2,1)S(1)}, bf16[64,1152]{1,0:T(8,128)(2,1)}, u32[]{:S(2)}, u32[]{:S(2)}) %collective-permute-start) | collective-permute-done | bytes 147488 | tf_op jit(solution)/shard_map/ppermute | solution.py:148
  86.3 2.2 %collective-permute-start.2 = (bf16[1168,216]{0,1:T(8,128)(2,1)}, bf16[1168,216]{0,1:T(8,128)(2,1)}, u32[]{:S(2)}, u32[]{:S(2)}) collective-permute-start(bf16[1168,216]{0,1:T(8,128)(2,1)} %copy.13), channel_id=1, source_target_pairs={{0,2},{2,0},{1,3},{3,1},{4,6},{6,4},{5,7},{7,5},{8,10},{10,8},{9,1... | collective-permute-start | bytes 1513736 | tf_op jit(solution)/shard_map/ppermute | solution.py:154
  88.5 0.0 collective-permute-done.1
  88.5 4.1 %collective-permute-start.3 = (bf16[1168,216]{0,1:T(8,128)(2,1)S(1)}, bf16[1168,216]{0,1:T(8,128)(2,1)}, u32[]{:S(2)}, u32[]{:S(2)}) collective-permute-start(bf16[1168,216]{0,1:T(8,128)(2,1)S(1)} %collective-permute-done.1), channel_id=1, source_target_pairs={{0,258},{258,0},{2,256},{256,2},{1,259},{259,1},{3,257},{257,3},{4... | collective-permute-start | bytes 1513736 | tf_op jit(solution)/shard_map/ppermute | solution.py:160
  92.6 1.1 slice.13
  94.4 0.9 slice.12
  95.3 0.2 select_reduce_fusion.refs_1_.refs_3_
  95.5 13.2 %all_gather.15.refs_0_.refs_2_ = bf16[192,1152]{1,0:T(8,128)(2,1)S(1)} all-gather(bf16[48,1152]{1,0:T(8,128)(2,1)S(1)} %slice.12), channel_id=1, replica_groups=mesh['yhi'=2,'z'=16,'x'=4,'ylo'=2,'core'=2] {'x'}, dimensions={0}, use_global_device_ids=true | all-gather | bytes 552960 | tf_op jit(solution)/shard_map/all_gather | solution.py:167
  108.7 0.2 copy.15.refs_3_
  109.0 2.1 %copy.16.refs_4_ = bf16[1168,216]{1,0:T(8,128)(2,1)} copy(bf16[1168,216]{0,1:T(8,128)(2,1)} %collective-permute-done.2) | data formatting | bytes 1009152 | tf_op jit(solution)/shard_map/ppermute | solution.py:154
  111.1 2.1 %copy.17.refs_5_ = bf16[1168,216]{1,0:T(8,128)(2,1)} copy(bf16[1168,216]{0,1:T(8,128)(2,1)} %collective-permute-done.3) | data formatting | bytes 1009152 | tf_op jit(solution)/shard_map/ppermute | solution.py:160
  113.2 1.1 copy-done
  114.3 1.1 copy-done.1
  115.3 1.1 shard_map.100
  116.4 1.9 collective-permute-start.4
  118.3 2.6 %collective-permute-start.5 = (bf16[192,576]{1,0:T(8,128)(2,1)S(1)}, bf16[192,576]{1,0:T(8,128)(2,1)S(1)}, u32[]{:S(2)}, u32[]{:S(2)}) collective-permute-start(bf16[192,576]{1,0:T(8,128)(2,1)S(1)} %get-tuple-element.12.refs_5_), channel_id=1, source_target_pairs={{0,16},{16,32},{32,48},{48,64},{64,80},{80,96},{96,112},{112,128},... | collective-permute-start | bytes 663560 | tf_op jit(solution)/shard_map/ppermute | solution.py:148
  120.9 11.9 %collective-permute-done.4.refs_3_ = bf16[192,576]{1,0:T(8,128)(2,1)S(1)} collective-permute-done((bf16[192,576]{1,0:T(8,128)(2,1)S(1)}, bf16[192,576]{1,0:T(8,128)(2,1)S(1)}, u32[]{:S(2)}, u32[]{:S(2)}) %collective-permute-start.4) | collective-permute-done | bytes 221216 | tf_op jit(solution)/shard_map/ppermute | solution.py:148
  132.8 1.9 collective-permute-start.6
  134.7 0.7 collective-permute-done.5.refs_4_
  135.5 3.7 %collective-permute-start.7 = (bf16[192,576]{1,0:T(8,128)(2,1)S(1)}, bf16[192,576]{1,0:T(8,128)(2,1)S(1)}, u32[]{:S(2)}, u32[]{:S(2)}) collective-permute-start(bf16[192,576]{1,0:T(8,128)(2,1)S(1)} %get-tuple-element.12.refs_5_), channel_id=1, source_target_pairs={{0,480},{16,496},{32,0},{48,16},{64,32},{80,48},{96,64},{112,80},{... | collective-permute-start | bytes 663560 | tf_op jit(solution)/shard_map/ppermute | solution.py:148
  139.2 7.0 %collective-permute-done.6.refs_6_ = bf16[192,576]{1,0:T(8,128)(2,1)S(1)} collective-permute-done((bf16[192,576]{1,0:T(8,128)(2,1)S(1)}, bf16[192,576]{1,0:T(8,128)(2,1)S(1)}, u32[]{:S(2)}, u32[]{:S(2)}) %collective-permute-start.6) | collective-permute-done | bytes 221216 | tf_op jit(solution)/shard_map/ppermute | solution.py:148
  146.2 4.7 %collective-permute-done.7.refs_7_ = bf16[192,576]{1,0:T(8,128)(2,1)S(1)} collective-permute-done((bf16[192,576]{1,0:T(8,128)(2,1)S(1)}, bf16[192,576]{1,0:T(8,128)(2,1)S(1)}, u32[]{:S(2)}, u32[]{:S(2)}) %collective-permute-start.7) | collective-permute-done | bytes 221216 | tf_op jit(solution)/shard_map/ppermute | solution.py:148
  150.9 1.4 shard_map.101
  152.3 13.1 %all-gather = bf16[768,288]{1,0:T(8,128)(2,1)S(1)} all-gather(bf16[192,288]{1,0:T(8,128)(2,1)S(1)} %shard_map.101), channel_id=2, replica_groups=mesh['yhi'=2,'z'=16,'x'=4,'ylo'=2,'core'=2] {'x'}, dimensions={0}, use_global_device_ids=true | all-gather | bytes 552960 | tf_op jit(solution)/shard_map/all_gather | solution.py:203
  165.3 0.0 collective-permute-done.10.refs_8_
  165.4 0.0 collective-permute-done.11.refs_9_
  165.4 0.0 collective-permute-done.8.refs_5_
  165.4 1.3 copy-done.2
  166.7 8.6 %shard_map.102 = (bf16[192,1152]{1,0:T(8,128)(2,1)S(1)}, bf16[192,1152]{1,0:T(8,128)(2,1)}) custom-call(s32[1]{0:T(128)} %bitcast.refs_0_, bf16[4,192,288]{2,1,0:T(8,128)(2,1)S(1)} %bitcast.14, bf16[192,1152]{1,0:T(8,128)(2,1)S(1)} %all_gather.15.refs_0_.refs_2_, f32[6,1152]{1,0:T(8,128)S(1)} %select_reduce_fusion.refs_1_.refs_3_, ...), custom_call_target="tpu_custom_call" | custom-call | tf_op jit(solution)/shard_map/pallas_call | solution.py:116
  175.3 4.6 %all-to-all-start = ((bf16[4,48,1152]{2,1,0:T(8,128)(2,1)}), bf16[4,48,1152]{2,1,0:T(8,128)(2,1)S(1)}, u32[]{:S(2)}, u32[]{:S(2)}) async-start(bf16[4,48,1152]{2,1,0:T(8,128)(2,1)} %bitcast.9), calls=%async_computation | async-start | bytes 884736 | tf_op jit(solution)/shard_map/all_to_all | solution.py:219
  180.0 6.2 %all-to-all-done = bf16[4,48,1152]{2,1,0:T(8,128)(2,1)S(1)} async-done(((bf16[4,48,1152]{2,1,0:T(8,128)(2,1)}), bf16[4,48,1152]{2,1,0:T(8,128)(2,1)S(1)}, u32[]{:S(2)}, u32[]{:S(2)}) %all-to-all-start) | async-done | bytes 442400 | tf_op jit(solution)/shard_map/all_to_all | solution.py:219
  186.1 0.1 convert_reduce_fusion
  186.2 0.7 fusion.1
  (16 shorter events, 0.1 us)
Async XLA Ops:
  6.5 63.6 %all-gather.4.cloned.1.call-start = ((), (), s32[]{:S(2)}) async-start(), calls=%async_computation.1 | async-start | bytes 1492992 | tf_op jit(solution)/shard_map/all_gather | solution.py:161
  7.3 3.4 %copy-start.4 = (bf16[1152,216]{0,1:T(8,128)(2,1)S(1)}, bf16[1152,216]{0,1:T(8,128)(2,1)}, u32[]{:S(2)}) copy-start(bf16[1152,216]{0,1:T(8,128)(2,1)} %param.16) | copy-start | bytes 1492996
  7.3 4.3 %copy-start.6 = (s32[16]{0:T(128)S(1)}, s32[16]{0:T(128)}, u32[]{:S(2)}) copy-start(s32[16]{0:T(128)} %param.15) | copy-start | bytes 196
  8.7 11.1 %collective-permute-start.9 = (bf16[576,1152]{1,0:T(8,128)(2,1)S(1)}, bf16[576,1152]{1,0:T(8,128)(2,1)}, u32[]{:S(2)}, u32[]{:S(2)}) collective-permute-start(bf16[576,1152]{1,0:T(8,128)(2,1)S(1)} %pad_maximum_fusion.refs_6_), channel_id=1, source_target_pairs={{0,1},{1,0},{2,3},{3,2},{4,5},{5,4},{6,7},{7,6},{8,9},{9,8},{10,11... | collective-permute-start | bytes 3981320 | tf_op jit(solution)/shard_map/ppermute | solution.py:165
  12.9 82.4 %copy-start.3 = (f32[32,6,1152]{2,0,1:T(8,128)S(1)}, f32[32,6,1152]{2,0,1:T(8,128)}, u32[]{:S(2)}) copy-start(f32[32,6,1152]{2,0,1:T(8,128)} %param.13) | copy-start | bytes 2654212
  13.9 74.6 %collective-permute-start.1 = (bf16[1168,216]{0,1:T(8,128)(2,1)}, bf16[1168,216]{0,1:T(8,128)(2,1)S(1)}, u32[]{:S(2)}, u32[]{:S(2)}) collective-permute-start(bf16[1168,216]{0,1:T(8,128)(2,1)} %copy.13), channel_id=1, source_target_pairs={{0,1},{1,0},{2,3},{3,2},{4,5},{5,4},{6,7},{7,6},{8,9},{9,8},{10,11... | collective-permute-start | bytes 1513736 | tf_op jit(solution)/shard_map/ppermute | solution.py:155
  16.3 149.0 %collective-permute-start.10 = (bf16[576,1152]{1,0:T(8,128)(2,1)S(1)}, bf16[576,1152]{1,0:T(8,128)(2,1)}, u32[]{:S(2)}, u32[]{:S(2)}) collective-permute-start(bf16[576,1152]{1,0:T(8,128)(2,1)S(1)} %pad_maximum_fusion.refs_6_), channel_id=1, source_target_pairs={{0,2},{2,0},{1,3},{3,1},{4,6},{6,4},{5,7},{7,5},{8,10},{10,8},{9,1... | collective-permute-start | bytes 3981320 | tf_op jit(solution)/shard_map/ppermute | solution.py:189
  19.8 145.5 %collective-permute-start.11 = (bf16[576,1152]{1,0:T(8,128)(2,1)}, bf16[576,1152]{1,0:T(8,128)(2,1)}, u32[]{:S(2)}, u32[]{:S(2)}) collective-permute-start(bf16[576,1152]{1,0:T(8,128)(2,1)} %collective-permute-done.9.refs_7_), channel_id=1, source_target_pairs={{0,258},{258,0},{2,256},{256,2},{1,259},{259,1},{3,257},{257,3},{4... | collective-permute-start | bytes 3981320 | tf_op jit(solution)/shard_map/ppermute | solution.py:190
  70.1 95.2 %collective-permute-start.8 = (bf16[4,2,72,1152]{3,2,1,0:T(8,128)(2,1)}, bf16[4,2,72,1152]{3,2,1,0:T(8,128)(2,1)}, u32[]{:S(2)}, u32[]{:S(2)}) collective-permute-start(bf16[4,2,72,1152]{3,2,1,0:T(8,128)(2,1)} %bitcast.15), channel_id=1, source_target_pairs={{0,1},{1,0},{2,3},{3,2},{4,5},{5,4},{6,7},{7,6},{8,9},{9,8},{10,11... | collective-permute-start | bytes 3981320 | tf_op jit(solution)/shard_map/ppermute | solution.py:192
  73.7 12.7 %collective-permute-start = (bf16[64,1152]{1,0:T(8,128)(2,1)S(1)}, bf16[64,1152]{1,0:T(8,128)(2,1)}, u32[]{:S(2)}, u32[]{:S(2)}) collective-permute-start(bf16[64,1152]{1,0:T(8,128)(2,1)S(1)} %concatenate.9), channel_id=1, source_target_pairs={{0,16},{16,32},{32,48},{48,64},{64,80},{80,96},{96,112},{112,128},... | collective-permute-start | bytes 442376 | tf_op jit(solution)/shard_map/ppermute | solution.py:148
  86.3 22.6 %collective-permute-start.2 = (bf16[1168,216]{0,1:T(8,128)(2,1)}, bf16[1168,216]{0,1:T(8,128)(2,1)}, u32[]{:S(2)}, u32[]{:S(2)}) collective-permute-start(bf16[1168,216]{0,1:T(8,128)(2,1)} %copy.13), channel_id=1, source_target_pairs={{0,2},{2,0},{1,3},{3,1},{4,6},{6,4},{5,7},{7,5},{8,10},{10,8},{9,1... | collective-permute-start | bytes 1513736 | tf_op jit(solution)/shard_map/ppermute | solution.py:154
  88.5 22.6 %collective-permute-start.3 = (bf16[1168,216]{0,1:T(8,128)(2,1)S(1)}, bf16[1168,216]{0,1:T(8,128)(2,1)}, u32[]{:S(2)}, u32[]{:S(2)}) collective-permute-start(bf16[1168,216]{0,1:T(8,128)(2,1)S(1)} %collective-permute-done.1), channel_id=1, source_target_pairs={{0,258},{258,0},{2,256},{256,2},{1,259},{259,1},{3,257},{257,3},{4... | collective-permute-start | bytes 1513736 | tf_op jit(solution)/shard_map/ppermute | solution.py:160
  113.2 1.1 copy-start
  114.3 1.1 copy-start.1
  116.4 16.4 %collective-permute-start.4 = (bf16[192,576]{1,0:T(8,128)(2,1)S(1)}, bf16[192,576]{1,0:T(8,128)(2,1)S(1)}, u32[]{:S(2)}, u32[]{:S(2)}) collective-permute-start(bf16[192,576]{1,0:T(8,128)(2,1)S(1)} %get-tuple-element.12.refs_5_), channel_id=1, source_target_pairs={{0,32},{16,48},{32,64},{48,80},{64,96},{80,112},{96,128},{112,144}... | collective-permute-start | bytes 663560 | tf_op jit(solution)/shard_map/ppermute | solution.py:148
  118.3 17.2 %collective-permute-start.5 = (bf16[192,576]{1,0:T(8,128)(2,1)S(1)}, bf16[192,576]{1,0:T(8,128)(2,1)S(1)}, u32[]{:S(2)}, u32[]{:S(2)}) collective-permute-start(bf16[192,576]{1,0:T(8,128)(2,1)S(1)} %get-tuple-element.12.refs_5_), channel_id=1, source_target_pairs={{0,16},{16,32},{32,48},{48,64},{64,80},{80,96},{96,112},{112,128},... | collective-permute-start | bytes 663560 | tf_op jit(solution)/shard_map/ppermute | solution.py:148
  132.8 13.4 %collective-permute-start.6 = (bf16[192,576]{1,0:T(8,128)(2,1)S(1)}, bf16[192,576]{1,0:T(8,128)(2,1)S(1)}, u32[]{:S(2)}, u32[]{:S(2)}) collective-permute-start(bf16[192,576]{1,0:T(8,128)(2,1)S(1)} %get-tuple-element.12.refs_5_), channel_id=1, source_target_pairs={{0,496},{16,0},{32,16},{48,32},{64,48},{80,64},{96,80},{112,96},{1... | collective-permute-start | bytes 663560 | tf_op jit(solution)/shard_map/ppermute | solution.py:148
  135.5 15.4 %collective-permute-start.7 = (bf16[192,576]{1,0:T(8,128)(2,1)S(1)}, bf16[192,576]{1,0:T(8,128)(2,1)S(1)}, u32[]{:S(2)}, u32[]{:S(2)}) collective-permute-start(bf16[192,576]{1,0:T(8,128)(2,1)S(1)} %get-tuple-element.12.refs_5_), channel_id=1, source_target_pairs={{0,480},{16,496},{32,0},{48,16},{64,32},{80,48},{96,64},{112,80},{... | collective-permute-start | bytes 663560 | tf_op jit(solution)/shard_map/ppermute | solution.py:148
  165.4 1.3 copy-start.2
  175.3 10.9 %copy-start.5 = (bf16[48,1152]{1,0:T(8,128)(2,1)S(1)}, bf16[48,1152]{1,0:T(8,128)(2,1)}, u32[]{:S(2)}) copy-start(bf16[48,1152]{1,0:T(8,128)(2,1)} %param.11) | copy-start | bytes 331780
  175.3 10.8 %all-to-all-start = ((bf16[4,48,1152]{2,1,0:T(8,128)(2,1)}), bf16[4,48,1152]{2,1,0:T(8,128)(2,1)S(1)}, u32[]{:S(2)}, u32[]{:S(2)}) async-start(bf16[4,48,1152]{2,1,0:T(8,128)(2,1)} %bitcast.9), calls=%async_computation | async-start | bytes 884736 | tf_op jit(solution)/shard_map/all_to_all | solution.py:219
Sparse Core Ops, SparseCore 0:
  9.4 60.6 all-gather.3

commit v2 on v1

v2 whole, which is shorter than its diff:
```python
import jax
import jax.numpy as jnp
from jax import lax
from jax.experimental import pallas as pl
from jax.experimental.pallas import tpu as pltpu
from jax.sharding import Mesh
from jax.sharding import PartitionSpec as P

WMAX = 2
MEGA = 1024 * 1024
BF16, F32 = jnp.bfloat16, jnp.float32
SLOTS = ("yhi", "z")
SWAP = [(0, 1), (1, 0)]
FAR_Y = [(0, 3), (3, 0), (1, 2), (2, 1)]
FAR = [(2 * y + core, 2 * to + 1 - core) for y, to in FAR_Y for core in range(2)]


def normalise(floats, shift, scale):
    center = jnp.mean(floats, axis=-1, keepdims=True)
    spread = jnp.mean((floats - center) ** 2, axis=-1, keepdims=True)
    return ((floats - center) * lax.rsqrt(spread + 1e-06) * (1.0 + scale) + shift).astype(BF16)


def start_all(pairs, sems):
    copies = [pltpu.make_async_copy(src, dst, sems.at[i]) for i, (src, dst) in enumerate(pairs)]
    for copy in copies:
        copy.start()
    return copies


def prepare_kernel(
    levels_ref, map_ref, window_ref, latents_ref, qkv_ref, out_ref, fc1_ref, fc2_ref,
    tok_ref, packed_ref, mlp_ref, latents_here, qkv_here, out_here, sems,
):
    tokens, width = latents_ref.shape
    lines = qkv_ref.shape[0]
    hidden = fc2_ref.shape[0]
    copies = start_all(
        [
            (latents_ref, latents_here),
            (qkv_ref, qkv_here),
            (out_ref, out_here),
            (fc2_ref, mlp_ref.at[0:hidden]),
            (fc1_ref, mlp_ref.at[hidden : 2 * hidden]),
        ],
        sems,
    )
    tok_ref[tokens:, :] = jnp.full((tok_ref.shape[0] - tokens, width), levels_ref[0].astype(F32)).astype(BF16)
    half = jnp.full((8, width), window_ref[map_ref[0]].astype(F32))
    packed_ref[lines : lines + 8, :] = half.astype(BF16)
    copies[0].wait()
    tok_ref[0:tokens, :] = latents_here[...]
    copies[1].wait()
    packed_ref[0:lines, :] = qkv_here[...]
    copies[2].wait()
    packed_ref[lines + 8 : lines + 8 + out_ref.shape[0], :] = out_here[...]
    packed_ref[lines + 8 + out_ref.shape[0] :, :] = jnp.zeros((8, width), BF16)
    copies[3].wait()
    copies[4].wait()


def qkv_kernel(
    head, t0, t1, t2, t3, mods_ref, w0, w1, w2, w3, q_ref, kv_ref, half_ref, mod_ref,
    q_here, half_here, mod_here, sems,
):
    tokens, width = t1.shape
    level = t0[tokens:, :].astype(F32)[0:1, :]
    lines = lax.broadcasted_iota(jnp.int32, (mods_ref.shape[1], width), 0).astype(F32)
    chosen = lines == level
    picked = [
        jnp.sum(jnp.where(chosen, mods_ref[index], 0.0), axis=0, keepdims=True)
        for index in range(mods_ref.shape[0])
    ]
    mod_here[...] = jnp.concatenate(picked + picked[:2], axis=0)
    blocks = (t0[0:tokens, :], t1[...], t2[...], t3[...])
    normed = jnp.concatenate(
        [normalise(block.astype(F32), picked[0], picked[1]) for block in blocks], axis=0
    )
    queries, keys, values = [], [], []
    lane = lax.broadcasted_iota(jnp.int32, half_here.shape, 1)
    half = jnp.zeros(half_here.shape, F32)
    for slot, weight in enumerate((w0, w1, w2, w3)):
        part = lax.dot_general(
            normed, weight[0 : 3 * head, :], (((1,), (1,)), ((), ())), preferred_element_type=F32
        )
        queries.append(part[:, :head])
        keys.append(part[:, head : 2 * head])
        values.append(part[:, 2 * head :])
        mark = weight[3 * head - 8 : 3 * head + 8, 0:128].astype(F32)[8:16]
        half = jnp.where(lane == slot, mark, half)
    half_here[...] = half
    q_here[...] = jnp.concatenate(queries, axis=1).astype(BF16)
    copies = start_all([(mod_here, mod_ref), (half_here, half_ref), (q_here, q_ref)], sems)
    kv_ref[...] = jnp.concatenate(keys + values, axis=1).astype(BF16)
    for copy in copies:
        copy.wait()


def attention_kernel(
    head, frames, frame_ref, x_ref, half_ref, q_ref, k0, k1, k2, k3, k4, own_o, w1, w2, w3, out_ref,
    half_here, q_here, own_here, sems,
):
    rows, cols = q_ref.shape
    first = 3 * head + 8
    copies = start_all(
        [(half_ref, half_here), (q_ref, q_here), (own_o, own_here)],
        sems,
    )
    col = lax.broadcasted_iota(jnp.int32, (cols, 128), 0)
    lane = lax.broadcasted_iota(jnp.int32, (cols, 128), 1)
    gather = ((col >= lane * head) & (col < (lane + 1) * head)).astype(F32).astype(BF16)
    col = lax.broadcasted_iota(jnp.int32, (128, cols), 1)
    lane = lax.broadcasted_iota(jnp.int32, (128, cols), 0)
    spread = ((col >= lane * head) & (col < (lane + 1) * head)).astype(F32).astype(BF16)
    copies[0].wait()
    copies[1].wait()
    query = q_here[...].astype(F32)
    half = half_here[0:1, :]
    frame = frame_ref[0]
    keyvals = (k0, k1, k2, k3, k4)
    masked, valids = [], []
    for index, ref in enumerate(keyvals):
        offset = index - WMAX
        products = (query * ref[:, :cols].astype(F32)).astype(BF16)
        score = jnp.dot(products, gather, preferred_element_type=F32) / (float(head) ** 0.5)
        target = frame + offset
        inside = ((target >= 0) & (target < frames)).astype(F32)
        valid = (inside * (half >= abs(offset)).astype(F32)) > 0.5
        valids.append(valid)
        masked.append(jnp.where(valid, score, -1e30))
    top = masked[0]
    for value in masked[1:]:
        top = jnp.maximum(top, value)
    expo = [jnp.where(valid, jnp.exp(value - top), 0.0) for valid, value in zip(valids, masked)]
    total = expo[0]
    for value in expo[1:]:
        total = total + value
    mixed = jnp.zeros((rows, cols), F32)
    for value, ref in zip(expo, keyvals):
        wide = jnp.dot((value / total).astype(BF16), spread, preferred_element_type=F32)
        mixed = mixed + wide * ref[:, cols:].astype(F32)
    mixed = mixed.astype(BF16)
    for copy in copies[2:]:
        copy.wait()
    weight = [own_here[...].astype(F32)]
    weight += [ref[first : first + head, :].astype(F32) for ref in (w1, w2, w3)]
    weight = jnp.concatenate(weight, axis=0).astype(BF16)
    attn = jnp.dot(mixed, weight, preferred_element_type=F32).astype(BF16)
    tokens = rows // 4
    for block in range(4):
        place = lax.rem(x_ref[0] + 4 - block, 4) * tokens
        out_ref[pl.ds(pl.multiple_of(place, 16), tokens), :] = attn[block * tokens : (block + 1) * tokens]


def total_of(parts_ref, tokens):
    total = parts_ref[0:tokens, :].astype(F32)
    for block in range(1, parts_ref.shape[0] // tokens):
        total = total + parts_ref[block * tokens : (block + 1) * tokens, :].astype(F32)
    return total


def resid_kernel(parts_ref, tok_ref, mod_ref, resid_ref, normed_ref):
    tokens = resid_ref.shape[0]
    attn = total_of(parts_ref, tokens)
    resid = (tok_ref[0:tokens, :].astype(F32) + mod_ref[2:3, :] * attn).astype(BF16)
    resid_ref[...] = resid
    normed_ref[...] = normalise(resid.astype(F32), mod_ref[3:4, :], mod_ref[4:5, :])


def mlp_kernel(hidden, normed_ref, m0, m1, m2, m3, part_ref):
    normed = normed_ref[...]
    total = jnp.zeros(normed.shape, F32)
    for ref in (m0, m1, m2, m3):
        wide = lax.dot_general(
            normed, ref[hidden:, :], (((1,), (1,)), ((), ())), preferred_element_type=F32
        )
        active = jax.nn.gelu(wide, approximate=True).astype(BF16)
        total = total + jnp.dot(active, ref[:hidden, :], preferred_element_type=F32)
    part_ref[...] = total.astype(BF16)


def final_kernel(slot_ref, parts_ref, resid_ref, mod_ref, fresh_ref, out_ref):
    tokens = resid_ref.shape[0]
    mlp = total_of(parts_ref, tokens)
    block_out = (resid_ref[...].astype(F32) + mod_ref[5:6, :] * mlp).astype(BF16)
    out_ref[...] = jnp.where(slot_ref[0] == 0, fresh_ref[...].astype(F32), block_out.astype(F32)).astype(BF16)


SPECS = {
    "s": pl.BlockSpec(memory_space=pltpu.SMEM),
    "v": pl.BlockSpec(memory_space=pltpu.VMEM),
    "a": pl.BlockSpec(memory_space=pltpu.HBM),
}


def call(kernel, outs, kinds, *args, scratch=(), flops=0, limit=16):
    ins, back = ([SPECS[kind] for kind in part] for part in kinds.split(">"))
    args = [
        pltpu.with_memory_space_constraint(arg, pltpu.HBM) if kind == "a" else arg
        for arg, kind in zip(args, kinds)
    ]
    return pl.pallas_call(
        kernel,
        out_shape=outs,
        in_specs=ins,
        out_specs=tuple(back) if isinstance(outs, tuple) else back[0],
        scratch_shapes=scratch,
        compiler_params=pltpu.CompilerParams(vmem_limit_bytes=limit * MEGA),
        cost_estimate=pl.CostEstimate(flops=flops, bytes_accessed=1 << 20, transcendentals=0),
    )(*args)


def per_device(
    latents,
    fresh_noise,
    levels,
    modulation,
    head_map,
    window,
    qkv_weight,
    out_weight,
    fc1_weight,
    fc2_weight,
):
    tokens, width = latents.shape[1:]
    head = out_weight.shape[0]
    hidden = fc2_weight.shape[0]
    slots = lax.axis_size(SLOTS)
    slot = lax.axis_index(SLOTS)
    around = lax.axis_size("x")

    def slid(value, steps):
        return lax.ppermute(value, SLOTS, [(s, (s + steps) % slots) for s in range(slots)])

    def shape(*dims, dtype=BF16):
        return jax.ShapeDtypeStruct(dims, dtype)

    payload, own_w, own_m = call(
        prepare_kernel,
        (shape(tokens + 16, width), shape(4 * head + 16, width), shape(2 * hidden, width)),
        "sssaaaaa>vvv",
        levels,
        head_map,
        window,
        latents[0],
        qkv_weight.T,
        out_weight,
        fc1_weight.T,
        fc2_weight,
        scratch=[
            pltpu.VMEM((tokens, width), BF16),
            pltpu.VMEM((3 * head, width), BF16),
            pltpu.VMEM((head, width), BF16),
            pltpu.SemaphoreType.DMA((5,)),
        ],
    )
    def come(value, back):
        pairs = [
            (s * around + x, (s + 1) % slots * around + (x + back) % around)
            for s in range(slots)
            for x in range(around)
        ]
        return lax.ppermute(value, SLOTS + ("x",), pairs)

    core_w = lax.ppermute(own_w, "core", SWAP)
    near_w = lax.ppermute(own_w, "ylo", SWAP)
    far_w = lax.ppermute(own_w, ("yhi", "ylo", "core"), FAR)
    toks = [come(payload if back == 0 else latents[0], back) for back in range(around)]

    rows = around * tokens
    cols = 4 * head
    query, keyval, halfs, mod = call(
        lambda *refs: qkv_kernel(head, *refs),
        (
            pltpu.HBM((rows, cols), BF16),
            shape(rows, 2 * cols),
            pltpu.HBM((8, 128), F32),
            pltpu.HBM((8, width), F32),
        ),
        "vvvvvvvvv>avaa",
        *toks,
        modulation.transpose(1, 0, 2),
        own_w,
        core_w,
        near_w,
        far_w,
        scratch=[
            pltpu.VMEM((rows, cols), BF16),
            pltpu.VMEM((8, 128), F32),
            pltpu.VMEM((8, width), F32),
            pltpu.SemaphoreType.DMA((3,)),
        ],
    )
    arrived = [slid(keyval, 2), slid(keyval, 1), slid(keyval, -1), slid(keyval, -2)]
    own_m, keyval = lax.optimization_barrier((own_m, keyval))
    core_m = lax.ppermute(own_m, "core", SWAP)
    near_m = lax.ppermute(own_m, "ylo", SWAP)
    far_m = lax.ppermute(own_m, ("yhi", "ylo", "core"), FAR)
    frame = jnp.where(slot == 0, slots - 1, slot - 1).astype(jnp.int32)
    attended = call(
        lambda *refs: attention_kernel(head, slots, *refs),
        shape(rows, width),
        "ssaavvvvvavvv>v",
        frame[None],
        lax.axis_index("x").astype(jnp.int32)[None],
        halfs,
        query,
        *arrived[:2],
        keyval,
        *arrived[2:],
        out_weight,
        core_w,
        near_w,
        far_w,
        scratch=[
            pltpu.VMEM((8, 128), F32),
            pltpu.VMEM((rows, cols), BF16),
            pltpu.VMEM((head, width), BF16),
            pltpu.SemaphoreType.DMA((3,)),
        ],
        flops=100 * 10**9,
    )
    parts = lax.all_to_all(attended, "x", 0, 0, tiled=True)
    resid, normed = call(
        resid_kernel, (shape(tokens, width), shape(tokens, width)), "vvv>vv", parts, toks[0], mod
    )
    part = call(
        lambda *refs: mlp_kernel(hidden, *refs),
        shape(rows, width),
        "vvvvv>v",
        lax.all_gather(normed, "x", axis=0, tiled=True),
        own_m,
        core_m,
        near_m,
        far_m,
    )
    parts = lax.all_to_all(part, "x", 0, 0, tiled=True)
    return call(
        final_kernel,
        shape(tokens, width),
        "svvvv>v",
        slot[None].astype(jnp.int32),
        parts,
        resid,
        mod,
        fresh_noise,
    )[None]


def solution(mesh):
    split = Mesh(mesh.devices.reshape(2, 16, 4, 2, 2), ("yhi", "z", "x", "ylo", "core"))
    mp = ("x", "ylo", "core")
    in_specs = (
        P(SLOTS, mp, None),
        P(mp, None),
        P(SLOTS),
        P(),
        P(mp),
        P(),
        P(None, mp),
        P(mp, None),
        P(None, mp),
        P(mp, None),
    )
    return jax.shard_map(
        per_device, mesh=split, in_specs=in_specs, out_specs=P(SLOTS, mp, None), check_vma=False
    )
```

time: 195 us -> 118 us (0.61)
  the two profiles are of different devices: /device:TPU:2 before, /device:TPU:32 now
where the time goes in v2:
time: 118 us; the launch traced here: 117 us
  starting transfers between devices  52.5 us (44%)
  blocking collectives  32.9 us (28%)
  waiting for transfers between devices  17.4 us (15%)
  Pallas kernels  12.2 us (10%)
  between operations  1.63 us (1%)
    ppermute x4, starting transfers between devices, come(): return lax.ppermute(value, SLOTS + ('x',), pairs)  19.3 us
    ppermute x4, starting transfers between devices, slid(): lax.ppermute(value, SLOTS, [(s, (s + steps) % slots) for s in range(slots)])  17.5 us
    all_gather x1, blocking collectives, per_device(): lax.all_gather(normed, 'x', axis=0, tiled=True)  12.7 us
    pallas_call x6, Pallas kernels, call(): pl.pallas_call(kernel, out_shape=outs, in_specs=ins, out_specs=tuple(back...  12.2 us
    ppermute x4, waiting for transfers between devices, slid(): lax.ppermute(value, SLOTS, [(s, (s + steps) % slots) for s in range(slots)])  10.2 us
    all_to_all x1, blocking collectives, per_device(): parts = lax.all_to_all(part, 'x', 0, 0, tiled=True)  10.2 us
    all_to_all x1, blocking collectives, per_device(): parts = lax.all_to_all(attended, 'x', 0, 0, tiled=True)  10 us
    ppermute x4, waiting for transfers between devices, come(): return lax.ppermute(value, SLOTS + ('x',), pairs)  7.11 us
  transfers between devices with their start and end apart: 14, of which 4 were waited for; matrix products, arithmetic and copies ran while one was open for 0% of the time, Pallas kernels for 3%

profile of v2, /device:TPU:32, one launch (start us, length us, event | category | flops | bytes accessed | tf_op | source)
XLA Modules:
  0.0 117.2 jit_solution(15896209588888033357)
XLA Ops:
  1.4 0.0 copy-start.5
  1.4 0.6 copy-done.5
  2.0 0.0 copy-start.6
  2.0 2.1 %shard_map.100 = (bf16[64,1152]{1,0:T(8,128)(2,1)S(1)}, bf16[304,1152]{1,0:T(8,128)(2,1)S(1)}, bf16[576,1152]{1,0:T(8,128)(2,1)S(1)}) custom-call(s32[1]{0:T(128)S(6)} %copy.11.levels_ref, s32[1]{0:T(128)S(6)} %copy.12.map_ref, s32[16]{0:T(128)S(1)} %copy-done.5, bf16[48,1152]{1,0:T(8,128)(2,1)} %bitcast.19, bf16[216,1152]{1,0:T(8,128)(2,1)} %bitcast.18, ...), custom_call_target="tpu_custom_call" | custom-call | bytes 1048576 | tf_op jit(solution)/shard_map/pallas_call | solution.py:202
  4.2 4.4 %collective-permute-start.6 = (bf16[304,1152]{1,0:T(8,128)(2,1)S(1)}, bf16[304,1152]{1,0:T(8,128)(2,1)S(1)}, u32[]{:S(2)}, u32[]{:S(2)}) collective-permute-start(bf16[304,1152]{1,0:T(8,128)(2,1)S(1)} %get-tuple-element.17.refs_5_), channel_id=1, source_target_pairs={{0,259},{1,258},{258,1},{259,0},{2,257},{3,256},{256,3},{257,2},{4... | collective-permute-start | bytes 2101256 | tf_op jit(solution)/shard_map/ppermute | solution.py:267
  8.6 2.0 %collective-permute-start.5 = (bf16[304,1152]{1,0:T(8,128)(2,1)S(1)}, bf16[304,1152]{1,0:T(8,128)(2,1)S(1)}, u32[]{:S(2)}, u32[]{:S(2)}) collective-permute-start(bf16[304,1152]{1,0:T(8,128)(2,1)S(1)} %get-tuple-element.17.refs_5_), channel_id=1, source_target_pairs={{0,2},{2,0},{1,3},{3,1},{4,6},{6,4},{5,7},{7,5},{8,10},{10,8},{9,1... | collective-permute-start | bytes 2101256 | tf_op jit(solution)/shard_map/ppermute | solution.py:266
  10.6 2.5 %collective-permute-start.4 = (bf16[304,1152]{1,0:T(8,128)(2,1)S(1)}, bf16[304,1152]{1,0:T(8,128)(2,1)S(1)}, u32[]{:S(2)}, u32[]{:S(2)}) collective-permute-start(bf16[304,1152]{1,0:T(8,128)(2,1)S(1)} %get-tuple-element.17.refs_5_), channel_id=1, source_target_pairs={{0,1},{1,0},{2,3},{3,2},{4,5},{5,4},{6,7},{7,6},{8,9},{9,8},{10,11... | collective-permute-start | bytes 2101256 | tf_op jit(solution)/shard_map/ppermute | solution.py:265
  13.1 0.0 copy-done.6
  13.1 6.0 %collective-permute-start.3 = (bf16[48,1152]{1,0:T(8,128)(2,1)S(1)}, bf16[48,1152]{1,0:T(8,128)(2,1)S(1)}, u32[]{:S(2)}, u32[]{:S(2)}) collective-permute-start(bf16[48,1152]{1,0:T(8,128)(2,1)S(1)} %bitcast.20), channel_id=1, source_target_pairs={{0,28},{4,16},{8,20},{12,24},{16,44},{20,32},{24,36},{28,40},{32,6... | collective-permute-start | bytes 331784 | tf_op jit(solution)/shard_map/ppermute | solution.py:263
  19.1 4.1 %collective-permute-start.2 = (bf16[48,1152]{1,0:T(8,128)(2,1)S(1)}, bf16[48,1152]{1,0:T(8,128)(2,1)S(1)}, u32[]{:S(2)}, u32[]{:S(2)}) collective-permute-start(bf16[48,1152]{1,0:T(8,128)(2,1)S(1)} %bitcast.21), channel_id=1, source_target_pairs={{0,24},{4,28},{8,16},{12,20},{16,40},{20,44},{24,32},{28,36},{32,5... | collective-permute-start | bytes 331784 | tf_op jit(solution)/shard_map/ppermute | solution.py:263
  23.2 0.0 collective-permute-done.3.refs_3_
  23.2 5.0 %collective-permute-start = (bf16[64,1152]{1,0:T(8,128)(2,1)S(1)}, bf16[64,1152]{1,0:T(8,128)(2,1)S(1)}, u32[]{:S(2)}, u32[]{:S(2)}) collective-permute-start(bf16[64,1152]{1,0:T(8,128)(2,1)S(1)} %get-tuple-element.16), channel_id=1, source_target_pairs={{0,16},{4,20},{8,24},{12,28},{16,32},{20,36},{24,40},{28,44},{32,4... | collective-permute-start | bytes 442376 | tf_op jit(solution)/shard_map/ppermute | solution.py:263
  28.2 0.0 collective-permute-done.2.refs_2_
  28.2 4.1 %collective-permute-start.1 = (bf16[48,1152]{1,0:T(8,128)(2,1)S(1)}, bf16[48,1152]{1,0:T(8,128)(2,1)S(1)}, u32[]{:S(2)}, u32[]{:S(2)}) collective-permute-start(bf16[48,1152]{1,0:T(8,128)(2,1)S(1)} %bitcast.22), channel_id=1, source_target_pairs={{0,20},{4,24},{8,28},{12,16},{16,36},{20,40},{24,44},{28,32},{32,5... | collective-permute-start | bytes 331784 | tf_op jit(solution)/shard_map/ppermute | solution.py:263
  32.4 7.1 %collective-permute-done.1.refs_1_ = bf16[48,1152]{1,0:T(8,128)(2,1)S(1)} collective-permute-done((bf16[48,1152]{1,0:T(8,128)(2,1)S(1)}, bf16[48,1152]{1,0:T(8,128)(2,1)S(1)}, u32[]{:S(2)}, u32[]{:S(2)}) %collective-permute-start.1) | collective-permute-done | bytes 110624 | tf_op jit(solution)/shard_map/ppermute | solution.py:263
  39.5 0.0 collective-permute-done.refs_0_.tok_ref
  39.5 0.0 copy-start.1
  39.5 0.0 collective-permute-done.6.refs_8_.refs_12_
  39.5 0.0 collective-permute-done.5.refs_7_.refs_11_
  39.5 0.0 collective-permute-done.4.refs_6_.refs_10_
  39.5 0.0 copy-done
  39.5 2.7 %shard_map.101 = (bf16[192,288]{1,0:T(8,128)(2,1)}, bf16[192,576]{1,0:T(8,128)(2,1)}, f32[8,128]{1,0:T(8,128)}, f32[8,1152]{1,0:T(8,128)}) custom-call(bf16[64,1152]{1,0:T(8,128)(2,1)S(1)} %collective-permute-done.refs_0_.tok_ref, bf16[48,1152]{1,0:T(8,128)(2,1)S(1)} %collective-permute-done.1.refs_1_, bf16[48,1152]{1,0:T(8,128)(2,1)S(1)} %collective-permute-done.2.refs_2_, ...), custom_call_target="tpu_custom_call" | custom-call | bytes 1048576 | tf_op jit(solution)/shard_map/pallas_call | solution.py:202
  42.3 0.0 copy-done.1
  42.3 8.4 %collective-permute-start.10 = (bf16[192,576]{1,0:T(8,128)(2,1)}, bf16[192,576]{1,0:T(8,128)(2,1)}, u32[]{:S(2)}, u32[]{:S(2)}) collective-permute-start(bf16[192,576]{1,0:T(8,128)(2,1)} %get-tuple-element.22.refs_6_), channel_id=1, source_target_pairs={{0,480},{16,496},{32,0},{48,16},{64,32},{80,48},{96,64},{112,80},{... | collective-permute-start | bytes 663560 | tf_op jit(solution)/shard_map/ppermute | solution.py:233
  50.7 3.1 %collective-permute-start.9 = (bf16[192,576]{1,0:T(8,128)(2,1)}, bf16[192,576]{1,0:T(8,128)(2,1)}, u32[]{:S(2)}, u32[]{:S(2)}) collective-permute-start(bf16[192,576]{1,0:T(8,128)(2,1)} %get-tuple-element.22.refs_6_), channel_id=1, source_target_pairs={{0,496},{16,0},{32,16},{48,32},{64,48},{80,64},{96,80},{112,96},{1... | collective-permute-start | bytes 663560 | tf_op jit(solution)/shard_map/ppermute | solution.py:233
  53.9 2.7 %collective-permute-start.8 = (bf16[192,576]{1,0:T(8,128)(2,1)}, bf16[192,576]{1,0:T(8,128)(2,1)}, u32[]{:S(2)}, u32[]{:S(2)}) collective-permute-start(bf16[192,576]{1,0:T(8,128)(2,1)} %get-tuple-element.22.refs_6_), channel_id=1, source_target_pairs={{0,16},{16,32},{32,48},{48,64},{64,80},{80,96},{96,112},{112,128},... | collective-permute-start | bytes 663560 | tf_op jit(solution)/shard_map/ppermute | solution.py:233
  56.6 3.2 %collective-permute-start.7 = (bf16[192,576]{1,0:T(8,128)(2,1)}, bf16[192,576]{1,0:T(8,128)(2,1)}, u32[]{:S(2)}, u32[]{:S(2)}) collective-permute-start(bf16[192,576]{1,0:T(8,128)(2,1)} %get-tuple-element.22.refs_6_), channel_id=1, source_target_pairs={{0,32},{16,48},{32,64},{48,80},{64,96},{80,112},{96,128},{112,144}... | collective-permute-start | bytes 663560 | tf_op jit(solution)/shard_map/ppermute | solution.py:233
  59.8 1.9 %collective-permute-start.13 = (bf16[576,1152]{1,0:T(8,128)(2,1)S(1)}, bf16[576,1152]{1,0:T(8,128)(2,1)S(1)}, u32[]{:S(2)}, u32[]{:S(2)}) collective-permute-start(bf16[576,1152]{1,0:T(8,128)(2,1)S(1)} %get-tuple-element.25.refs_1_), channel_id=1, source_target_pairs={{0,259},{1,258},{258,1},{259,0},{2,257},{3,256},{256,3},{257,2},{4... | collective-permute-start | bytes 3981320 | tf_op jit(solution)/shard_map/ppermute | solution.py:298
  61.7 0.6 collective-permute-done.10.refs_8_
  62.3 1.9 %collective-permute-start.12 = (bf16[576,1152]{1,0:T(8,128)(2,1)S(1)}, bf16[576,1152]{1,0:T(8,128)(2,1)S(1)}, u32[]{:S(2)}, u32[]{:S(2)}) collective-permute-start(bf16[576,1152]{1,0:T(8,128)(2,1)S(1)} %get-tuple-element.25.refs_1_), channel_id=1, source_target_pairs={{0,2},{2,0},{1,3},{3,1},{4,6},{6,4},{5,7},{7,5},{8,10},{10,8},{9,1... | collective-permute-start | bytes 3981320 | tf_op jit(solution)/shard_map/ppermute | solution.py:297
  64.3 0.9 collective-permute-done.9.refs_7_
  65.2 3.1 %collective-permute-start.11 = (bf16[576,1152]{1,0:T(8,128)(2,1)S(1)}, bf16[576,1152]{1,0:T(8,128)(2,1)S(1)}, u32[]{:S(2)}, u32[]{:S(2)}) collective-permute-start(bf16[576,1152]{1,0:T(8,128)(2,1)S(1)} %get-tuple-element.25.refs_1_), channel_id=1, source_target_pairs={{0,1},{1,0},{2,3},{3,2},{4,5},{5,4},{6,7},{7,6},{8,9},{9,8},{10,11... | collective-permute-start | bytes 3981320 | tf_op jit(solution)/shard_map/ppermute | solution.py:296
  68.2 0.0 collective-permute-done.8.refs_5_
  68.2 8.7 %collective-permute-done.7.refs_4_ = bf16[192,576]{1,0:T(8,128)(2,1)} collective-permute-done((bf16[192,576]{1,0:T(8,128)(2,1)}, bf16[192,576]{1,0:T(8,128)(2,1)}, u32[]{:S(2)}, u32[]{:S(2)}) %collective-permute-start.7) | collective-permute-done | bytes 221216 | tf_op jit(solution)/shard_map/ppermute | solution.py:233
  76.9 0.0 copy-start.2
  76.9 3.5 %shard_map.102 = bf16[192,1152]{1,0:T(8,128)(2,1)S(1)} custom-call(s32[1]{0:T(128)} %bitcast.1.refs_0_, s32[1]{0:T(128)} %bitcast.2.refs_1_, f32[8,128]{1,0:T(8,128)} %get-tuple-element.18.refs_2_, bf16[192,288]{1,0:T(8,128)(2,1)} %get-tuple-element.19.refs_3_, bf16[192,576]{1,0:T(8,128)(2,1)} %collective-permute-done.7.refs_4_, ...), custom_call_target="tpu_custom_call" | custom-call | flops 99999997952 | bytes 1048576 | tf_op jit(solution)/shard_map/pallas_call | solution.py:202
  80.5 10.0 %all_to_all.22 = bf16[4,48,1152]{2,1,0:T(8,128)(2,1)S(1)} all-to-all(bf16[4,48,1152]{2,1,0:T(8,128)(2,1)S(1)} %bitcast.16), channel_id=1, replica_groups=mesh['yhi'=2,'z'=16,'x'=4,'ylo'=2,'core'=2] {'x'}, dimensions={0} | all-to-all | bytes 884736 | tf_op jit(solution)/shard_map/all_to_all | solution.py:323
  90.5 0.0 copy-done.2
  90.5 0.0 copy-done.3
  90.5 0.3 shard_map.103
  90.8 12.7 %all_gather.3.refs_0_ = bf16[192,1152]{1,0:T(8,128)(2,1)S(1)} all-gather(bf16[48,1152]{1,0:T(8,128)(2,1)S(1)} %get-tuple-element.24), channel_id=1, replica_groups=mesh['yhi'=2,'z'=16,'x'=4,'ylo'=2,'core'=2] {'x'}, dimensions={0}, use_global_device_ids=true | all-gather | bytes 552960 | tf_op jit(solution)/shard_map/all_gather | solution.py:331
  103.5 0.0 collective-permute-done.13.refs_4_
  103.5 0.0 collective-permute-done.12.refs_3_
  103.5 0.0 collective-permute-done.11.refs_2_
  103.5 2.8 %shard_map.104 = bf16[192,1152]{1,0:T(8,128)(2,1)S(1)} custom-call(bf16[192,1152]{1,0:T(8,128)(2,1)S(1)} %all_gather.3.refs_0_, bf16[576,1152]{1,0:T(8,128)(2,1)S(1)} %get-tuple-element.25.refs_1_, bf16[576,1152]{1,0:T(8,128)(2,1)S(1)} %collective-permute-done.11.refs_2_, bf16[576,1152]{1,0:T(8,128)(2,1)S(1)} %collective-permute-done.12.refs_3_, ...), custom_call_target="tpu_custom_call" | custom-call | bytes 1048576 | tf_op jit(solution)/shard_map/pallas_call | solution.py:202
  106.3 10.2 %all_to_all.23 = bf16[4,48,1152]{2,1,0:T(8,128)(2,1)S(1)} all-to-all(bf16[4,48,1152]{2,1,0:T(8,128)(2,1)S(1)} %bitcast.12), channel_id=1, replica_groups=mesh['yhi'=2,'z'=16,'x'=4,'ylo'=2,'core'=2] {'x'}, dimensions={0} | all-to-all | bytes 884736 | tf_op jit(solution)/shard_map/all_to_all | solution.py:337
  116.5 0.0 copy-done.4
  116.5 0.7 shard_map.105
  (3 shorter events, 0.0 us)
Async XLA Ops:
  0.0 39.5 %copy-start = (f32[32,6,1152]{2,0,1:T(8,128)S(1)}, f32[32,6,1152]{2,0,1:T(8,128)}, u32[]{:S(2)}) copy-start(f32[32,6,1152]{2,0,1:T(8,128)} %param.13) | copy-start | bytes 2654212
  1.4 0.7 copy-start.5
  2.0 11.0 %copy-start.6 = (bf16[1,48,1152]{2,1,0:T(8,128)(2,1)S(1)}, bf16[1,48,1152]{2,1,0:T(8,128)(2,1)}, u32[]{:S(2)}) copy-start(bf16[1,48,1152]{2,1,0:T(8,128)(2,1)} %param.10) | copy-start | bytes 331780
  4.2 35.3 %collective-permute-start.6 = (bf16[304,1152]{1,0:T(8,128)(2,1)S(1)}, bf16[304,1152]{1,0:T(8,128)(2,1)S(1)}, u32[]{:S(2)}, u32[]{:S(2)}) collective-permute-start(bf16[304,1152]{1,0:T(8,128)(2,1)S(1)} %get-tuple-element.17.refs_5_), channel_id=1, source_target_pairs={{0,259},{1,258},{258,1},{259,0},{2,257},{3,256},{256,3},{257,2},{4... | collective-permute-start | bytes 2101256 | tf_op jit(solution)/shard_map/ppermute | solution.py:267
  8.6 31.0 %collective-permute-start.5 = (bf16[304,1152]{1,0:T(8,128)(2,1)S(1)}, bf16[304,1152]{1,0:T(8,128)(2,1)S(1)}, u32[]{:S(2)}, u32[]{:S(2)}) collective-permute-start(bf16[304,1152]{1,0:T(8,128)(2,1)S(1)} %get-tuple-element.17.refs_5_), channel_id=1, source_target_pairs={{0,2},{2,0},{1,3},{3,1},{4,6},{6,4},{5,7},{7,5},{8,10},{10,8},{9,1... | collective-permute-start | bytes 2101256 | tf_op jit(solution)/shard_map/ppermute | solution.py:266
  10.6 28.9 %collective-permute-start.4 = (bf16[304,1152]{1,0:T(8,128)(2,1)S(1)}, bf16[304,1152]{1,0:T(8,128)(2,1)S(1)}, u32[]{:S(2)}, u32[]{:S(2)}) collective-permute-start(bf16[304,1152]{1,0:T(8,128)(2,1)S(1)} %get-tuple-element.17.refs_5_), channel_id=1, source_target_pairs={{0,1},{1,0},{2,3},{3,2},{4,5},{5,4},{6,7},{7,6},{8,9},{9,8},{10,11... | collective-permute-start | bytes 2101256 | tf_op jit(solution)/shard_map/ppermute | solution.py:265
  13.1 10.1 %collective-permute-start.3 = (bf16[48,1152]{1,0:T(8,128)(2,1)S(1)}, bf16[48,1152]{1,0:T(8,128)(2,1)S(1)}, u32[]{:S(2)}, u32[]{:S(2)}) collective-permute-start(bf16[48,1152]{1,0:T(8,128)(2,1)S(1)} %bitcast.20), channel_id=1, source_target_pairs={{0,28},{4,16},{8,20},{12,24},{16,44},{20,32},{24,36},{28,40},{32,6... | collective-permute-start | bytes 331784 | tf_op jit(solution)/shard_map/ppermute | solution.py:263
  19.1 9.1 %collective-permute-start.2 = (bf16[48,1152]{1,0:T(8,128)(2,1)S(1)}, bf16[48,1152]{1,0:T(8,128)(2,1)S(1)}, u32[]{:S(2)}, u32[]{:S(2)}) collective-permute-start(bf16[48,1152]{1,0:T(8,128)(2,1)S(1)} %bitcast.21), channel_id=1, source_target_pairs={{0,24},{4,28},{8,16},{12,20},{16,40},{20,44},{24,32},{28,36},{32,5... | collective-permute-start | bytes 331784 | tf_op jit(solution)/shard_map/ppermute | solution.py:263
  23.2 16.3 %collective-permute-start = (bf16[64,1152]{1,0:T(8,128)(2,1)S(1)}, bf16[64,1152]{1,0:T(8,128)(2,1)S(1)}, u32[]{:S(2)}, u32[]{:S(2)}) collective-permute-start(bf16[64,1152]{1,0:T(8,128)(2,1)S(1)} %get-tuple-element.16), channel_id=1, source_target_pairs={{0,16},{4,20},{8,24},{12,28},{16,32},{20,36},{24,40},{28,44},{32,4... | collective-permute-start | bytes 442376 | tf_op jit(solution)/shard_map/ppermute | solution.py:263
  28.2 11.3 %collective-permute-start.1 = (bf16[48,1152]{1,0:T(8,128)(2,1)S(1)}, bf16[48,1152]{1,0:T(8,128)(2,1)S(1)}, u32[]{:S(2)}, u32[]{:S(2)}) collective-permute-start(bf16[48,1152]{1,0:T(8,128)(2,1)S(1)} %bitcast.22), channel_id=1, source_target_pairs={{0,20},{4,24},{8,28},{12,16},{16,36},{20,40},{24,44},{28,32},{32,5... | collective-permute-start | bytes 331784 | tf_op jit(solution)/shard_map/ppermute | solution.py:263
  39.5 2.8 %copy-start.1 = (bf16[64,1152]{1,0:T(8,128)(2,1)}, bf16[64,1152]{1,0:T(8,128)(2,1)S(1)}, u32[]{:S(2)}) copy-start(bf16[64,1152]{1,0:T(8,128)(2,1)S(1)} %collective-permute-done.refs_0_.tok_ref) | copy-start | bytes 442372
  42.3 20.1 %collective-permute-start.10 = (bf16[192,576]{1,0:T(8,128)(2,1)}, bf16[192,576]{1,0:T(8,128)(2,1)}, u32[]{:S(2)}, u32[]{:S(2)}) collective-permute-start(bf16[192,576]{1,0:T(8,128)(2,1)} %get-tuple-element.22.refs_6_), channel_id=1, source_target_pairs={{0,480},{16,496},{32,0},{48,16},{64,32},{80,48},{96,64},{112,80},{... | collective-permute-start | bytes 663560 | tf_op jit(solution)/shard_map/ppermute | solution.py:233
  50.7 14.4 %collective-permute-start.9 = (bf16[192,576]{1,0:T(8,128)(2,1)}, bf16[192,576]{1,0:T(8,128)(2,1)}, u32[]{:S(2)}, u32[]{:S(2)}) collective-permute-start(bf16[192,576]{1,0:T(8,128)(2,1)} %get-tuple-element.22.refs_6_), channel_id=1, source_target_pairs={{0,496},{16,0},{32,16},{48,32},{64,48},{80,64},{96,80},{112,96},{1... | collective-permute-start | bytes 663560 | tf_op jit(solution)/shard_map/ppermute | solution.py:233
  53.9 14.4 %collective-permute-start.8 = (bf16[192,576]{1,0:T(8,128)(2,1)}, bf16[192,576]{1,0:T(8,128)(2,1)}, u32[]{:S(2)}, u32[]{:S(2)}) collective-permute-start(bf16[192,576]{1,0:T(8,128)(2,1)} %get-tuple-element.22.refs_6_), channel_id=1, source_target_pairs={{0,16},{16,32},{32,48},{48,64},{64,80},{80,96},{96,112},{112,128},... | collective-permute-start | bytes 663560 | tf_op jit(solution)/shard_map/ppermute | solution.py:233
  56.6 20.3 %collective-permute-start.7 = (bf16[192,576]{1,0:T(8,128)(2,1)}, bf16[192,576]{1,0:T(8,128)(2,1)}, u32[]{:S(2)}, u32[]{:S(2)}) collective-permute-start(bf16[192,576]{1,0:T(8,128)(2,1)} %get-tuple-element.22.refs_6_), channel_id=1, source_target_pairs={{0,32},{16,48},{32,64},{48,80},{64,96},{80,112},{96,128},{112,144}... | collective-permute-start | bytes 663560 | tf_op jit(solution)/shard_map/ppermute | solution.py:233
  59.8 43.7 %collective-permute-start.13 = (bf16[576,1152]{1,0:T(8,128)(2,1)S(1)}, bf16[576,1152]{1,0:T(8,128)(2,1)S(1)}, u32[]{:S(2)}, u32[]{:S(2)}) collective-permute-start(bf16[576,1152]{1,0:T(8,128)(2,1)S(1)} %get-tuple-element.25.refs_1_), channel_id=1, source_target_pairs={{0,259},{1,258},{258,1},{259,0},{2,257},{3,256},{256,3},{257,2},{4... | collective-permute-start | bytes 3981320 | tf_op jit(solution)/shard_map/ppermute | solution.py:298
  62.3 41.1 %collective-permute-start.12 = (bf16[576,1152]{1,0:T(8,128)(2,1)S(1)}, bf16[576,1152]{1,0:T(8,128)(2,1)S(1)}, u32[]{:S(2)}, u32[]{:S(2)}) collective-permute-start(bf16[576,1152]{1,0:T(8,128)(2,1)S(1)} %get-tuple-element.25.refs_1_), channel_id=1, source_target_pairs={{0,2},{2,0},{1,3},{3,1},{4,6},{6,4},{5,7},{7,5},{8,10},{10,8},{9,1... | collective-permute-start | bytes 3981320 | tf_op jit(solution)/shard_map/ppermute | solution.py:297
  65.2 38.3 %collective-permute-start.11 = (bf16[576,1152]{1,0:T(8,128)(2,1)S(1)}, bf16[576,1152]{1,0:T(8,128)(2,1)S(1)}, u32[]{:S(2)}, u32[]{:S(2)}) collective-permute-start(bf16[576,1152]{1,0:T(8,128)(2,1)S(1)} %get-tuple-element.25.refs_1_), channel_id=1, source_target_pairs={{0,1},{1,0},{2,3},{3,2},{4,5},{5,4},{6,7},{7,6},{8,9},{9,8},{10,11... | collective-permute-start | bytes 3981320 | tf_op jit(solution)/shard_map/ppermute | solution.py:296
  76.9 13.6 %copy-start.2 = (bf16[64,1152]{1,0:T(8,128)(2,1)S(1)}, bf16[64,1152]{1,0:T(8,128)(2,1)}, u32[]{:S(2)}) copy-start(bf16[64,1152]{1,0:T(8,128)(2,1)} %copy-done.1) | copy-start | bytes 442372
  76.9 13.6 %copy-start.3 = (f32[8,1152]{1,0:T(8,128)S(1)}, f32[8,1152]{1,0:T(8,128)}, u32[]{:S(2)}) copy-start(f32[8,1152]{1,0:T(8,128)} %get-tuple-element.23.mod_ref) | copy-start | bytes 110596
  103.5 13.0 %copy-start.4 = (bf16[48,1152]{1,0:T(8,128)(2,1)S(1)}, bf16[48,1152]{1,0:T(8,128)(2,1)}, u32[]{:S(2)}) copy-start(bf16[48,1152]{1,0:T(8,128)(2,1)} %fresh_ref.1) | copy-start | bytes 331780

commit v3 on v2

v3 whole, which is shorter than its diff:
```python
import jax
import jax.numpy as jnp
from jax import lax
from jax.experimental import pallas as pl
from jax.experimental.pallas import tpu as pltpu
from jax.sharding import Mesh
from jax.sharding import PartitionSpec as P

MEGA = 1024 * 1024
BF16, F32 = jnp.bfloat16, jnp.float32
SLOTS = ("yhi", "z")
SWAP = [(0, 1), (1, 0)]
FAR_Y = [(0, 3), (3, 0), (1, 2), (2, 1)]
FAR = [(2 * y + core, 2 * to + 1 - core) for y, to in FAR_Y for core in range(2)]


def normalise(floats, shift, scale):
    center = jnp.mean(floats, axis=-1, keepdims=True)
    spread = jnp.mean((floats - center) ** 2, axis=-1, keepdims=True)
    return ((floats - center) * lax.rsqrt(spread + 1e-06) * (1.0 + scale) + shift).astype(BF16)


def start_all(pairs, sems):
    copies = [pltpu.make_async_copy(src, dst, sems.at[i]) for i, (src, dst) in enumerate(pairs)]
    for copy in copies:
        copy.start()
    return copies


def prepare_kernel(
    levels_ref, map_ref, window_ref, latents_ref, mods_ref, qkv_ref, out_ref,
    tok_ref, packed_ref, window_here, latents_here, mods_here, qkv_here, out_here, sems,
):
    tokens, width = latents_ref.shape
    lines, rows = qkv_ref.shape[0], out_ref.shape[0]
    level = levels_ref[0]
    group = pl.multiple_of(level // 8 * 8, 8)
    copies = start_all(
        [
            (window_ref, window_here),
            (mods_ref.at[:, pl.ds(group, 8), :], mods_here),
            (latents_ref, latents_here),
            (qkv_ref, qkv_here),
            (out_ref, out_here),
        ],
        sems,
    )
    packed_ref[lines + 8 + rows :, :] = jnp.zeros((8, width), BF16)
    copies[0].wait()
    half = jnp.full((8, width), window_here[map_ref[0]].astype(F32))
    packed_ref[lines : lines + 8, :] = half.astype(BF16)
    copies[1].wait()
    chosen = lax.broadcasted_iota(jnp.int32, (8, width), 0) == level - group
    picked = [
        jnp.sum(jnp.where(chosen, mods_here[index], 0.0), axis=0, keepdims=True)
        for index in range(mods_here.shape[0])
    ]
    rest = jnp.concatenate(picked + picked[:2], axis=0)
    terms = []
    for _ in range(3):
        term = rest.astype(BF16).astype(F32)
        terms.append(term)
        rest = rest - term
    tok_ref[tokens:, :] = jnp.concatenate(terms + terms[:1], axis=0).astype(BF16)
    copies[2].wait()
    tok_ref[0:tokens, :] = latents_here[...]
    copies[3].wait()
    packed_ref[0:lines, :] = qkv_here[...]
    copies[4].wait()
    packed_ref[lines + 8 : lines + 8 + rows, :] = out_here[...]


def mod_of(tok_ref, tokens):
    terms = tok_ref[tokens:, :].astype(F32)
    return terms[0:8] + (terms[8:16] + terms[16:24])


def norm_kernel(tok_ref, normed_ref):
    tokens = normed_ref.shape[0]
    mod = mod_of(tok_ref, tokens)
    normed_ref[...] = normalise(tok_ref[0:tokens, :].astype(F32), mod[0:1, :], mod[1:2, :])


def qkv_kernel(
    head, t0, t1, t2, t3, w0, w1, w2, w3, fc1_ref, fc2_ref, q_ref, kv_ref, half_ref, mlp_ref,
    q_here, half_here, sems,
):
    hidden = fc2_ref.shape[0]
    weights = start_all(
        [(fc2_ref, mlp_ref.at[0:hidden]), (fc1_ref, mlp_ref.at[hidden : 2 * hidden])], sems
    )
    normed = jnp.concatenate([block[...] for block in (t0, t1, t2, t3)], axis=0)
    queries, keys, values = [], [], []
    lane = lax.broadcasted_iota(jnp.int32, half_here.shape, 1)
    half = jnp.zeros(half_here.shape, F32)
    for slot, weight in enumerate((w0, w1, w2, w3)):
        part = lax.dot_general(
            normed, weight[0 : 3 * head, :], (((1,), (1,)), ((), ())), preferred_element_type=F32
        )
        queries.append(part[:, :head])
        keys.append(part[:, head : 2 * head])
        values.append(part[:, 2 * head :])
        mark = weight[3 * head - 8 : 3 * head + 8, 0:128].astype(F32)[8:16]
        half = jnp.where(lane == slot, mark, half)
    half_here[...] = half
    q_here[...] = jnp.concatenate(queries, axis=1).astype(BF16)
    copies = weights + start_all([(half_here, half_ref), (q_here, q_ref)], sems.at[2:4])
    kv_ref[...] = jnp.concatenate(keys + values, axis=1).astype(BF16)
    for copy in copies:
        copy.wait()


def attention_kernel(
    head, slots, slot_ref, x_ref, half_ref, q_ref, k0, k1, k2, k3, k4, own_o, w1, w2, w3, out_ref,
    half_here, q_here, own_here, sems,
):
    rows, cols = q_ref.shape
    first = 3 * head + 8
    copies = start_all(
        [(half_ref, half_here), (q_ref, q_here), (own_o, own_here)],
        sems,
    )
    col = lax.broadcasted_iota(jnp.int32, (cols, 128), 0)
    lane = lax.broadcasted_iota(jnp.int32, (cols, 128), 1)
    gather = ((col >= lane * head) & (col < (lane + 1) * head)).astype(F32).astype(BF16)
    col = lax.broadcasted_iota(jnp.int32, (128, cols), 1)
    lane = lax.broadcasted_iota(jnp.int32, (128, cols), 0)
    spread = ((col >= lane * head) & (col < (lane + 1) * head)).astype(F32).astype(BF16)
    copies[0].wait()
    copies[1].wait()
    query = q_here[...].astype(F32)
    half = half_here[0:1, :]
    place = slot_ref[0]
    frame = lax.rem(place + slots - 1, slots)
    odd, upper = place & 1, place & 2
    keyvals = (k0, k1, k2, k3, k4)
    offsets = (0, 1 - 2 * odd, 2 * odd - 1, 2 - 2 * upper, 2 * upper - 2)
    products = [(query * ref[:, :cols].astype(F32)).astype(BF16) for ref in keyvals]
    scores = jnp.dot(jnp.concatenate(products, axis=0), gather, preferred_element_type=F32)
    masked, valids = [], []
    for index, (offset, reach) in enumerate(zip(offsets, (0, 1, 1, 2, 2))):
        score = scores[index * rows : (index + 1) * rows] / (float(head) ** 0.5)
        target = frame + offset
        inside = ((target >= 0) & (target < slots)).astype(F32)
        valid = (inside * (half >= reach).astype(F32)) > 0.5
        valids.append(valid)
        masked.append(jnp.where(valid, score, -1e30))
    top = masked[0]
    for value in masked[1:]:
        top = jnp.maximum(top, value)
    expo = [jnp.where(valid, jnp.exp(value - top), 0.0) for valid, value in zip(valids, masked)]
    total = expo[0]
    for value in expo[1:]:
        total = total + value
    probs = jnp.concatenate([(value / total).astype(BF16) for value in expo], axis=0)
    wide = jnp.dot(probs, spread, preferred_element_type=F32)
    mixed = jnp.zeros((rows, cols), F32)
    for index, ref in enumerate(keyvals):
        mixed = mixed + wide[index * rows : (index + 1) * rows] * ref[:, cols:].astype(F32)
    mixed = mixed.astype(BF16)
    for copy in copies[2:]:
        copy.wait()
    weight = [own_here[...].astype(F32)]
    weight += [ref[first : first + head, :].astype(F32) for ref in (w1, w2, w3)]
    weight = jnp.concatenate(weight, axis=0).astype(BF16)
    attn = jnp.dot(mixed, weight, preferred_element_type=F32).astype(BF16)
    tokens = rows // 4
    for block in range(4):
        place = (x_ref[0] ^ block) * tokens
        out_ref[pl.ds(pl.multiple_of(place, 16), tokens), :] = attn[block * tokens : (block + 1) * tokens]


def total_of(parts_ref, tokens):
    total = parts_ref[0:tokens, :].astype(F32)
    for block in range(1, parts_ref.shape[0] // tokens):
        total = total + parts_ref[block * tokens : (block + 1) * tokens, :].astype(F32)
    return total


def resid_kernel(parts_ref, tok_ref, resid_ref, normed_ref):
    tokens = resid_ref.shape[0]
    mod = mod_of(tok_ref, tokens)
    attn = total_of(parts_ref, tokens)
    resid = (tok_ref[0:tokens, :].astype(F32) + mod[2:3, :] * attn).astype(BF16)
    resid_ref[...] = resid
    normed_ref[...] = normalise(resid.astype(F32), mod[3:4, :], mod[4:5, :])


def mlp_kernel(hidden, normed_ref, m0, m1, m2, m3, part_ref):
    refs = (m0, m1, m2, m3)
    first = jnp.concatenate([ref[hidden:, :] for ref in refs], axis=0)
    wide = lax.dot_general(
        normed_ref[...], first, (((1,), (1,)), ((), ())), preferred_element_type=F32
    )
    active = jax.nn.gelu(wide, approximate=True).astype(BF16)
    second = jnp.concatenate([ref[:hidden, :] for ref in refs], axis=0)
    part_ref[...] = jnp.dot(active, second, preferred_element_type=F32).astype(BF16)


def final_kernel(slot_ref, parts_ref, resid_ref, tok_ref, fresh_ref, out_ref):
    tokens = resid_ref.shape[0]
    mod = mod_of(tok_ref, tokens)
    mlp = total_of(parts_ref, tokens)
    block_out = (resid_ref[...].astype(F32) + mod[5:6, :] * mlp).astype(BF16)
    out_ref[...] = jnp.where(slot_ref[0] == 0, fresh_ref[...].astype(F32), block_out.astype(F32)).astype(BF16)


SPECS = {
    "s": pl.BlockSpec(memory_space=pltpu.SMEM),
    "v": pl.BlockSpec(memory_space=pltpu.VMEM),
    "a": pl.BlockSpec(memory_space=pltpu.HBM),
}


def call(kernel, outs, kinds, *args, scratch=(), flops=0, limit=16):
    ins, back = ([SPECS[kind] for kind in part] for part in kinds.split(">"))
    args = [
        pltpu.with_memory_space_constraint(arg, pltpu.HBM) if kind == "a" else arg
        for arg, kind in zip(args, kinds)
    ]
    return pl.pallas_call(
        kernel,
        out_shape=outs,
        in_specs=ins,
        out_specs=tuple(back) if isinstance(outs, tuple) else back[0],
        scratch_shapes=scratch,
        compiler_params=pltpu.CompilerParams(vmem_limit_bytes=limit * MEGA),
        cost_estimate=pl.CostEstimate(flops=flops, bytes_accessed=1 << 20, transcendentals=0),
    )(*args)


def per_device(
    latents,
    fresh_noise,
    levels,
    modulation,
    head_map,
    window,
    qkv_weight,
    out_weight,
    fc1_weight,
    fc2_weight,
):
    tokens, width = latents.shape[1:]
    head = out_weight.shape[0]
    hidden = fc2_weight.shape[0]
    slots = lax.axis_size(SLOTS)
    slot = lax.axis_index(SLOTS)
    around = lax.axis_size("x")

    def shape(*dims, dtype=BF16):
        return jax.ShapeDtypeStruct(dims, dtype)

    payload, own_w = call(
        prepare_kernel,
        (shape(tokens + 32, width), shape(4 * head + 16, width)),
        "ssaaaaa>vv",
        levels,
        head_map,
        window,
        latents[0],
        modulation.transpose(1, 0, 2),
        qkv_weight.T,
        out_weight,
        scratch=[
            pltpu.SMEM(window.shape, jnp.int32),
            pltpu.VMEM((tokens, width), BF16),
            pltpu.VMEM((modulation.shape[1], 8, width), F32),
            pltpu.VMEM((3 * head, width), BF16),
            pltpu.VMEM((head, width), BF16),
            pltpu.SemaphoreType.DMA((5,)),
        ],
    )
    moved = lax.ppermute(payload, SLOTS, [(s, (s + 1) % slots) for s in range(slots)])
    core_w = lax.ppermute(own_w, "core", SWAP)
    near_w = lax.ppermute(own_w, "ylo", SWAP)
    far_w = lax.ppermute(own_w, ("yhi", "ylo", "core"), FAR)
    normed = call(norm_kernel, shape(tokens, width), "v>v", moved, flops=100 * 10**9)
    toks = [normed]
    toks += [lax.ppermute(normed, "x", [(x, x ^ j) for x in range(around)]) for j in range(1, around)]

    rows = around * tokens
    cols = 4 * head
    query, keyval, halfs, own_m = call(
        lambda *refs: qkv_kernel(head, *refs),
        (
            pltpu.HBM((rows, cols), BF16),
            shape(rows, 2 * cols),
            pltpu.HBM((8, 128), F32),
            shape(2 * hidden, width),
        ),
        "vvvvvvvvaa>avav",
        *toks,
        own_w,
        core_w,
        near_w,
        far_w,
        fc1_weight.T,
        fc2_weight,
        scratch=[
            pltpu.VMEM((rows, cols), BF16),
            pltpu.VMEM((8, 128), F32),
            pltpu.SemaphoreType.DMA((4,)),
        ],
    )
    ones = [(s, s ^ 1) for s in range(slots)]
    others = [(s, (((s - 1) ^ 1) + 1) % slots) for s in range(1, slots + 1)]
    others = [(s % slots, to) for s, to in others]
    twos = [(s, s ^ 2) for s in range(slots)]
    rest = [(s % slots, (((s - 2) ^ 2) + 2) % slots) for s in range(2, slots + 2)]
    arrived = [lax.ppermute(keyval, SLOTS, pairs) for pairs in (ones, others, twos, rest)]
    near_m = lax.ppermute(own_m, "ylo", SWAP)
    far_m = lax.ppermute(own_m, ("yhi", "ylo", "core"), FAR)
    core_m = lax.ppermute(lax.optimization_barrier((own_m, arrived[2]))[0], "core", SWAP)
    attended = call(
        lambda *refs: attention_kernel(head, slots, *refs),
        shape(rows, width),
        "ssaavvvvvavvv>v",
        slot.astype(jnp.int32)[None],
        lax.axis_index("x").astype(jnp.int32)[None],
        halfs,
        query,
        keyval,
        *arrived,
        out_weight,
        core_w,
        near_w,
        far_w,
        scratch=[
            pltpu.VMEM((8, 128), F32),
            pltpu.VMEM((rows, cols), BF16),
            pltpu.VMEM((head, width), BF16),
            pltpu.SemaphoreType.DMA((3,)),
        ],
        flops=100 * 10**9,
    )
    parts = lax.all_to_all(attended, "x", 0, 0, tiled=True)
    resid, normed = call(
        resid_kernel, (shape(tokens, width), shape(tokens, width)), "vv>vv", parts, moved
    )
    part = call(
        lambda *refs: mlp_kernel(hidden, *refs),
        shape(rows, width),
        "vvvvv>v",
        lax.all_gather(normed, "x", axis=0, tiled=True),
        own_m,
        core_m,
        near_m,
        far_m,
    )
    parts = lax.all_to_all(part, "x", 0, 0, tiled=True)
    return call(
        final_kernel,
        shape(tokens, width),
        "svvvv>v",
        slot[None].astype(jnp.int32),
        parts,
        resid,
        moved,
        fresh_noise,
    )[None]


def solution(mesh):
    split = Mesh(mesh.devices.reshape(2, 16, 4, 2, 2), ("yhi", "z", "x", "ylo", "core"))
    mp = ("x", "ylo", "core")
    in_specs = (
        P(SLOTS, mp, None),
        P(mp, None),
        P(SLOTS),
        P(),
        P(mp),
        P(),
        P(None, mp),
        P(mp, None),
        P(None, mp),
        P(mp, None),
    )
    return jax.shard_map(
        per_device, mesh=split, in_specs=in_specs, out_specs=P(SLOTS, mp, None), check_vma=False
    )
```

time: 118 us -> 108 us (0.915)
  the two profiles are of different devices: /device:TPU:32 before, /device:TPU:8 now
where the time goes in v3:
time: 108 us; the launch traced here: 107 us
  starting transfers between devices  46.1 us (43%)
  blocking collectives  37.2 us (34%)
  waiting for transfers between devices  11.5 us (11%)
  Pallas kernels  9.86 us (9%)
  between operations  1.51 us (1%)
  local copies, waits for them, and re-layouts  1.11 us (1%)
    ppermute x4, starting transfers between devices, per_device(): lax.ppermute(keyval, SLOTS, pairs)  14.1 us
    all_to_all x1, blocking collectives, per_device(): parts = lax.all_to_all(attended, 'x', 0, 0, tiled=True)  12.7 us
    all_gather x1, blocking collectives, per_device(): lax.all_gather(normed, 'x', axis=0, tiled=True)  12.6 us
    all_to_all x1, blocking collectives, per_device(): parts = lax.all_to_all(part, 'x', 0, 0, tiled=True)  11.9 us
    pallas_call x7, Pallas kernels, call(): pl.pallas_call(kernel, out_shape=outs, in_specs=ins, out_specs=tuple(back...  9.86 us
    ppermute x3, starting transfers between devices, per_device(): lax.ppermute(normed, 'x', [(x, x ^ j) for x in range(around)])  9.28 us
    ppermute x3, waiting for transfers between devices, per_device(): lax.ppermute(normed, 'x', [(x, x ^ j) for x in range(around)])  5.46 us
    ppermute x1, starting transfers between devices, per_device(): near_w = lax.ppermute(own_w, 'ylo', SWAP)  5.1 us
  transfers between devices with their start and end apart: 14, of which 6 were waited for; matrix products, arithmetic and copies ran while one was open for 0% of the time, Pallas kernels for 4%

profile of v3, /device:TPU:8, one launch (start us, length us, event | category | flops | bytes accessed | tf_op | source)
XLA Modules:
  0.0 107.3 jit_solution(16056709849984672459)
XLA Ops:
  1.3 1.3 %shard_map.100 = (bf16[80,1152]{1,0:T(8,128)(2,1)S(1)}, bf16[304,1152]{1,0:T(8,128)(2,1)S(1)}) custom-call(s32[1]{0:T(128)S(6)} %copy.11.levels_ref, s32[1]{0:T(128)S(6)} %copy.12.map_ref, s32[16]{0:T(128)} %window_ref.1, bf16[48,1152]{1,0:T(8,128)(2,1)} %bitcast.18, f32[6,32,1152]{2,1,0:T(8,128)} %bitcast.15, bf16[216,1152]{1,0:T(8,128)(2,1)} %bitcast.17, ...), custom_call_target="tpu_custom_call" | custom-call | bytes 1048576 | tf_op jit(solution)/shard_map/pallas_call | solution.py:221
  2.6 3.8 %collective-permute-start = (bf16[80,1152]{1,0:T(8,128)(2,1)S(1)}, bf16[80,1152]{1,0:T(8,128)(2,1)S(1)}, u32[]{:S(2)}, u32[]{:S(2)}) collective-permute-start(bf16[80,1152]{1,0:T(8,128)(2,1)S(1)} %get-tuple-element.14), channel_id=1, source_target_pairs={{0,16},{16,32},{32,48},{48,64},{64,80},{80,96},{96,112},{112,128},... | collective-permute-start | bytes 552968 | tf_op jit(solution)/shard_map/ppermute | solution.py:274
  6.4 2.6 %collective-permute-start.6 = (bf16[304,1152]{1,0:T(8,128)(2,1)S(1)}, bf16[304,1152]{1,0:T(8,128)(2,1)S(1)}, u32[]{:S(2)}, u32[]{:S(2)}) collective-permute-start(bf16[304,1152]{1,0:T(8,128)(2,1)S(1)} %get-tuple-element.15.refs_4_), channel_id=1, source_target_pairs={{0,259},{1,258},{258,1},{259,0},{2,257},{3,256},{256,3},{257,2},{4... | collective-permute-start | bytes 2101256 | tf_op jit(solution)/shard_map/ppermute | solution.py:277
  9.1 5.1 %collective-permute-start.5 = (bf16[304,1152]{1,0:T(8,128)(2,1)S(1)}, bf16[304,1152]{1,0:T(8,128)(2,1)S(1)}, u32[]{:S(2)}, u32[]{:S(2)}) collective-permute-start(bf16[304,1152]{1,0:T(8,128)(2,1)S(1)} %get-tuple-element.15.refs_4_), channel_id=1, source_target_pairs={{0,2},{2,0},{1,3},{3,1},{4,6},{6,4},{5,7},{7,5},{8,10},{10,8},{9,1... | collective-permute-start | bytes 2101256 | tf_op jit(solution)/shard_map/ppermute | solution.py:276
  14.2 1.9 %collective-permute-start.4 = (bf16[304,1152]{1,0:T(8,128)(2,1)S(1)}, bf16[304,1152]{1,0:T(8,128)(2,1)S(1)}, u32[]{:S(2)}, u32[]{:S(2)}) collective-permute-start(bf16[304,1152]{1,0:T(8,128)(2,1)S(1)} %get-tuple-element.15.refs_4_), channel_id=1, source_target_pairs={{0,1},{1,0},{2,3},{3,2},{4,5},{5,4},{6,7},{7,6},{8,9},{9,8},{10,11... | collective-permute-start | bytes 2101256 | tf_op jit(solution)/shard_map/ppermute | solution.py:275
  16.1 4.4 %collective-permute-done.tok_ref = bf16[80,1152]{1,0:T(8,128)(2,1)S(1)} collective-permute-done((bf16[80,1152]{1,0:T(8,128)(2,1)S(1)}, bf16[80,1152]{1,0:T(8,128)(2,1)S(1)}, u32[]{:S(2)}, u32[]{:S(2)}) %collective-permute-start) | collective-permute-done | bytes 184352 | tf_op jit(solution)/shard_map/ppermute | solution.py:274
  20.5 0.2 shard_map.101.refs_0_
  20.8 4.7 %collective-permute-start.3 = (bf16[48,1152]{1,0:T(8,128)(2,1)S(1)}, bf16[48,1152]{1,0:T(8,128)(2,1)S(1)}, u32[]{:S(2)}, u32[]{:S(2)}) collective-permute-start(bf16[48,1152]{1,0:T(8,128)(2,1)S(1)} %shard_map.101.refs_0_), channel_id=1, source_target_pairs={{0,12},{4,8},{8,4},{12,0},{1,13},{5,9},{9,5},{13,1},{2,14},{6,10},... | collective-permute-start | bytes 331784 | tf_op jit(solution)/shard_map/ppermute | solution.py:280
  25.4 2.7 %collective-permute-start.2 = (bf16[48,1152]{1,0:T(8,128)(2,1)S(1)}, bf16[48,1152]{1,0:T(8,128)(2,1)S(1)}, u32[]{:S(2)}, u32[]{:S(2)}) collective-permute-start(bf16[48,1152]{1,0:T(8,128)(2,1)S(1)} %shard_map.101.refs_0_), channel_id=1, source_target_pairs={{0,8},{4,12},{8,0},{12,4},{1,9},{5,13},{9,1},{13,5},{2,10},{6,14},... | collective-permute-start | bytes 331784 | tf_op jit(solution)/shard_map/ppermute | solution.py:280
  28.1 0.7 collective-permute-done.3.refs_3_
  28.9 1.9 %collective-permute-start.1 = (bf16[48,1152]{1,0:T(8,128)(2,1)S(1)}, bf16[48,1152]{1,0:T(8,128)(2,1)S(1)}, u32[]{:S(2)}, u32[]{:S(2)}) collective-permute-start(bf16[48,1152]{1,0:T(8,128)(2,1)S(1)} %shard_map.101.refs_0_), channel_id=1, source_target_pairs={{0,4},{4,0},{8,12},{12,8},{1,5},{5,1},{9,13},{13,9},{2,6},{6,2},{1... | collective-permute-start | bytes 331784 | tf_op jit(solution)/shard_map/ppermute | solution.py:280
  30.8 3.1 %collective-permute-done.2.refs_2_ = bf16[48,1152]{1,0:T(8,128)(2,1)S(1)} collective-permute-done((bf16[48,1152]{1,0:T(8,128)(2,1)S(1)}, bf16[48,1152]{1,0:T(8,128)(2,1)S(1)}, u32[]{:S(2)}, u32[]{:S(2)}) %collective-permute-start.2) | collective-permute-done | bytes 110624 | tf_op jit(solution)/shard_map/ppermute | solution.py:280
  33.9 1.7 %collective-permute-done.1.refs_1_ = bf16[48,1152]{1,0:T(8,128)(2,1)S(1)} collective-permute-done((bf16[48,1152]{1,0:T(8,128)(2,1)S(1)}, bf16[48,1152]{1,0:T(8,128)(2,1)S(1)}, u32[]{:S(2)}, u32[]{:S(2)}) %collective-permute-start.1) | collective-permute-done | bytes 110624 | tf_op jit(solution)/shard_map/ppermute | solution.py:280
  35.5 0.0 collective-permute-done.6.refs_7_.refs_12_
  35.5 0.0 collective-permute-done.5.refs_6_.refs_11_
  35.5 0.0 collective-permute-done.4.refs_5_.refs_10_
  35.5 0.0 copy-start
  35.5 2.2 %shard_map.102 = (bf16[192,288]{1,0:T(8,128)(2,1)}, bf16[192,576]{1,0:T(8,128)(2,1)S(1)}, f32[8,128]{1,0:T(8,128)}, bf16[576,1152]{1,0:T(8,128)(2,1)S(1)}) custom-call(bf16[48,1152]{1,0:T(8,128)(2,1)S(1)} %shard_map.101.refs_0_, bf16[48,1152]{1,0:T(8,128)(2,1)S(1)} %collective-permute-done.1.refs_1_, bf16[48,1152]{1,0:T(8,128)(2,1)S(1)} %collective-permute-done.2.refs_2_, ...), custom_call_target="tpu_custom_call" | custom-call | bytes 1048576 | tf_op jit(solution)/shard_map/pallas_call | solution.py:221
  37.7 0.0 copy-done
  37.7 1.9 %collective-permute-start.9 = (bf16[192,576]{1,0:T(8,128)(2,1)S(1)}, bf16[192,576]{1,0:T(8,128)(2,1)S(1)}, u32[]{:S(2)}, u32[]{:S(2)}) collective-permute-start(bf16[192,576]{1,0:T(8,128)(2,1)S(1)} %get-tuple-element.18.refs_4_), channel_id=1, source_target_pairs={{0,32},{16,48},{32,0},{48,16},{64,96},{80,112},{96,64},{112,80},{1... | collective-permute-start | bytes 663560 | tf_op jit(solution)/shard_map/ppermute | solution.py:311
  39.6 7.0 %collective-permute-start.10 = (bf16[192,576]{1,0:T(8,128)(2,1)S(1)}, bf16[192,576]{1,0:T(8,128)(2,1)}, u32[]{:S(2)}, u32[]{:S(2)}) collective-permute-start(bf16[192,576]{1,0:T(8,128)(2,1)S(1)} %get-tuple-element.18.refs_4_), channel_id=1, source_target_pairs={{32,64},{48,80},{64,32},{80,48},{96,128},{112,144},{128,96},{144,1... | collective-permute-start | bytes 663560 | tf_op jit(solution)/shard_map/ppermute | solution.py:311
  46.6 3.2 %collective-permute-start.8 = (bf16[192,576]{1,0:T(8,128)(2,1)S(1)}, bf16[192,576]{1,0:T(8,128)(2,1)}, u32[]{:S(2)}, u32[]{:S(2)}) collective-permute-start(bf16[192,576]{1,0:T(8,128)(2,1)S(1)} %get-tuple-element.18.refs_4_), channel_id=1, source_target_pairs={{16,32},{32,16},{48,64},{64,48},{80,96},{96,80},{112,128},{128,112... | collective-permute-start | bytes 663560 | tf_op jit(solution)/shard_map/ppermute | solution.py:311
  49.9 2.0 %collective-permute-start.7 = (bf16[192,576]{1,0:T(8,128)(2,1)S(1)}, bf16[192,576]{1,0:T(8,128)(2,1)}, u32[]{:S(2)}, u32[]{:S(2)}) collective-permute-start(bf16[192,576]{1,0:T(8,128)(2,1)S(1)} %get-tuple-element.18.refs_4_), channel_id=1, source_target_pairs={{0,16},{16,0},{32,48},{48,32},{64,80},{80,64},{96,112},{112,96},{1... | collective-permute-start | bytes 663560 | tf_op jit(solution)/shard_map/ppermute | solution.py:311
  51.9 2.6 %collective-permute-start.13 = (bf16[576,1152]{1,0:T(8,128)(2,1)S(1)}, bf16[576,1152]{1,0:T(8,128)(2,1)S(1)}, u32[]{:S(2)}, u32[]{:S(2)}) collective-permute-start(bf16[576,1152]{1,0:T(8,128)(2,1)S(1)} %get-tuple-element.21.refs_1_), channel_id=1, source_target_pairs={{0,259},{1,258},{258,1},{259,0},{2,257},{3,256},{256,3},{257,2},{4... | collective-permute-start | bytes 3981320 | tf_op jit(solution)/shard_map/ppermute | solution.py:313
  54.5 0.0 collective-permute-done.9.refs_7_
  54.5 3.3 %collective-permute-start.12 = (bf16[576,1152]{1,0:T(8,128)(2,1)S(1)}, bf16[576,1152]{1,0:T(8,128)(2,1)S(1)}, u32[]{:S(2)}, u32[]{:S(2)}) collective-permute-start(bf16[576,1152]{1,0:T(8,128)(2,1)S(1)} %get-tuple-element.21.refs_1_), channel_id=1, source_target_pairs={{0,2},{2,0},{1,3},{3,1},{4,6},{6,4},{5,7},{7,5},{8,10},{10,8},{9,1... | collective-permute-start | bytes 3981320 | tf_op jit(solution)/shard_map/ppermute | solution.py:312
  57.8 0.4 collective-permute-done.10.refs_8_
  58.2 3.4 %collective-permute-start.11 = (bf16[576,1152]{1,0:T(8,128)(2,1)S(1)}, bf16[576,1152]{1,0:T(8,128)(2,1)S(1)}, u32[]{:S(2)}, u32[]{:S(2)}) collective-permute-start(bf16[576,1152]{1,0:T(8,128)(2,1)S(1)} %get-tuple-element.21.refs_1_), channel_id=1, source_target_pairs={{0,1},{1,0},{2,3},{3,2},{4,5},{5,4},{6,7},{7,6},{8,9},{9,8},{10,11... | collective-permute-start | bytes 3981320 | tf_op jit(solution)/shard_map/ppermute | solution.py:314
  61.6 1.2 %collective-permute-done.8.refs_6_ = bf16[192,576]{1,0:T(8,128)(2,1)} collective-permute-done((bf16[192,576]{1,0:T(8,128)(2,1)S(1)}, bf16[192,576]{1,0:T(8,128)(2,1)}, u32[]{:S(2)}, u32[]{:S(2)}) %collective-permute-start.8) | collective-permute-done | bytes 221216 | tf_op jit(solution)/shard_map/ppermute | solution.py:311
  62.8 0.0 collective-permute-done.7.refs_5_
  62.8 0.0 copy-start.1
  62.8 1.1 %copy-done.1 = bf16[304,1152]{1,0:T(8,128)(2,1)S(1)} copy-done((bf16[304,1152]{1,0:T(8,128)(2,1)S(1)}, bf16[304,1152]{1,0:T(8,128)(2,1)}, u32[]{:S(2)}) %copy-start.1) | copy-done | bytes 700440
  63.9 3.4 %shard_map.103 = bf16[192,1152]{1,0:T(8,128)(2,1)S(1)} custom-call(s32[1]{0:T(128)} %bitcast.refs_0_.slot_ref, s32[1]{0:T(128)} %bitcast.1.refs_1_, f32[8,128]{1,0:T(8,128)} %get-tuple-element.16.refs_2_, bf16[192,288]{1,0:T(8,128)(2,1)} %get-tuple-element.17.refs_3_, bf16[192,576]{1,0:T(8,128)(2,1)S(1)} %get-tuple-element.18.refs_4_, ...), custom_call_target="tpu_custom_call" | custom-call | flops 99999997952 | bytes 1048576 | tf_op jit(solution)/shard_map/pallas_call | solution.py:221
  67.3 12.7 %all_to_all.22 = bf16[4,48,1152]{2,1,0:T(8,128)(2,1)S(1)} all-to-all(bf16[4,48,1152]{2,1,0:T(8,128)(2,1)S(1)} %bitcast.14), channel_id=1, replica_groups=mesh['yhi'=2,'z'=16,'x'=4,'ylo'=2,'core'=2] {'x'}, dimensions={0} | all-to-all | bytes 884736 | tf_op jit(solution)/shard_map/all_to_all | solution.py:337
  80.0 0.3 shard_map.104
  80.3 12.6 %all_gather.3.refs_0_ = bf16[192,1152]{1,0:T(8,128)(2,1)S(1)} all-gather(bf16[48,1152]{1,0:T(8,128)(2,1)S(1)} %get-tuple-element.19), channel_id=1, replica_groups=mesh['yhi'=2,'z'=16,'x'=4,'ylo'=2,'core'=2] {'x'}, dimensions={0}, use_global_device_ids=true | all-gather | bytes 552960 | tf_op jit(solution)/shard_map/all_gather | solution.py:345
  92.9 0.0 copy-start.2
  92.9 0.0 collective-permute-done.13.refs_4_
  92.9 0.0 collective-permute-done.12.refs_3_
  92.9 0.0 collective-permute-done.11.refs_2_
  92.9 1.7 %shard_map.105 = bf16[192,1152]{1,0:T(8,128)(2,1)S(1)} custom-call(bf16[192,1152]{1,0:T(8,128)(2,1)S(1)} %all_gather.3.refs_0_, bf16[576,1152]{1,0:T(8,128)(2,1)S(1)} %get-tuple-element.21.refs_1_, bf16[576,1152]{1,0:T(8,128)(2,1)S(1)} %collective-permute-done.11.refs_2_, bf16[576,1152]{1,0:T(8,128)(2,1)S(1)} %collective-permute-done.12.refs_3_, ...), custom_call_target="tpu_custom_call" | custom-call | bytes 1048576 | tf_op jit(solution)/shard_map/pallas_call | solution.py:221
  94.6 11.9 %all_to_all.23 = bf16[4,48,1152]{2,1,0:T(8,128)(2,1)S(1)} all-to-all(bf16[4,48,1152]{2,1,0:T(8,128)(2,1)S(1)} %bitcast.11), channel_id=1, replica_groups=mesh['yhi'=2,'z'=16,'x'=4,'ylo'=2,'core'=2] {'x'}, dimensions={0} | all-to-all | bytes 884736 | tf_op jit(solution)/shard_map/all_to_all | solution.py:351
  106.6 0.0 copy-done.2
  106.6 0.7 shard_map.106
Async XLA Ops:
  2.6 17.9 %collective-permute-start = (bf16[80,1152]{1,0:T(8,128)(2,1)S(1)}, bf16[80,1152]{1,0:T(8,128)(2,1)S(1)}, u32[]{:S(2)}, u32[]{:S(2)}) collective-permute-start(bf16[80,1152]{1,0:T(8,128)(2,1)S(1)} %get-tuple-element.14), channel_id=1, source_target_pairs={{0,16},{16,32},{32,48},{48,64},{64,80},{80,96},{96,112},{112,128},... | collective-permute-start | bytes 552968 | tf_op jit(solution)/shard_map/ppermute | solution.py:274
  6.4 29.1 %collective-permute-start.6 = (bf16[304,1152]{1,0:T(8,128)(2,1)S(1)}, bf16[304,1152]{1,0:T(8,128)(2,1)S(1)}, u32[]{:S(2)}, u32[]{:S(2)}) collective-permute-start(bf16[304,1152]{1,0:T(8,128)(2,1)S(1)} %get-tuple-element.15.refs_4_), channel_id=1, source_target_pairs={{0,259},{1,258},{258,1},{259,0},{2,257},{3,256},{256,3},{257,2},{4... | collective-permute-start | bytes 2101256 | tf_op jit(solution)/shard_map/ppermute | solution.py:277
  9.1 26.4 %collective-permute-start.5 = (bf16[304,1152]{1,0:T(8,128)(2,1)S(1)}, bf16[304,1152]{1,0:T(8,128)(2,1)S(1)}, u32[]{:S(2)}, u32[]{:S(2)}) collective-permute-start(bf16[304,1152]{1,0:T(8,128)(2,1)S(1)} %get-tuple-element.15.refs_4_), channel_id=1, source_target_pairs={{0,2},{2,0},{1,3},{3,1},{4,6},{6,4},{5,7},{7,5},{8,10},{10,8},{9,1... | collective-permute-start | bytes 2101256 | tf_op jit(solution)/shard_map/ppermute | solution.py:276
  14.2 21.3 %collective-permute-start.4 = (bf16[304,1152]{1,0:T(8,128)(2,1)S(1)}, bf16[304,1152]{1,0:T(8,128)(2,1)S(1)}, u32[]{:S(2)}, u32[]{:S(2)}) collective-permute-start(bf16[304,1152]{1,0:T(8,128)(2,1)S(1)} %get-tuple-element.15.refs_4_), channel_id=1, source_target_pairs={{0,1},{1,0},{2,3},{3,2},{4,5},{5,4},{6,7},{7,6},{8,9},{9,8},{10,11... | collective-permute-start | bytes 2101256 | tf_op jit(solution)/shard_map/ppermute | solution.py:275
  20.8 8.1 %collective-permute-start.3 = (bf16[48,1152]{1,0:T(8,128)(2,1)S(1)}, bf16[48,1152]{1,0:T(8,128)(2,1)S(1)}, u32[]{:S(2)}, u32[]{:S(2)}) collective-permute-start(bf16[48,1152]{1,0:T(8,128)(2,1)S(1)} %shard_map.101.refs_0_), channel_id=1, source_target_pairs={{0,12},{4,8},{8,4},{12,0},{1,13},{5,9},{9,5},{13,1},{2,14},{6,10},... | collective-permute-start | bytes 331784 | tf_op jit(solution)/shard_map/ppermute | solution.py:280
  25.4 8.4 %collective-permute-start.2 = (bf16[48,1152]{1,0:T(8,128)(2,1)S(1)}, bf16[48,1152]{1,0:T(8,128)(2,1)S(1)}, u32[]{:S(2)}, u32[]{:S(2)}) collective-permute-start(bf16[48,1152]{1,0:T(8,128)(2,1)S(1)} %shard_map.101.refs_0_), channel_id=1, source_target_pairs={{0,8},{4,12},{8,0},{12,4},{1,9},{5,13},{9,1},{13,5},{2,10},{6,14},... | collective-permute-start | bytes 331784 | tf_op jit(solution)/shard_map/ppermute | solution.py:280
  28.9 6.6 %collective-permute-start.1 = (bf16[48,1152]{1,0:T(8,128)(2,1)S(1)}, bf16[48,1152]{1,0:T(8,128)(2,1)S(1)}, u32[]{:S(2)}, u32[]{:S(2)}) collective-permute-start(bf16[48,1152]{1,0:T(8,128)(2,1)S(1)} %shard_map.101.refs_0_), channel_id=1, source_target_pairs={{0,4},{4,0},{8,12},{12,8},{1,5},{5,1},{9,13},{13,9},{2,6},{6,2},{1... | collective-permute-start | bytes 331784 | tf_op jit(solution)/shard_map/ppermute | solution.py:280
  35.5 2.2 %copy-start = (bf16[304,1152]{1,0:T(8,128)(2,1)}, bf16[304,1152]{1,0:T(8,128)(2,1)S(1)}, u32[]{:S(2)}) copy-start(bf16[304,1152]{1,0:T(8,128)(2,1)S(1)} %collective-permute-done.4.refs_5_.refs_10_) | copy-start | bytes 2101252
  37.7 16.8 %collective-permute-start.9 = (bf16[192,576]{1,0:T(8,128)(2,1)S(1)}, bf16[192,576]{1,0:T(8,128)(2,1)S(1)}, u32[]{:S(2)}, u32[]{:S(2)}) collective-permute-start(bf16[192,576]{1,0:T(8,128)(2,1)S(1)} %get-tuple-element.18.refs_4_), channel_id=1, source_target_pairs={{0,32},{16,48},{32,0},{48,16},{64,96},{80,112},{96,64},{112,80},{1... | collective-permute-start | bytes 663560 | tf_op jit(solution)/shard_map/ppermute | solution.py:311
  39.6 18.5 %collective-permute-start.10 = (bf16[192,576]{1,0:T(8,128)(2,1)S(1)}, bf16[192,576]{1,0:T(8,128)(2,1)}, u32[]{:S(2)}, u32[]{:S(2)}) collective-permute-start(bf16[192,576]{1,0:T(8,128)(2,1)S(1)} %get-tuple-element.18.refs_4_), channel_id=1, source_target_pairs={{32,64},{48,80},{64,32},{80,48},{96,128},{112,144},{128,96},{144,1... | collective-permute-start | bytes 663560 | tf_op jit(solution)/shard_map/ppermute | solution.py:311
  46.6 16.1 %collective-permute-start.8 = (bf16[192,576]{1,0:T(8,128)(2,1)S(1)}, bf16[192,576]{1,0:T(8,128)(2,1)}, u32[]{:S(2)}, u32[]{:S(2)}) collective-permute-start(bf16[192,576]{1,0:T(8,128)(2,1)S(1)} %get-tuple-element.18.refs_4_), channel_id=1, source_target_pairs={{16,32},{32,16},{48,64},{64,48},{80,96},{96,80},{112,128},{128,112... | collective-permute-start | bytes 663560 | tf_op jit(solution)/shard_map/ppermute | solution.py:311
  49.9 12.9 %collective-permute-start.7 = (bf16[192,576]{1,0:T(8,128)(2,1)S(1)}, bf16[192,576]{1,0:T(8,128)(2,1)}, u32[]{:S(2)}, u32[]{:S(2)}) collective-permute-start(bf16[192,576]{1,0:T(8,128)(2,1)S(1)} %get-tuple-element.18.refs_4_), channel_id=1, source_target_pairs={{0,16},{16,0},{32,48},{48,32},{64,80},{80,64},{96,112},{112,96},{1... | collective-permute-start | bytes 663560 | tf_op jit(solution)/shard_map/ppermute | solution.py:311
  51.9 41.0 %collective-permute-start.13 = (bf16[576,1152]{1,0:T(8,128)(2,1)S(1)}, bf16[576,1152]{1,0:T(8,128)(2,1)S(1)}, u32[]{:S(2)}, u32[]{:S(2)}) collective-permute-start(bf16[576,1152]{1,0:T(8,128)(2,1)S(1)} %get-tuple-element.21.refs_1_), channel_id=1, source_target_pairs={{0,259},{1,258},{258,1},{259,0},{2,257},{3,256},{256,3},{257,2},{4... | collective-permute-start | bytes 3981320 | tf_op jit(solution)/shard_map/ppermute | solution.py:313
  54.5 38.4 %collective-permute-start.12 = (bf16[576,1152]{1,0:T(8,128)(2,1)S(1)}, bf16[576,1152]{1,0:T(8,128)(2,1)S(1)}, u32[]{:S(2)}, u32[]{:S(2)}) collective-permute-start(bf16[576,1152]{1,0:T(8,128)(2,1)S(1)} %get-tuple-element.21.refs_1_), channel_id=1, source_target_pairs={{0,2},{2,0},{1,3},{3,1},{4,6},{6,4},{5,7},{7,5},{8,10},{10,8},{9,1... | collective-permute-start | bytes 3981320 | tf_op jit(solution)/shard_map/ppermute | solution.py:312
  58.2 34.7 %collective-permute-start.11 = (bf16[576,1152]{1,0:T(8,128)(2,1)S(1)}, bf16[576,1152]{1,0:T(8,128)(2,1)S(1)}, u32[]{:S(2)}, u32[]{:S(2)}) collective-permute-start(bf16[576,1152]{1,0:T(8,128)(2,1)S(1)} %get-tuple-element.21.refs_1_), channel_id=1, source_target_pairs={{0,1},{1,0},{2,3},{3,2},{4,5},{5,4},{6,7},{7,6},{8,9},{9,8},{10,11... | collective-permute-start | bytes 3981320 | tf_op jit(solution)/shard_map/ppermute | solution.py:314
  62.8 1.1 %copy-start.1 = (bf16[304,1152]{1,0:T(8,128)(2,1)S(1)}, bf16[304,1152]{1,0:T(8,128)(2,1)}, u32[]{:S(2)}) copy-start(bf16[304,1152]{1,0:T(8,128)(2,1)} %copy-done) | copy-start | bytes 2101252
  92.9 13.7 %copy-start.2 = (bf16[48,1152]{1,0:T(8,128)(2,1)S(1)}, bf16[48,1152]{1,0:T(8,128)(2,1)}, u32[]{:S(2)}) copy-start(bf16[48,1152]{1,0:T(8,128)(2,1)} %fresh_ref.1) | copy-start | bytes 331780

commit v4 on v3

v4 whole, which is shorter than its diff:
```python
import jax
import jax.numpy as jnp
from jax import lax
from jax.experimental import pallas as pl
from jax.experimental.pallas import tpu as pltpu
from jax.sharding import Mesh
from jax.sharding import PartitionSpec as P

MEGA = 1024 * 1024
BF16, F32 = jnp.bfloat16, jnp.float32
SLOTS = ("yhi", "z")
SWAP = [(0, 1), (1, 0)]
FAR_Y = [(0, 3), (3, 0), (1, 2), (2, 1)]
FAR = [(2 * y + core, 2 * to + 1 - core) for y, to in FAR_Y for core in range(2)]


def normalise(floats, shift, scale):
    center = jnp.mean(floats, axis=-1, keepdims=True)
    spread = jnp.mean((floats - center) ** 2, axis=-1, keepdims=True)
    return ((floats - center) * lax.rsqrt(spread + 1e-06) * (1.0 + scale) + shift).astype(BF16)


def start_all(pairs, sems):
    copies = [pltpu.make_async_copy(src, dst, sems.at[i]) for i, (src, dst) in enumerate(pairs)]
    for copy in copies:
        copy.start()
    return copies


def payload_kernel(levels_ref, latents_ref, mods_ref, tok_ref, latents_here, mods_here, sems):
    tokens, width = latents_ref.shape
    level = levels_ref[0]
    group = pl.multiple_of(level // 8 * 8, 8)
    copies = start_all(
        [(mods_ref.at[:, pl.ds(group, 8), :], mods_here), (latents_ref, latents_here)], sems
    )
    copies[0].wait()
    chosen = lax.broadcasted_iota(jnp.int32, (8, width), 0) == level - group
    picked = [
        jnp.sum(jnp.where(chosen, mods_here[index], 0.0), axis=0, keepdims=True)
        for index in range(mods_here.shape[0])
    ]
    whole = jnp.concatenate(picked + picked[:2], axis=0)
    high = whole.astype(BF16).astype(F32)
    tok_ref[tokens:, :] = jnp.concatenate([high, whole - high], axis=0).astype(BF16)
    copies[1].wait()
    tok_ref[0:tokens, :] = latents_here[...]


def weight_kernel(
    map_ref, window_ref, qkv_ref, out_ref, packed_ref, window_here, qkv_here, out_here, sems
):
    lines, width = qkv_ref.shape
    rows = out_ref.shape[0]
    copies = start_all(
        [(window_ref, window_here), (qkv_ref, qkv_here), (out_ref, out_here)], sems
    )
    packed_ref[lines + 8 + rows :, :] = jnp.zeros((8, width), BF16)
    copies[0].wait()
    half = jnp.full((8, width), window_here[map_ref[0]].astype(F32))
    packed_ref[lines : lines + 8, :] = half.astype(BF16)
    copies[1].wait()
    packed_ref[0:lines, :] = qkv_here[...]
    copies[2].wait()
    packed_ref[lines + 8 : lines + 8 + rows, :] = out_here[...]


def join_mlp(fc1_ref, fc2_ref, to_ref, start, sems):
    hidden = fc2_ref.shape[0]
    return start_all(
        [
            (fc2_ref, to_ref.at[start : start + hidden]),
            (fc1_ref, to_ref.at[start + hidden : start + 2 * hidden]),
        ],
        sems,
    )


def whole_kernel(packed_ref, fc1_ref, fc2_ref, whole_ref, sems):
    start = packed_ref.shape[0]
    copies = join_mlp(fc1_ref, fc2_ref, whole_ref, start, sems)
    whole_ref[0:start, :] = packed_ref[...]
    for copy in copies:
        copy.wait()


def mod_of(tok_ref, tokens):
    terms = tok_ref[tokens:, :].astype(F32)
    return terms[0:8] + terms[8:16]


def fill(ref, value):
    rows = value.shape[0]
    for block in range(ref.shape[0] // rows):
        ref[block * rows : (block + 1) * rows, :] = value


def norm_kernel(tokens, tok_ref, normed_ref):
    mod = mod_of(tok_ref, tokens)
    fill(normed_ref, normalise(tok_ref[0:tokens, :].astype(F32), mod[0:1, :], mod[1:2, :]))


def project(head, normed, weight):
    return lax.dot_general(
        normed, weight[0 : 3 * head, :], (((1,), (1,)), ((), ())), preferred_element_type=F32
    )


def some_qkv_kernel(head, tok_ref, w0, w1, w2, fc1_ref, fc2_ref, part_ref, mlp_ref, sems):
    copies = join_mlp(fc1_ref, fc2_ref, mlp_ref, 0, sems)
    for slot, weight in enumerate((w0, w1, w2)):
        part_ref[slot, :, :] = project(head, tok_ref[...], weight).astype(BF16)
    for copy in copies:
        copy.wait()


def last_qkv_kernel(
    head, tok_ref, part_ref, w0, w1, w2, w3, q_ref, kv_ref, half_ref, outs_ref,
    q_here, half_here, outs_here, sems,
):
    first = 3 * head + 8
    weights = (w0, w1, w2, w3)
    outs = [ref[first : first + head, :].astype(F32) for ref in weights]
    outs_here[...] = jnp.concatenate(outs, axis=0).astype(BF16)
    copies = start_all([(outs_here, outs_ref)], sems)
    parts = [part_ref[slot].astype(F32) for slot in range(3)] + [project(head, tok_ref[...], w3)]
    query = jnp.concatenate([part[:, :head] for part in parts], axis=1)
    q_here[...] = query.astype(BF16)
    lane = lax.broadcasted_iota(jnp.int32, half_here.shape, 1)
    half = jnp.zeros(half_here.shape, F32)
    for slot, weight in enumerate(weights):
        mark = weight[3 * head - 8 : 3 * head + 8, 0:128].astype(F32)[8:16]
        half = jnp.where(lane == slot, mark, half)
    half_here[...] = half
    copies += start_all([(half_here, half_ref), (q_here, q_ref)], sems.at[1:3])
    keys = [part[:, head : 2 * head] for part in parts]
    keyval = jnp.concatenate(keys + [part[:, 2 * head :] for part in parts], axis=1)
    middle = keyval.shape[0] // 2
    kv_ref[...] = jnp.concatenate([keyval[:middle], keyval[middle:]], axis=1).astype(BF16)
    for copy in copies:
        copy.wait()


def indicators(head, cols):
    col = lax.broadcasted_iota(jnp.int32, (cols, 128), 0)
    lane = lax.broadcasted_iota(jnp.int32, (cols, 128), 1)
    gather = ((col >= lane * head) & (col < (lane + 1) * head)).astype(F32).astype(BF16)
    col = lax.broadcasted_iota(jnp.int32, (128, cols), 1)
    lane = lax.broadcasted_iota(jnp.int32, (128, cols), 0)
    spread = ((col >= lane * head) & (col < (lane + 1) * head)).astype(F32).astype(BF16)
    return gather, spread


def masked_scores(head, slots, place, half, query, gather, refs, offsets, reaches):
    rows, cols = query.shape
    frame = lax.rem(place + slots - 1, slots)
    products = [(query * unpack(ref, cols, 0)).astype(BF16) for ref in refs]
    scores = jnp.dot(jnp.concatenate(products, axis=0), gather, preferred_element_type=F32)
    masked, valids = [], []
    for index, (offset, reach) in enumerate(zip(offsets, reaches)):
        score = scores[index * rows : (index + 1) * rows] / (float(head) ** 0.5)
        target = frame + offset
        inside = ((target >= 0) & (target < slots)).astype(F32)
        valid = (inside * (half >= reach).astype(F32)) > 0.5
        valids.append(valid)
        masked.append(jnp.where(valid, score, -1e30))
    return masked, valids


def unpack(ref, cols, start):
    floats = ref[...].astype(F32)
    lanes = 2 * cols
    return jnp.concatenate(
        [floats[:, start : start + cols], floats[:, lanes + start : lanes + start + cols]], axis=0
    )


def early_kernel(
    head, slots, slot_ref, half_ref, q_ref, k0, k1, k2, outs_ref,
    half_here, q_here, outs_here, mixed_ref, top_ref, total_ref, sems,
):
    rows, cols = q_ref.shape
    copies = start_all([(half_ref, half_here), (q_ref, q_here), (outs_ref, outs_here)], sems)
    gather, spread = indicators(head, cols)
    place = slot_ref[0]
    copies[0].wait()
    copies[1].wait()
    refs = (k0, k1, k2)
    masked, valids = masked_scores(
        head, slots, place, half_here[0:1, :], q_here[...].astype(F32), gather, refs,
        (0, 2 * (place & 2) - 2, 2 * (place & 1) - 1), (0, 2, 1),
    )
    top = jnp.maximum(jnp.maximum(masked[0], masked[1]), masked[2])
    expo = [jnp.where(valid, jnp.exp(value - top), 0.0) for valid, value in zip(valids, masked)]
    top_ref[...] = top
    total_ref[...] = expo[0] + expo[1] + expo[2]
    wide = jnp.dot(
        jnp.concatenate(expo, axis=0).astype(BF16), spread, preferred_element_type=F32
    )
    mixed = jnp.zeros((rows, cols), F32)
    for index, ref in enumerate(refs):
        mixed = mixed + wide[index * rows : (index + 1) * rows] * unpack(ref, cols, cols)
    mixed_ref[...] = mixed
    copies[2].wait()


def late_kernel(
    head, slots, slot_ref, half_here, q_here, k3, k4, outs_here, mixed_ref, top_ref, total_ref, out_ref
):
    rows, cols = q_here.shape
    gather, spread = indicators(head, cols)
    place = slot_ref[0]
    refs = (k3, k4)
    masked, valids = masked_scores(
        head, slots, place, half_here[0:1, :], q_here[...].astype(F32), gather, refs,
        (2 - 2 * (place & 2), 1 - 2 * (place & 1)), (2, 1),
    )
    before = top_ref[...]
    top = jnp.maximum(jnp.maximum(masked[0], masked[1]), before)
    expo = [jnp.where(valid, jnp.exp(value - top), 0.0) for valid, value in zip(valids, masked)]
    scale = jnp.exp(before - top)
    total = total_ref[...] * scale + expo[0] + expo[1]
    shares = [(value / total).astype(BF16) for value in [scale] + expo]
    wide = jnp.dot(jnp.concatenate(shares, axis=0), spread, preferred_element_type=F32)
    mixed = wide[:rows] * mixed_ref[...]
    for index, ref in enumerate(refs):
        mixed = mixed + wide[(index + 1) * rows : (index + 2) * rows] * unpack(ref, cols, cols)
    out_ref[...] = jnp.dot(
        mixed.astype(BF16), outs_here[...], preferred_element_type=F32
    ).astype(BF16)


def total_of(parts_ref, tokens):
    total = parts_ref[0:tokens, :].astype(F32)
    for block in range(1, parts_ref.shape[0] // tokens):
        total = total + parts_ref[block * tokens : (block + 1) * tokens, :].astype(F32)
    return total


def resid_kernel(parts_ref, tok_ref, resid_ref, normed_ref):
    tokens = resid_ref.shape[0]
    mod = mod_of(tok_ref, tokens)
    attn = total_of(parts_ref, tokens)
    resid = (tok_ref[0:tokens, :].astype(F32) + mod[2:3, :] * attn).astype(BF16)
    resid_ref[...] = resid
    fill(normed_ref, normalise(resid.astype(F32), mod[3:4, :], mod[4:5, :]))


def mlp_of(hidden, normed, refs):
    first = jnp.concatenate([ref[ref.shape[0] - hidden :, :] for ref in refs], axis=0)
    wide = lax.dot_general(
        normed, first, (((1,), (1,)), ((), ())), preferred_element_type=F32
    )
    active = jax.nn.gelu(wide, approximate=True).astype(BF16)
    second = jnp.concatenate(
        [ref[ref.shape[0] - 2 * hidden : ref.shape[0] - hidden, :] for ref in refs], axis=0
    )
    return jnp.dot(active, second, preferred_element_type=F32)


def some_mlp_kernel(hidden, normed_ref, m0, m1, m2, sum_ref):
    sum_ref[...] = mlp_of(hidden, normed_ref[...], (m0, m1, m2))


def last_mlp_kernel(hidden, normed_ref, m3, sum_ref, part_ref):
    part_ref[...] = (sum_ref[...] + mlp_of(hidden, normed_ref[...], (m3,))).astype(BF16)


def final_kernel(slot_ref, parts_ref, resid_ref, tok_ref, fresh_ref, out_ref):
    tokens = resid_ref.shape[0]
    mod = mod_of(tok_ref, tokens)
    mlp = total_of(parts_ref, tokens)
    block_out = (resid_ref[...].astype(F32) + mod[5:6, :] * mlp).astype(BF16)
    out_ref[...] = jnp.where(slot_ref[0] == 0, fresh_ref[...].astype(F32), block_out.astype(F32)).astype(BF16)


SPECS = {
    "s": pl.BlockSpec(memory_space=pltpu.SMEM),
    "v": pl.BlockSpec(memory_space=pltpu.VMEM),
    "a": pl.BlockSpec(memory_space=pltpu.HBM),
}


def call(kernel, outs, kinds, *args, scratch=(), flops=0, limit=16):
    ins, back = ([SPECS[kind] for kind in part] for part in kinds.split(">"))
    args = [
        pltpu.with_memory_space_constraint(arg, pltpu.HBM) if kind == "a" else arg
        for arg, kind in zip(args, kinds)
    ]
    return pl.pallas_call(
        kernel,
        out_shape=outs,
        in_specs=ins,
        out_specs=tuple(back) if isinstance(outs, tuple) else back[0],
        scratch_shapes=scratch,
        compiler_params=pltpu.CompilerParams(vmem_limit_bytes=limit * MEGA),
        cost_estimate=pl.CostEstimate(flops=flops, bytes_accessed=1 << 20, transcendentals=0),
    )(*args)


def per_device(
    latents,
    fresh_noise,
    levels,
    modulation,
    head_map,
    window,
    qkv_weight,
    out_weight,
    fc1_weight,
    fc2_weight,
):
    tokens, width = latents.shape[1:]
    head = out_weight.shape[0]
    hidden = fc2_weight.shape[0]
    slots = lax.axis_size(SLOTS)
    slot = lax.axis_index(SLOTS)
    around = lax.axis_size("x")

    def shape(*dims, dtype=BF16):
        return jax.ShapeDtypeStruct(dims, dtype)

    payload = call(
        payload_kernel,
        shape(tokens + 16, width),
        "saa>v",
        levels,
        latents[0],
        modulation.transpose(1, 0, 2),
        scratch=[
            pltpu.VMEM((tokens, width), BF16),
            pltpu.VMEM((modulation.shape[1], 8, width), F32),
            pltpu.SemaphoreType.DMA((2,)),
        ],
    )
    moved = lax.ppermute(payload, SLOTS, [(s, (s + 1) % slots) for s in range(slots)])
    own_w = call(
        weight_kernel,
        shape(4 * head + 16, width),
        "saaa>v",
        head_map,
        window,
        qkv_weight.T,
        out_weight,
        scratch=[
            pltpu.SMEM(window.shape, jnp.int32),
            pltpu.VMEM((3 * head, width), BF16),
            pltpu.VMEM((head, width), BF16),
            pltpu.SemaphoreType.DMA((3,)),
        ],
    )
    near_w = lax.ppermute(own_w, "ylo", SWAP)
    far_w = lax.ppermute(own_w, ("yhi", "ylo", "core"), FAR)
    whole = call(
        whole_kernel,
        shape(4 * head + 16 + 2 * hidden, width),
        "vaa>v",
        own_w,
        fc1_weight.T,
        fc2_weight,
        scratch=[pltpu.SemaphoreType.DMA((2,))],
    )
    core_w = lax.ppermute(whole, "core", SWAP)
    rows = around * tokens
    cols = 4 * head
    normed = call(
        lambda *refs: norm_kernel(tokens, *refs), shape(rows, width), "v>v", moved, flops=100 * 10**9
    )
    tok = lax.all_to_all(normed, "x", 0, 0, tiled=True)
    part, own_m = call(
        lambda *refs: some_qkv_kernel(head, *refs),
        (shape(3, rows, 3 * head), shape(2 * hidden, width)),
        "vvvvaa>vv",
        tok,
        own_w,
        core_w,
        near_w,
        fc1_weight.T,
        fc2_weight,
        scratch=[pltpu.SemaphoreType.DMA((2,))],
    )
    query, keyval, halfs, outs = call(
        lambda *refs: last_qkv_kernel(head, *refs),
        (
            pltpu.HBM((rows, cols), BF16),
            shape(rows // 2, 4 * cols),
            pltpu.HBM((8, 128), F32),
            pltpu.HBM((cols, width), BF16),
        ),
        "vvvvvv>avaa",
        tok,
        part,
        own_w,
        core_w,
        near_w,
        far_w,
        scratch=[
            pltpu.VMEM((rows, cols), BF16),
            pltpu.VMEM((8, 128), F32),
            pltpu.VMEM((cols, width), BF16),
            pltpu.SemaphoreType.DMA((3,)),
        ],
    )
    ones = [(s, s ^ 1) for s in range(slots)]
    others = [(s, (((s - 1) ^ 1) + 1) % slots) for s in range(1, slots + 1)]
    others = [(s % slots, to) for s, to in others]
    twos = [(s, s ^ 2) for s in range(slots)]
    rest = [(s % slots, (((s - 2) ^ 2) + 2) % slots) for s in range(2, slots + 2)]
    arrived = [lax.ppermute(keyval, SLOTS, pairs) for pairs in (rest, others, twos, ones)]
    own_m, keyval = lax.optimization_barrier((own_m, keyval))
    near_m = lax.ppermute(own_m, "ylo", SWAP)
    far_m = lax.ppermute(own_m, ("yhi", "ylo", "core"), FAR)
    place = slot.astype(jnp.int32)[None]
    halfs, query, outs, mixed, top, total = call(
        lambda *refs: early_kernel(head, slots, *refs),
        (
            shape(8, 128, dtype=F32),
            shape(rows, cols),
            shape(cols, width),
            shape(rows, cols, dtype=F32),
            shape(rows, 128, dtype=F32),
            shape(rows, 128, dtype=F32),
        ),
        "saavvva>vvvvvv",
        place,
        halfs,
        query,
        keyval,
        *arrived[:2],
        outs,
        scratch=[pltpu.SemaphoreType.DMA((3,))],
    )
    attended = call(
        lambda *refs: late_kernel(head, slots, *refs),
        shape(rows, width),
        "svvvvvvvv>v",
        place,
        halfs,
        query,
        *arrived[2:],
        outs,
        mixed,
        top,
        total,
        flops=100 * 10**9,
    )
    parts = lax.all_to_all(attended, "x", 0, 0, tiled=True)
    resid, normed = call(
        resid_kernel, (shape(tokens, width), shape(rows, width)), "vv>vv", parts, moved
    )
    normed = lax.all_to_all(normed, "x", 0, 0, tiled=True)
    some = call(
        lambda *refs: some_mlp_kernel(hidden, *refs),
        shape(rows, width, dtype=F32),
        "vvvv>v",
        normed,
        own_m,
        core_w,
        near_m,
    )
    part = call(
        lambda *refs: last_mlp_kernel(hidden, *refs), shape(rows, width), "vvv>v", normed, far_m, some
    )
    parts = lax.all_to_all(part, "x", 0, 0, tiled=True)
    return call(
        final_kernel,
        shape(tokens, width),
        "svvvv>v",
        slot[None].astype(jnp.int32),
        parts,
        resid,
        moved,
        fresh_noise,
    )[None]


def solution(mesh):
    split = Mesh(mesh.devices.reshape(2, 16, 4, 2, 2), ("yhi", "z", "x", "ylo", "core"))
    mp = ("x", "ylo", "core")
    in_specs = (
        P(SLOTS, mp, None),
        P(mp, None),
        P(SLOTS),
        P(),
        P(mp),
        P(),
        P(None, mp),
        P(mp, None),
        P(None, mp),
        P(mp, None),
    )
    return jax.shard_map(
        per_device, mesh=split, in_specs=in_specs, out_specs=P(SLOTS, mp, None), check_vma=False
    )
```

time: 108 us -> 104 us (0.963)
  the two profiles are of different devices: /device:TPU:8 before, /device:TPU:32 now
where the time goes in v4:
time: 104 us; the launch traced here: 103 us
  blocking collectives  46.6 us (45%)
  starting transfers between devices  36.9 us (35%)
  Pallas kernels  15.2 us (15%)
  waiting for transfers between devices  3.03 us (3%)
  between operations  1.51 us (1%)
    ppermute x4, starting transfers between devices, per_device(): lax.ppermute(keyval, SLOTS, pairs)  18.8 us
    pallas_call x12, Pallas kernels, call(): pl.pallas_call(kernel, out_shape=outs, in_specs=ins, out_specs=tuple(back...  15.2 us
    all_to_all x1, blocking collectives, per_device(): tok = lax.all_to_all(normed, 'x', 0, 0, tiled=True)  12.9 us
    all_to_all x1, blocking collectives, per_device(): parts = lax.all_to_all(attended, 'x', 0, 0, tiled=True)  12.6 us
    all_to_all x1, blocking collectives, per_device(): parts = lax.all_to_all(part, 'x', 0, 0, tiled=True)  11.1 us
    all_to_all x1, blocking collectives, per_device(): normed = lax.all_to_all(normed, 'x', 0, 0, tiled=True)  10 us
    ppermute x1, starting transfers between devices, per_device(): lax.ppermute(payload, SLOTS, [(s, (s + 1) % slots) for s in range(slots)])  3.83 us
    ppermute x1, starting transfers between devices, per_device(): near_w = lax.ppermute(own_w, 'ylo', SWAP)  3.48 us
  transfers between devices with their start and end apart: 10, of which 3 were waited for; matrix products, arithmetic and copies ran while one was open for 0% of the time, Pallas kernels for 10%

profile of v4, /device:TPU:32, one launch (start us, length us, event | category | flops | bytes accessed | tf_op | source)
XLA Modules:
  0.0 103.2 jit_solution(17602995805028398474)
XLA Ops:
  0.7 1.0 %shard_map.100 = bf16[64,1152]{1,0:T(8,128)(2,1)S(1)} custom-call(s32[1]{0:T(128)S(6)} %copy.11.levels_ref, bf16[48,1152]{1,0:T(8,128)(2,1)} %bitcast.28, f32[6,32,1152]{2,1,0:T(8,128)} %bitcast.26), custom_call_target="tpu_custom_call" | custom-call | bytes 1048576 | tf_op jit(solution)/shard_map/pallas_call | solution.py:290
  1.7 3.8 %collective-permute-start = (bf16[64,1152]{1,0:T(8,128)(2,1)S(1)}, bf16[64,1152]{1,0:T(8,128)(2,1)S(1)}, u32[]{:S(2)}, u32[]{:S(2)}) collective-permute-start(bf16[64,1152]{1,0:T(8,128)(2,1)S(1)} %shard_map.100), channel_id=1, source_target_pairs={{0,16},{16,32},{32,48},{48,64},{64,80},{80,96},{96,112},{112,128},... | collective-permute-start | bytes 442376 | tf_op jit(solution)/shard_map/ppermute | solution.py:336
  6.2 1.1 %shard_map.102.packed_ref.refs_1_.refs_2_ = bf16[304,1152]{1,0:T(8,128)(2,1)S(1)} custom-call(s32[1]{0:T(128)S(6)} %copy.12.map_ref, s32[16]{0:T(128)} %window_ref.1, bf16[216,1152]{1,0:T(8,128)(2,1)} %bitcast.27, bf16[72,1152]{1,0:T(8,128)(2,1)} %out_ref.1), custom_call_target="tpu_custom_call" | custom-call | bytes 1048576 | tf_op jit(solution)/shard_map/pallas_call | solution.py:290
  7.3 3.5 %collective-permute-start.2 = (bf16[304,1152]{1,0:T(8,128)(2,1)S(1)}, bf16[304,1152]{1,0:T(8,128)(2,1)S(1)}, u32[]{:S(2)}, u32[]{:S(2)}) collective-permute-start(bf16[304,1152]{1,0:T(8,128)(2,1)S(1)} %shard_map.102.packed_ref.refs_1_.refs_2_), channel_id=1, source_target_pairs={{0,2},{2,0},{1,3},{3,1},{4,6},{6,4},{5,7},{7,5},{8,10},{10,8},{9,1... | collective-permute-start | bytes 2101256 | tf_op jit(solution)/shard_map/ppermute | solution.py:352
  10.8 3.0 %collective-permute-start.3 = (bf16[304,1152]{1,0:T(8,128)(2,1)S(1)}, bf16[304,1152]{1,0:T(8,128)(2,1)S(1)}, u32[]{:S(2)}, u32[]{:S(2)}) collective-permute-start(bf16[304,1152]{1,0:T(8,128)(2,1)S(1)} %shard_map.102.packed_ref.refs_1_.refs_2_), channel_id=1, source_target_pairs={{0,259},{1,258},{258,1},{259,0},{2,257},{3,256},{256,3},{257,2},{4... | collective-permute-start | bytes 2101256 | tf_op jit(solution)/shard_map/ppermute | solution.py:353
  13.8 1.3 %shard_map.103 = bf16[880,1152]{1,0:T(8,128)(2,1)S(1)} custom-call(bf16[304,1152]{1,0:T(8,128)(2,1)S(1)} %shard_map.102.packed_ref.refs_1_.refs_2_, bf16[288,1152]{1,0:T(8,128)(2,1)} %bitcast.24, bf16[288,1152]{1,0:T(8,128)(2,1)} %refs_5_.1), custom_call_target="tpu_custom_call" | custom-call | bytes 1048576 | tf_op jit(solution)/shard_map/pallas_call | solution.py:290
  15.1 3.1 %collective-permute-start.1 = (bf16[880,1152]{1,0:T(8,128)(2,1)S(1)}, bf16[880,1152]{1,0:T(8,128)(2,1)S(1)}, u32[]{:S(2)}, u32[]{:S(2)}) collective-permute-start(bf16[880,1152]{1,0:T(8,128)(2,1)S(1)} %shard_map.103), channel_id=1, source_target_pairs={{0,1},{1,0},{2,3},{3,2},{4,5},{5,4},{6,7},{7,6},{8,9},{9,8},{10,11... | collective-permute-start | bytes 6082568 | tf_op jit(solution)/shard_map/ppermute | solution.py:363
  18.2 0.0 collective-permute-done.refs_0_.tok_ref
  18.3 0.2 shard_map.101
  18.5 12.9 %all_to_all.44 = bf16[4,48,1152]{2,1,0:T(8,128)(2,1)S(1)} all-to-all(bf16[4,48,1152]{2,1,0:T(8,128)(2,1)S(1)} %bitcast.23), channel_id=1, replica_groups=mesh['yhi'=2,'z'=16,'x'=4,'ylo'=2,'core'=2] {'x'}, dimensions={0} | all-to-all | bytes 884736 | tf_op jit(solution)/shard_map/all_to_all | solution.py:369
  31.3 0.0 collective-permute-done.2.refs_3_.refs_4_
  31.4 0.0 collective-permute-done.1.refs_2_.refs_3_
  31.4 1.3 %shard_map.104 = (bf16[3,192,216]{2,1,0:T(8,128)(2,1)S(1)}, bf16[576,1152]{1,0:T(8,128)(2,1)S(1)}) custom-call(bf16[192,1152]{1,0:T(8,128)(2,1)S(1)} %bitcast.14, bf16[304,1152]{1,0:T(8,128)(2,1)S(1)} %shard_map.102.packed_ref.refs_1_.refs_2_, bf16[880,1152]{1,0:T(8,128)(2,1)S(1)} %collective-permute-done.1.refs_2_.refs_3_, ...), custom_call_target="tpu_custom_call" | custom-call | bytes 1048576 | tf_op jit(solution)/shard_map/pallas_call | solution.py:290
  32.7 0.0 collective-permute-done.3.refs_5_
  32.7 2.2 %shard_map.105 = (bf16[192,288]{1,0:T(8,128)(2,1)}, bf16[96,1152]{1,0:T(8,128)(2,1)}, f32[8,128]{1,0:T(8,128)}, bf16[288,1152]{1,0:T(8,128)(2,1)}) custom-call(bf16[192,1152]{1,0:T(8,128)(2,1)S(1)} %bitcast.15, bf16[3,192,216]{2,1,0:T(8,128)(2,1)S(1)} %get-tuple-element.21.refs_1_, bf16[304,1152]{1,0:T(8,128)(2,1)S(1)} %shard_map.102.packed_ref.refs_1_.refs_2_, ...), custom_call_target="tpu_custom_call" | custom-call | bytes 1048576 | tf_op jit(solution)/shard_map/pallas_call | solution.py:290
  34.9 9.6 %collective-permute-start.4 = (bf16[96,1152]{1,0:T(8,128)(2,1)}, bf16[96,1152]{1,0:T(8,128)(2,1)}, u32[]{:S(2)}, u32[]{:S(2)}) collective-permute-start(bf16[96,1152]{1,0:T(8,128)(2,1)} %get-tuple-element.26.refs_3_), channel_id=1, source_target_pairs={{32,64},{48,80},{64,32},{80,48},{96,128},{112,144},{128,96},{144,1... | collective-permute-start | bytes 663560 | tf_op jit(solution)/shard_map/ppermute | solution.py:409
  44.5 1.9 %collective-permute-start.5 = (bf16[96,1152]{1,0:T(8,128)(2,1)}, bf16[96,1152]{1,0:T(8,128)(2,1)}, u32[]{:S(2)}, u32[]{:S(2)}) collective-permute-start(bf16[96,1152]{1,0:T(8,128)(2,1)} %get-tuple-element.26.refs_3_), channel_id=1, source_target_pairs={{16,32},{32,16},{48,64},{64,48},{80,96},{96,80},{112,128},{128,112... | collective-permute-start | bytes 663560 | tf_op jit(solution)/shard_map/ppermute | solution.py:409
  46.4 2.0 %collective-permute-start.6 = (bf16[96,1152]{1,0:T(8,128)(2,1)}, bf16[96,1152]{1,0:T(8,128)(2,1)}, u32[]{:S(2)}, u32[]{:S(2)}) collective-permute-start(bf16[96,1152]{1,0:T(8,128)(2,1)} %get-tuple-element.26.refs_3_), channel_id=1, source_target_pairs={{0,32},{16,48},{32,0},{48,16},{64,96},{80,112},{96,64},{112,80},{1... | collective-permute-start | bytes 663560 | tf_op jit(solution)/shard_map/ppermute | solution.py:409
  48.4 5.3 %collective-permute-start.7 = (bf16[96,1152]{1,0:T(8,128)(2,1)}, bf16[96,1152]{1,0:T(8,128)(2,1)}, u32[]{:S(2)}, u32[]{:S(2)}) collective-permute-start(bf16[96,1152]{1,0:T(8,128)(2,1)} %get-tuple-element.26.refs_3_), channel_id=1, source_target_pairs={{0,16},{16,0},{32,48},{48,32},{64,80},{80,64},{96,112},{112,96},{1... | collective-permute-start | bytes 663560 | tf_op jit(solution)/shard_map/ppermute | solution.py:409
  53.7 2.8 %collective-permute-start.9 = (bf16[576,1152]{1,0:T(8,128)(2,1)S(1)}, bf16[576,1152]{1,0:T(8,128)(2,1)S(1)}, u32[]{:S(2)}, u32[]{:S(2)}) collective-permute-start(bf16[576,1152]{1,0:T(8,128)(2,1)S(1)} %get-tuple-element.35.refs_1_), channel_id=1, source_target_pairs={{0,2},{2,0},{1,3},{3,1},{4,6},{6,4},{5,7},{7,5},{8,10},{10,8},{9,1... | collective-permute-start | bytes 3981320 | tf_op jit(solution)/shard_map/ppermute | solution.py:411
  56.5 0.0 collective-permute-done.4.refs_4_
  56.5 1.9 %collective-permute-start.8 = (bf16[576,1152]{1,0:T(8,128)(2,1)S(1)}, bf16[576,1152]{1,0:T(8,128)(2,1)S(1)}, u32[]{:S(2)}, u32[]{:S(2)}) collective-permute-start(bf16[576,1152]{1,0:T(8,128)(2,1)S(1)} %get-tuple-element.35.refs_1_), channel_id=1, source_target_pairs={{0,259},{1,258},{258,1},{259,0},{2,257},{3,256},{256,3},{257,2},{4... | collective-permute-start | bytes 3981320 | tf_op jit(solution)/shard_map/ppermute | solution.py:412
  58.4 1.1 %collective-permute-done.5.refs_5_ = bf16[96,1152]{1,0:T(8,128)(2,1)} collective-permute-done((bf16[96,1152]{1,0:T(8,128)(2,1)}, bf16[96,1152]{1,0:T(8,128)(2,1)}, u32[]{:S(2)}, u32[]{:S(2)}) %collective-permute-start.5) | collective-permute-done | bytes 221216 | tf_op jit(solution)/shard_map/ppermute | solution.py:409
  59.6 2.7 %shard_map.106 = (f32[8,128]{1,0:T(8,128)S(1)}, bf16[192,288]{1,0:T(8,128)(2,1)S(1)}, bf16[288,1152]{1,0:T(8,128)(2,1)S(1)}, f32[192,288]{1,0:T(8,128)S(1)}, f32...) custom-call(s32[1]{0:T(128)} %bitcast.refs_0_.slot_ref, f32[8,128]{1,0:T(8,128)} %get-tuple-element.22.refs_1_, ...), custom_call_target="tpu_custom_call" | custom-call | bytes 1048576 | tf_op jit(solution)/shard_map/pallas_call | solution.py:290
  62.3 0.0 collective-permute-done.6.refs_3_
  62.3 0.6 collective-permute-done.7.refs_4_
  62.9 1.9 %shard_map.107 = bf16[192,1152]{1,0:T(8,128)(2,1)S(1)} custom-call(s32[1]{0:T(128)} %bitcast.refs_0_.slot_ref, f32[8,128]{1,0:T(8,128)S(1)} %get-tuple-element.28.refs_1_, bf16[192,288]{1,0:T(8,128)(2,1)S(1)} %get-tuple-element.29.refs_2_, bf16[96,1152]{1,0:T(8,128)(2,1)} %collective-permute-done.6.refs_3_, bf16[96,1152]{1,0:T(8,128)(2,1)} %collective-permute-done.7.refs_4_, ...), custom_call_target="tpu_custom_call" | custom-call | flops 99999997952 | bytes 1048576 | tf_op jit(solution)/shard_map/pallas_call | solution.py:290
  64.9 12.6 %all_to_all.45 = bf16[4,48,1152]{2,1,0:T(8,128)(2,1)S(1)} all-to-all(bf16[4,48,1152]{2,1,0:T(8,128)(2,1)S(1)} %bitcast.21), channel_id=1, replica_groups=mesh['yhi'=2,'z'=16,'x'=4,'ylo'=2,'core'=2] {'x'}, dimensions={0} | all-to-all | bytes 884736 | tf_op jit(solution)/shard_map/all_to_all | solution.py:447
  77.5 0.3 shard_map.108
  77.8 10.0 %all_to_all.46 = bf16[4,48,1152]{2,1,0:T(8,128)(2,1)S(1)} all-to-all(bf16[4,48,1152]{2,1,0:T(8,128)(2,1)S(1)} %bitcast.22), channel_id=1, replica_groups=mesh['yhi'=2,'z'=16,'x'=4,'ylo'=2,'core'=2] {'x'}, dimensions={0} | all-to-all | bytes 884736 | tf_op jit(solution)/shard_map/all_to_all | solution.py:451
  87.8 0.0 collective-permute-done.9.refs_3_
  87.8 1.4 %shard_map.109.refs_2_ = f32[192,1152]{1,0:T(8,128)S(1)} custom-call(bf16[192,1152]{1,0:T(8,128)(2,1)S(1)} %bitcast.16, bf16[576,1152]{1,0:T(8,128)(2,1)S(1)} %get-tuple-element.35.refs_1_, bf16[880,1152]{1,0:T(8,128)(2,1)S(1)} %collective-permute-done.1.refs_2_.refs_3_, bf16[576,1152]{1,0:T(8,128)(2,1)S(1)} %collective-permute-done.9.refs_3_), custom_call_target="tpu_custom_call" | custom-call | bytes 1048576 | tf_op jit(solution)/shard_map/pallas_call | solution.py:290
  89.2 0.0 copy-start
  89.2 1.3 %collective-permute-done.8.refs_1_ = bf16[576,1152]{1,0:T(8,128)(2,1)S(1)} collective-permute-done((bf16[576,1152]{1,0:T(8,128)(2,1)S(1)}, bf16[576,1152]{1,0:T(8,128)(2,1)S(1)}, u32[]{:S(2)}, u32[]{:S(2)}) %collective-permute-start.8) | collective-permute-done | bytes 1327136 | tf_op jit(solution)/shard_map/ppermute | solution.py:412
  90.5 0.9 shard_map.110
  91.4 11.1 %all_to_all.47 = bf16[4,48,1152]{2,1,0:T(8,128)(2,1)S(1)} all-to-all(bf16[4,48,1152]{2,1,0:T(8,128)(2,1)S(1)} %bitcast.20), channel_id=1, replica_groups=mesh['yhi'=2,'z'=16,'x'=4,'ylo'=2,'core'=2] {'x'}, dimensions={0} | all-to-all | bytes 884736 | tf_op jit(solution)/shard_map/all_to_all | solution.py:464
  102.5 0.0 copy-done
  102.5 0.7 shard_map.111
Async XLA Ops:
  1.7 16.5 %collective-permute-start = (bf16[64,1152]{1,0:T(8,128)(2,1)S(1)}, bf16[64,1152]{1,0:T(8,128)(2,1)S(1)}, u32[]{:S(2)}, u32[]{:S(2)}) collective-permute-start(bf16[64,1152]{1,0:T(8,128)(2,1)S(1)} %shard_map.100), channel_id=1, source_target_pairs={{0,16},{16,32},{32,48},{48,64},{64,80},{80,96},{96,112},{112,128},... | collective-permute-start | bytes 442376 | tf_op jit(solution)/shard_map/ppermute | solution.py:336
  7.3 24.0 %collective-permute-start.2 = (bf16[304,1152]{1,0:T(8,128)(2,1)S(1)}, bf16[304,1152]{1,0:T(8,128)(2,1)S(1)}, u32[]{:S(2)}, u32[]{:S(2)}) collective-permute-start(bf16[304,1152]{1,0:T(8,128)(2,1)S(1)} %shard_map.102.packed_ref.refs_1_.refs_2_), channel_id=1, source_target_pairs={{0,2},{2,0},{1,3},{3,1},{4,6},{6,4},{5,7},{7,5},{8,10},{10,8},{9,1... | collective-permute-start | bytes 2101256 | tf_op jit(solution)/shard_map/ppermute | solution.py:352
  10.8 21.9 %collective-permute-start.3 = (bf16[304,1152]{1,0:T(8,128)(2,1)S(1)}, bf16[304,1152]{1,0:T(8,128)(2,1)S(1)}, u32[]{:S(2)}, u32[]{:S(2)}) collective-permute-start(bf16[304,1152]{1,0:T(8,128)(2,1)S(1)} %shard_map.102.packed_ref.refs_1_.refs_2_), channel_id=1, source_target_pairs={{0,259},{1,258},{258,1},{259,0},{2,257},{3,256},{256,3},{257,2},{4... | collective-permute-start | bytes 2101256 | tf_op jit(solution)/shard_map/ppermute | solution.py:353
  15.1 16.3 %collective-permute-start.1 = (bf16[880,1152]{1,0:T(8,128)(2,1)S(1)}, bf16[880,1152]{1,0:T(8,128)(2,1)S(1)}, u32[]{:S(2)}, u32[]{:S(2)}) collective-permute-start(bf16[880,1152]{1,0:T(8,128)(2,1)S(1)} %shard_map.103), channel_id=1, source_target_pairs={{0,1},{1,0},{2,3},{3,2},{4,5},{5,4},{6,7},{7,6},{8,9},{9,8},{10,11... | collective-permute-start | bytes 6082568 | tf_op jit(solution)/shard_map/ppermute | solution.py:363
  34.9 21.6 %collective-permute-start.4 = (bf16[96,1152]{1,0:T(8,128)(2,1)}, bf16[96,1152]{1,0:T(8,128)(2,1)}, u32[]{:S(2)}, u32[]{:S(2)}) collective-permute-start(bf16[96,1152]{1,0:T(8,128)(2,1)} %get-tuple-element.26.refs_3_), channel_id=1, source_target_pairs={{32,64},{48,80},{64,32},{80,48},{96,128},{112,144},{128,96},{144,1... | collective-permute-start | bytes 663560 | tf_op jit(solution)/shard_map/ppermute | solution.py:409
  44.5 15.1 %collective-permute-start.5 = (bf16[96,1152]{1,0:T(8,128)(2,1)}, bf16[96,1152]{1,0:T(8,128)(2,1)}, u32[]{:S(2)}, u32[]{:S(2)}) collective-permute-start(bf16[96,1152]{1,0:T(8,128)(2,1)} %get-tuple-element.26.refs_3_), channel_id=1, source_target_pairs={{16,32},{32,16},{48,64},{64,48},{80,96},{96,80},{112,128},{128,112... | collective-permute-start | bytes 663560 | tf_op jit(solution)/shard_map/ppermute | solution.py:409
  46.4 15.9 %collective-permute-start.6 = (bf16[96,1152]{1,0:T(8,128)(2,1)}, bf16[96,1152]{1,0:T(8,128)(2,1)}, u32[]{:S(2)}, u32[]{:S(2)}) collective-permute-start(bf16[96,1152]{1,0:T(8,128)(2,1)} %get-tuple-element.26.refs_3_), channel_id=1, source_target_pairs={{0,32},{16,48},{32,0},{48,16},{64,96},{80,112},{96,64},{112,80},{1... | collective-permute-start | bytes 663560 | tf_op jit(solution)/shard_map/ppermute | solution.py:409
  48.4 14.5 %collective-permute-start.7 = (bf16[96,1152]{1,0:T(8,128)(2,1)}, bf16[96,1152]{1,0:T(8,128)(2,1)}, u32[]{:S(2)}, u32[]{:S(2)}) collective-permute-start(bf16[96,1152]{1,0:T(8,128)(2,1)} %get-tuple-element.26.refs_3_), channel_id=1, source_target_pairs={{0,16},{16,0},{32,48},{48,32},{64,80},{80,64},{96,112},{112,96},{1... | collective-permute-start | bytes 663560 | tf_op jit(solution)/shard_map/ppermute | solution.py:409
  53.7 34.1 %collective-permute-start.9 = (bf16[576,1152]{1,0:T(8,128)(2,1)S(1)}, bf16[576,1152]{1,0:T(8,128)(2,1)S(1)}, u32[]{:S(2)}, u32[]{:S(2)}) collective-permute-start(bf16[576,1152]{1,0:T(8,128)(2,1)S(1)} %get-tuple-element.35.refs_1_), channel_id=1, source_target_pairs={{0,2},{2,0},{1,3},{3,1},{4,6},{6,4},{5,7},{7,5},{8,10},{10,8},{9,1... | collective-permute-start | bytes 3981320 | tf_op jit(solution)/shard_map/ppermute | solution.py:411
  56.5 34.0 %collective-permute-start.8 = (bf16[576,1152]{1,0:T(8,128)(2,1)S(1)}, bf16[576,1152]{1,0:T(8,128)(2,1)S(1)}, u32[]{:S(2)}, u32[]{:S(2)}) collective-permute-start(bf16[576,1152]{1,0:T(8,128)(2,1)S(1)} %get-tuple-element.35.refs_1_), channel_id=1, source_target_pairs={{0,259},{1,258},{258,1},{259,0},{2,257},{3,256},{256,3},{257,2},{4... | collective-permute-start | bytes 3981320 | tf_op jit(solution)/shard_map/ppermute | solution.py:412
  89.2 13.3 %copy-start = (bf16[48,1152]{1,0:T(8,128)(2,1)S(1)}, bf16[48,1152]{1,0:T(8,128)(2,1)}, u32[]{:S(2)}) copy-start(bf16[48,1152]{1,0:T(8,128)(2,1)} %fresh_ref.1) | copy-start | bytes 331780

commit v5 on v4

--- a/solution.py
+++ b/solution.py
@@ -27,12 +27,12 @@
     return copies
 
 
-def payload_kernel(levels_ref, latents_ref, mods_ref, tok_ref, latents_here, mods_here, sems):
+def payload_kernel(levels_ref, latents_ref, mods_ref, tok_ref, mods_here, sems):
     tokens, width = latents_ref.shape
     level = levels_ref[0]
     group = pl.multiple_of(level // 8 * 8, 8)
     copies = start_all(
-        [(mods_ref.at[:, pl.ds(group, 8), :], mods_here), (latents_ref, latents_here)], sems
+        [(mods_ref.at[:, pl.ds(group, 8), :], mods_here), (latents_ref, tok_ref.at[0:tokens])], sems
     )
     copies[0].wait()
     chosen = lax.broadcasted_iota(jnp.int32, (8, width), 0) == level - group
@@ -44,25 +44,25 @@
     high = whole.astype(BF16).astype(F32)
     tok_ref[tokens:, :] = jnp.concatenate([high, whole - high], axis=0).astype(BF16)
     copies[1].wait()
-    tok_ref[0:tokens, :] = latents_here[...]
 
 
 def weight_kernel(
     map_ref, window_ref, qkv_ref, out_ref, packed_ref, window_here, qkv_here, out_here, sems
 ):
-    lines, width = qkv_ref.shape
+    width = qkv_ref.shape[1]
     rows = out_ref.shape[0]
     copies = start_all(
         [(window_ref, window_here), (qkv_ref, qkv_here), (out_ref, out_here)], sems
     )
-    packed_ref[lines + 8 + rows :, :] = jnp.zeros((8, width), BF16)
     copies[0].wait()
-    half = jnp.full((8, width), window_here[map_ref[0]].astype(F32))
-    packed_ref[lines : lines + 8, :] = half.astype(BF16)
+    heads = lax.broadcasted_iota(jnp.int32, window_here.shape, 1)
+    half = jnp.where(heads == map_ref[...], window_here[...].astype(F32), 0.0)
+    half = jnp.broadcast_to(jnp.sum(half, axis=1, keepdims=True), (8, width))
+    packed_ref[rows : rows + 8, :] = half.astype(BF16)
     copies[1].wait()
-    packed_ref[0:lines, :] = qkv_here[...]
+    packed_ref[rows + 8 :, :] = qkv_here[...]
     copies[2].wait()
-    packed_ref[lines + 8 : lines + 8 + rows, :] = out_here[...]
+    packed_ref[0:rows, :] = out_here[...]
 
 
 def join_mlp(fc1_ref, fc2_ref, to_ref, start, sems):
@@ -76,14 +76,6 @@
     )
 
 
-def whole_kernel(packed_ref, fc1_ref, fc2_ref, whole_ref, sems):
-    start = packed_ref.shape[0]
-    copies = join_mlp(fc1_ref, fc2_ref, whole_ref, start, sems)
-    whole_ref[0:start, :] = packed_ref[...]
-    for copy in copies:
-        copy.wait()
-
-
 def mod_of(tok_ref, tokens):
     terms = tok_ref[tokens:, :].astype(F32)
     return terms[0:8] + terms[8:16]
@@ -102,37 +94,43 @@
 
 def project(head, normed, weight):
     return lax.dot_general(
-        normed, weight[0 : 3 * head, :], (((1,), (1,)), ((), ())), preferred_element_type=F32
-    )
-
-
-def some_qkv_kernel(head, tok_ref, w0, w1, w2, fc1_ref, fc2_ref, part_ref, mlp_ref, sems):
+        normed, weight[head + 8 :, :], (((1,), (1,)), ((), ())), preferred_element_type=F32
+    )
+
+
+def some_qkv_kernel(
+    head, moved_ref, tok_ref, w0, w1, w2, fc1_ref, fc2_ref, part_ref, mlp_ref, kept_ref, outs_ref, sems
+):
+    count = head + 8
+    weights = (w0, w1, w2)
     copies = join_mlp(fc1_ref, fc2_ref, mlp_ref, 0, sems)
-    for slot, weight in enumerate((w0, w1, w2)):
+    copies += start_all(
+        [(ref.at[0:count], outs_ref.at[i]) for i, ref in enumerate(weights)]
+        + [(moved_ref, kept_ref)],
+        sems.at[2:6],
+    )
+    for slot, weight in enumerate(weights):
         part_ref[slot, :, :] = project(head, tok_ref[...], weight).astype(BF16)
     for copy in copies:
         copy.wait()
 
 
 def last_qkv_kernel(
-    head, tok_ref, part_ref, w0, w1, w2, w3, q_ref, kv_ref, half_ref, outs_ref,
-    q_here, half_here, outs_here, sems,
-):
-    first = 3 * head + 8
+    head, tok_ref, part_ref, w0, w1, w2, w3, q_ref, kv_ref, half_ref, last_ref, q_here, half_here, sems
+):
     weights = (w0, w1, w2, w3)
-    outs = [ref[first : first + head, :].astype(F32) for ref in weights]
-    outs_here[...] = jnp.concatenate(outs, axis=0).astype(BF16)
-    copies = start_all([(outs_here, outs_ref)], sems)
+    copies = start_all([(w3.at[0 : head + 8], last_ref)], sems)
     parts = [part_ref[slot].astype(F32) for slot in range(3)] + [project(head, tok_ref[...], w3)]
     query = jnp.concatenate([part[:, :head] for part in parts], axis=1)
     q_here[...] = query.astype(BF16)
+    copies += start_all([(q_here, q_ref)], sems.at[1:2])
     lane = lax.broadcasted_iota(jnp.int32, half_here.shape, 1)
     half = jnp.zeros(half_here.shape, F32)
     for slot, weight in enumerate(weights):
-        mark = weight[3 * head - 8 : 3 * head + 8, 0:128].astype(F32)[8:16]
+        mark = weight[head - 8 : head + 8, 0:128].astype(F32)[8:16]
         half = jnp.where(lane == slot, mark, half)
     half_here[...] = half
-    copies += start_all([(half_here, half_ref), (q_here, q_ref)], sems.at[1:3])
+    copies += start_all([(half_here, half_ref)], sems.at[2:3])
     keys = [part[:, head : 2 * head] for part in parts]
     keyval = jnp.concatenate(keys + [part[:, 2 * head :] for part in parts], axis=1)
     middle = keyval.shape[0] // 2
@@ -151,10 +149,10 @@
     return gather, spread
 
 
-def masked_scores(head, slots, place, half, query, gather, refs, offsets, reaches):
+def masked_scores(head, slots, place, half, query, gather, keys, offsets, reaches):
     rows, cols = query.shape
     frame = lax.rem(place + slots - 1, slots)
-    products = [(query * unpack(ref, cols, 0)).astype(BF16) for ref in refs]
+    products = [(query * key).astype(BF16) for key in keys]
     scores = jnp.dot(jnp.concatenate(products, axis=0), gather, preferred_element_type=F32)
     masked, valids = [], []
     for index, (offset, reach) in enumerate(zip(offsets, reaches)):
@@ -176,18 +174,27 @@
 
 
 def early_kernel(
-    head, slots, slot_ref, half_ref, q_ref, k0, k1, k2, outs_ref,
+    head, slots, slot_ref, half_ref, q_ref, k0, k1, k2, outs_ref, last_ref,
     half_here, q_here, outs_here, mixed_ref, top_ref, total_ref, sems,
 ):
     rows, cols = q_ref.shape
-    copies = start_all([(half_ref, half_here), (q_ref, q_here), (outs_ref, outs_here)], sems)
+    copies = start_all(
+        [
+            (half_ref, half_here),
+            (q_ref, q_here),
+            (outs_ref, outs_here.at[0:3]),
+            (last_ref, outs_here.at[3]),
+        ],
+        sems,
+    )
     gather, spread = indicators(head, cols)
     place = slot_ref[0]
+    refs = (k0, k1, k2)
+    keys = [unpack(ref, cols, 0) for ref in refs]
     copies[0].wait()
     copies[1].wait()
-    refs = (k0, k1, k2)
     masked, valids = masked_scores(
-        head, slots, place, half_here[0:1, :], q_here[...].astype(F32), gather, refs,
+        head, slots, place, half_here[0:1, :], q_here[...].astype(F32), gather, keys,
         (0, 2 * (place & 2) - 2, 2 * (place & 1) - 1), (0, 2, 1),
     )
     top = jnp.maximum(jnp.maximum(masked[0], masked[1]), masked[2])
@@ -202,6 +209,7 @@
         mixed = mixed + wide[index * rows : (index + 1) * rows] * unpack(ref, cols, cols)
     mixed_ref[...] = mixed
     copies[2].wait()
+    copies[3].wait()
 
 
 def late_kernel(
@@ -212,7 +220,8 @@
     place = slot_ref[0]
     refs = (k3, k4)
     masked, valids = masked_scores(
-        head, slots, place, half_here[0:1, :], q_here[...].astype(F32), gather, refs,
+        head, slots, place, half_here[0:1, :], q_here[...].astype(F32), gather,
+        [unpack(ref, cols, 0) for ref in refs],
         (2 - 2 * (place & 2), 1 - 2 * (place & 1)), (2, 1),
     )
     before = top_ref[...]
@@ -225,9 +234,9 @@
     mixed = wide[:rows] * mixed_ref[...]
     for index, ref in enumerate(refs):
         mixed = mixed + wide[(index + 1) * rows : (index + 2) * rows] * unpack(ref, cols, cols)
-    out_ref[...] = jnp.dot(
-        mixed.astype(BF16), outs_here[...], preferred_element_type=F32
-    ).astype(BF16)
+    outs = [outs_here[slot].astype(F32)[0:head] for slot in range(4)]
+    outs = jnp.concatenate(outs, axis=0).astype(BF16)
+    out_ref[...] = jnp.dot(mixed.astype(BF16), outs, preferred_element_type=F32).astype(BF16)
 
 
 def total_of(parts_ref, tokens):
@@ -246,24 +255,23 @@
     fill(normed_ref, normalise(resid.astype(F32), mod[3:4, :], mod[4:5, :]))
 
 
-def mlp_of(hidden, normed, refs):
-    first = jnp.concatenate([ref[ref.shape[0] - hidden :, :] for ref in refs], axis=0)
+def mlp_of(normed, ins, outs):
     wide = lax.dot_general(
-        normed, first, (((1,), (1,)), ((), ())), preferred_element_type=F32
+        normed, jnp.concatenate(ins, axis=0), (((1,), (1,)), ((), ())), preferred_element_type=F32
     )
     active = jax.nn.gelu(wide, approximate=True).astype(BF16)
-    second = jnp.concatenate(
-        [ref[ref.shape[0] - 2 * hidden : ref.shape[0] - hidden, :] for ref in refs], axis=0
-    )
-    return jnp.dot(active, second, preferred_element_type=F32)
+    return jnp.dot(active, jnp.concatenate(outs, axis=0), preferred_element_type=F32)
 
 
 def some_mlp_kernel(hidden, normed_ref, m0, m1, m2, sum_ref):
-    sum_ref[...] = mlp_of(hidden, normed_ref[...], (m0, m1, m2))
+    refs = (m0, m1, m2)
+    ins, outs = [ref[hidden:, :] for ref in refs], [ref[0:hidden, :] for ref in refs]
+    sum_ref[...] = mlp_of(normed_ref[...], ins, outs)
 
 
 def last_mlp_kernel(hidden, normed_ref, m3, sum_ref, part_ref):
-    part_ref[...] = (sum_ref[...] + mlp_of(hidden, normed_ref[...], (m3,))).astype(BF16)
+    last = mlp_of(normed_ref[...], [m3[hidden:, :]], [m3[0:hidden, :]])
+    part_ref[...] = (sum_ref[...] + last).astype(BF16)
 
 
 def final_kernel(slot_ref, parts_ref, resid_ref, tok_ref, fresh_ref, out_ref):
@@ -328,7 +336,6 @@
         latents[0],
         modulation.transpose(1, 0, 2),
         scratch=[
-            pltpu.VMEM((tokens, width), BF16),
             pltpu.VMEM((modulation.shape[1], 8, width), F32),
             pltpu.SemaphoreType.DMA((2,)),
         ],
@@ -336,56 +343,53 @@
     moved = lax.ppermute(payload, SLOTS, [(s, (s + 1) % slots) for s in range(slots)])
     own_w = call(
         weight_kernel,
-        shape(4 * head + 16, width),
-        "saaa>v",
-        head_map,
-        window,
+        shape(4 * head + 8, width),
+        "vaaa>v",
+        head_map.reshape(1, 1),
+        window.reshape(1, -1),
         qkv_weight.T,
         out_weight,
         scratch=[
-            pltpu.SMEM(window.shape, jnp.int32),
+            pltpu.VMEM((1, window.shape[0]), jnp.int32),
             pltpu.VMEM((3 * head, width), BF16),
             pltpu.VMEM((head, width), BF16),
             pltpu.SemaphoreType.DMA((3,)),
         ],
     )
+    core_w = lax.ppermute(lax.optimization_barrier((own_w, moved))[0], "core", SWAP)
     near_w = lax.ppermute(own_w, "ylo", SWAP)
     far_w = lax.ppermute(own_w, ("yhi", "ylo", "core"), FAR)
-    whole = call(
-        whole_kernel,
-        shape(4 * head + 16 + 2 * hidden, width),
-        "vaa>v",
-        own_w,
-        fc1_weight.T,
-        fc2_weight,
-        scratch=[pltpu.SemaphoreType.DMA((2,))],
-    )
-    core_w = lax.ppermute(whole, "core", SWAP)
     rows = around * tokens
     cols = 4 * head
     normed = call(
         lambda *refs: norm_kernel(tokens, *refs), shape(rows, width), "v>v", moved, flops=100 * 10**9
     )
     tok = lax.all_to_all(normed, "x", 0, 0, tiled=True)
-    part, own_m = call(
+    part, own_m, kept, outs = call(
         lambda *refs: some_qkv_kernel(head, *refs),
-        (shape(3, rows, 3 * head), shape(2 * hidden, width)),
-        "vvvvaa>vv",
+        (
+            shape(3, rows, 3 * head),
+            shape(2 * hidden, width),
+            pltpu.HBM(moved.shape, BF16),
+            pltpu.HBM((3, head + 8, width), BF16),
+        ),
+        "vvvvvaa>vvaa",
+        moved,
         tok,
         own_w,
         core_w,
         near_w,
         fc1_weight.T,
         fc2_weight,
-        scratch=[pltpu.SemaphoreType.DMA((2,))],
-    )
-    query, keyval, halfs, outs = call(
+        scratch=[pltpu.SemaphoreType.DMA((6,))],
+    )
+    query, keyval, halfs, last_out = call(
         lambda *refs: last_qkv_kernel(head, *refs),
         (
             pltpu.HBM((rows, cols), BF16),
             shape(rows // 2, 4 * cols),
             pltpu.HBM((8, 128), F32),
-            pltpu.HBM((cols, width), BF16),
+            pltpu.HBM((head + 8, width), BF16),
         ),
         "vvvvvv>avaa",
         tok,
@@ -397,7 +401,6 @@
         scratch=[
             pltpu.VMEM((rows, cols), BF16),
             pltpu.VMEM((8, 128), F32),
-            pltpu.VMEM((cols, width), BF16),
             pltpu.SemaphoreType.DMA((3,)),
         ],
     )
@@ -416,20 +419,22 @@
         (
             shape(8, 128, dtype=F32),
             shape(rows, cols),
-            shape(cols, width),
+            shape(4, head + 8, width),
             shape(rows, cols, dtype=F32),
             shape(rows, 128, dtype=F32),
             shape(rows, 128, dtype=F32),
         ),
-        "saavvva>vvvvvv",
+        "saavvvaa>vvvvvv",
         place,
         halfs,
         query,
         keyval,
         *arrived[:2],
         outs,
-        scratch=[pltpu.SemaphoreType.DMA((3,))],
-    )
+        last_out,
+        scratch=[pltpu.SemaphoreType.DMA((4,))],
+    )
+    core_m = lax.ppermute(lax.optimization_barrier((own_m, mixed))[0], "core", SWAP)
     attended = call(
         lambda *refs: late_kernel(head, slots, *refs),
         shape(rows, width),
@@ -446,7 +451,7 @@
     )
     parts = lax.all_to_all(attended, "x", 0, 0, tiled=True)
     resid, normed = call(
-        resid_kernel, (shape(tokens, width), shape(rows, width)), "vv>vv", parts, moved
+        resid_kernel, (shape(tokens, width), shape(rows, width)), "vv>vv", parts, kept
     )
     normed = lax.all_to_all(normed, "x", 0, 0, tiled=True)
     some = call(
@@ -455,7 +460,7 @@
         "vvvv>v",
         normed,
         own_m,
-        core_w,
+        core_m,
         near_m,
     )
     part = call(
@@ -469,7 +474,7 @@
         slot[None].astype(jnp.int32),
         parts,
         resid,
-        moved,
+        kept,
         fresh_noise,
     )[None]
 

time: 104 us -> 102 us (0.981)
  Pallas kernels: 15.2 us -> 11 us
  starting transfers between devices: 36.9 us -> 40.5 us
  waiting for transfers between devices: 3.03 us -> 1.55 us
    pallas_call x12 -> x11, Pallas kernels: 15.2 us -> 11 us  [call(): pl.pallas_call(kernel, out_shape=outs, in_specs=ins, out_specs=tuple(back...]
    ppermute x1 -> x2, starting transfers between devices: 3.14 us -> 6.13 us  [the longest x1 3.14 us: per_device(): lax.ppermute(lax.optimization_barrier((own_w, moved))[0], 'core', SWAP)]
    ppermute x4, waiting for transfers between devices: 1.73 us -> 0.55 us  [per_device(): lax.ppermute(keyval, SLOTS, pairs)]
  transfers between devices with their start and end apart: 10 -> 11, of which waited for: 3 -> 2; matrix products, arithmetic and copies ran while one was open for 0% -> 0% of each run, Pallas kernels for 10% -> 7%
where the time goes in v5:
time: 102 us
  blocking collectives  47.1 us (46%)
  starting transfers between devices  40.5 us (40%)
  Pallas kernels  11 us (11%)
  waiting for transfers between devices  1.55 us (2%)
  between operations  1.52 us (1%)
    ppermute x4, starting transfers between devices, per_device(): lax.ppermute(keyval, SLOTS, pairs)  18.9 us
    all_to_all x1, blocking collectives, per_device(): tok = lax.all_to_all(normed, 'x', 0, 0, tiled=True)  12.9 us
    all_to_all x1, blocking collectives, per_device(): parts = lax.all_to_all(attended, 'x', 0, 0, tiled=True)  12.4 us
    all_to_all x1, blocking collectives, per_device(): parts = lax.all_to_all(part, 'x', 0, 0, tiled=True)  11.5 us
    pallas_call x11, Pallas kernels, call(): pl.pallas_call(kernel, out_shape=outs, in_specs=ins, out_specs=tuple(back...  11 us
    all_to_all x1, blocking collectives, per_device(): normed = lax.all_to_all(normed, 'x', 0, 0, tiled=True)  10.3 us
    ppermute x1, starting transfers between devices, per_device(): lax.ppermute(payload, SLOTS, [(s, (s + 1) % slots) for s in range(slots)])  3.83 us
    ppermute x1, starting transfers between devices, per_device(): near_w = lax.ppermute(own_w, 'ylo', SWAP)  3.48 us
  transfers between devices with their start and end apart: 11, of which 2 were waited for; matrix products, arithmetic and copies ran while one was open for 0% of the time, Pallas kernels for 7%

profile of v5, /device:TPU:32, one launch (start us, length us, event | category | flops | bytes accessed | tf_op | source)
XLA Modules:
  0.0 101.7 jit_solution(481494041032061132)
XLA Ops:
  0.7 1.0 %shard_map.100 = bf16[64,1152]{1,0:T(8,128)(2,1)S(1)} custom-call(s32[1]{0:T(128)S(6)} %copy.11.levels_ref, bf16[48,1152]{1,0:T(8,128)(2,1)} %bitcast.30, f32[6,32,1152]{2,1,0:T(8,128)} %bitcast.27), custom_call_target="tpu_custom_call" | custom-call | bytes 1048576 | tf_op jit(solution)/shard_map/pallas_call | solution.py:298
  1.7 3.8 %collective-permute-start = (bf16[64,1152]{1,0:T(8,128)(2,1)S(1)}, bf16[64,1152]{1,0:T(8,128)(2,1)S(1)}, u32[]{:S(2)}, u32[]{:S(2)}) collective-permute-start(bf16[64,1152]{1,0:T(8,128)(2,1)S(1)} %shard_map.100), channel_id=1, source_target_pairs={{0,16},{16,32},{32,48},{48,64},{64,80},{80,96},{96,112},{112,128},... | collective-permute-start | bytes 442376 | tf_op jit(solution)/shard_map/ppermute | solution.py:343
  6.2 1.1 %shard_map.102.refs_2_ = bf16[296,1152]{1,0:T(8,128)(2,1)S(1)} custom-call(s32[1,1]{1,0:T(1,128)} %bitcast.16.map_ref, s32[1,16]{1,0:T(1,128)} %bitcast.31, bf16[216,1152]{1,0:T(8,128)(2,1)} %bitcast.29, bf16[72,1152]{1,0:T(8,128)(2,1)} %out_ref.1), custom_call_target="tpu_custom_call" | custom-call | bytes 1048576 | tf_op jit(solution)/shard_map/pallas_call | solution.py:298
  7.3 3.5 %collective-permute-start.2 = (bf16[296,1152]{1,0:T(8,128)(2,1)S(1)}, bf16[296,1152]{1,0:T(8,128)(2,1)S(1)}, u32[]{:S(2)}, u32[]{:S(2)}) collective-permute-start(bf16[296,1152]{1,0:T(8,128)(2,1)S(1)} %shard_map.102.refs_2_), channel_id=1, source_target_pairs={{0,2},{2,0},{1,3},{3,1},{4,6},{6,4},{5,7},{7,5},{8,10},{10,8},{9,1... | collective-permute-start | bytes 2045960 | tf_op jit(solution)/shard_map/ppermute | solution.py:360
  10.8 3.0 %collective-permute-start.3 = (bf16[296,1152]{1,0:T(8,128)(2,1)S(1)}, bf16[296,1152]{1,0:T(8,128)(2,1)S(1)}, u32[]{:S(2)}, u32[]{:S(2)}) collective-permute-start(bf16[296,1152]{1,0:T(8,128)(2,1)S(1)} %shard_map.102.refs_2_), channel_id=1, source_target_pairs={{0,259},{1,258},{258,1},{259,0},{2,257},{3,256},{256,3},{257,2},{4... | collective-permute-start | bytes 2045960 | tf_op jit(solution)/shard_map/ppermute | solution.py:361
  13.8 0.0 collective-permute-done.refs_0_
  13.8 3.1 %collective-permute-start.1 = (bf16[296,1152]{1,0:T(8,128)(2,1)S(1)}, bf16[296,1152]{1,0:T(8,128)(2,1)S(1)}, u32[]{:S(2)}, u32[]{:S(2)}) collective-permute-start(bf16[296,1152]{1,0:T(8,128)(2,1)S(1)} %shard_map.102.refs_2_), channel_id=1, source_target_pairs={{0,1},{1,0},{2,3},{3,2},{4,5},{5,4},{6,7},{7,6},{8,9},{9,8},{10,11... | collective-permute-start | bytes 2045960 | tf_op jit(solution)/shard_map/ppermute | solution.py:359
  16.9 0.2 shard_map.101
  17.2 12.9 %all_to_all.44 = bf16[4,48,1152]{2,1,0:T(8,128)(2,1)S(1)} all-to-all(bf16[4,48,1152]{2,1,0:T(8,128)(2,1)S(1)} %bitcast.26), channel_id=1, replica_groups=mesh['yhi'=2,'z'=16,'x'=4,'ylo'=2,'core'=2] {'x'}, dimensions={0} | all-to-all | bytes 884736 | tf_op jit(solution)/shard_map/all_to_all | solution.py:367
  30.0 0.0 collective-permute-done.2.refs_4_
  30.0 0.0 collective-permute-done.1.refs_3_
  30.0 1.6 %shard_map.103 = (bf16[3,192,216]{2,1,0:T(8,128)(2,1)S(1)}, bf16[576,1152]{1,0:T(8,128)(2,1)S(1)}, bf16[64,1152]{1,0:T(8,128)(2,1)}, bf16[3,80,1152]{2,1,0:T(8,128)(2,1)}) custom-call(bf16[64,1152]{1,0:T(8,128)(2,1)S(1)} %collective-permute-done.refs_0_, bf16[192,1152]{1,0:T(8,128)(2,1)S(1)} %bitcast.17, bf16[296,1152]{1,0:T(8,128)(2,1)S(1)} %shard_map.102.refs_2_, ...), custom_call_target="tpu_custom_call" | custom-call | bytes 1048576 | tf_op jit(solution)/shard_map/pallas_call | solution.py:298
  31.7 0.0 collective-permute-done.3.refs_5_
  31.7 1.2 %shard_map.104 = (bf16[192,288]{1,0:T(8,128)(2,1)}, bf16[96,1152]{1,0:T(8,128)(2,1)S(1)}, f32[8,128]{1,0:T(8,128)}, bf16[80,1152]{1,0:T(8,128)(2,1)}) custom-call(bf16[192,1152]{1,0:T(8,128)(2,1)S(1)} %bitcast.18, bf16[3,192,216]{2,1,0:T(8,128)(2,1)S(1)} %get-tuple-element.26.refs_1_, bf16[296,1152]{1,0:T(8,128)(2,1)S(1)} %shard_map.102.refs_2_, ...), custom_call_target="tpu_custom_call" | custom-call | bytes 1048576 | tf_op jit(solution)/shard_map/pallas_call | solution.py:298
  32.9 9.7 %collective-permute-start.4 = (bf16[96,1152]{1,0:T(8,128)(2,1)S(1)}, bf16[96,1152]{1,0:T(8,128)(2,1)S(1)}, u32[]{:S(2)}, u32[]{:S(2)}) collective-permute-start(bf16[96,1152]{1,0:T(8,128)(2,1)S(1)} %get-tuple-element.31.refs_3_), channel_id=1, source_target_pairs={{32,64},{48,80},{64,32},{80,48},{96,128},{112,144},{128,96},{144,1... | collective-permute-start | bytes 663560 | tf_op jit(solution)/shard_map/ppermute | solution.py:412
  42.6 1.9 %collective-permute-start.5 = (bf16[96,1152]{1,0:T(8,128)(2,1)S(1)}, bf16[96,1152]{1,0:T(8,128)(2,1)S(1)}, u32[]{:S(2)}, u32[]{:S(2)}) collective-permute-start(bf16[96,1152]{1,0:T(8,128)(2,1)S(1)} %get-tuple-element.31.refs_3_), channel_id=1, source_target_pairs={{16,32},{32,16},{48,64},{64,48},{80,96},{96,80},{112,128},{128,112... | collective-permute-start | bytes 663560 | tf_op jit(solution)/shard_map/ppermute | solution.py:412
  44.5 1.9 %collective-permute-start.6 = (bf16[96,1152]{1,0:T(8,128)(2,1)S(1)}, bf16[96,1152]{1,0:T(8,128)(2,1)S(1)}, u32[]{:S(2)}, u32[]{:S(2)}) collective-permute-start(bf16[96,1152]{1,0:T(8,128)(2,1)S(1)} %get-tuple-element.31.refs_3_), channel_id=1, source_target_pairs={{0,32},{16,48},{32,0},{48,16},{64,96},{80,112},{96,64},{112,80},{1... | collective-permute-start | bytes 663560 | tf_op jit(solution)/shard_map/ppermute | solution.py:412
  46.5 5.4 %collective-permute-start.7 = (bf16[96,1152]{1,0:T(8,128)(2,1)S(1)}, bf16[96,1152]{1,0:T(8,128)(2,1)S(1)}, u32[]{:S(2)}, u32[]{:S(2)}) collective-permute-start(bf16[96,1152]{1,0:T(8,128)(2,1)S(1)} %get-tuple-element.31.refs_3_), channel_id=1, source_target_pairs={{0,16},{16,0},{32,48},{48,32},{64,80},{80,64},{96,112},{112,96},{1... | collective-permute-start | bytes 663560 | tf_op jit(solution)/shard_map/ppermute | solution.py:412
  51.8 3.3 %collective-permute-start.10 = (bf16[576,1152]{1,0:T(8,128)(2,1)S(1)}, bf16[576,1152]{1,0:T(8,128)(2,1)S(1)}, u32[]{:S(2)}, u32[]{:S(2)}) collective-permute-start(bf16[576,1152]{1,0:T(8,128)(2,1)S(1)} %get-tuple-element.43.refs_1_), channel_id=1, source_target_pairs={{0,2},{2,0},{1,3},{3,1},{4,6},{6,4},{5,7},{7,5},{8,10},{10,8},{9,1... | collective-permute-start | bytes 3981320 | tf_op jit(solution)/shard_map/ppermute | solution.py:414
  55.1 0.0 collective-permute-done.4.refs_4_
  55.1 1.9 %collective-permute-start.8 = (bf16[576,1152]{1,0:T(8,128)(2,1)S(1)}, bf16[576,1152]{1,0:T(8,128)(2,1)S(1)}, u32[]{:S(2)}, u32[]{:S(2)}) collective-permute-start(bf16[576,1152]{1,0:T(8,128)(2,1)S(1)} %get-tuple-element.43.refs_1_), channel_id=1, source_target_pairs={{0,259},{1,258},{258,1},{259,0},{2,257},{3,256},{256,3},{257,2},{4... | collective-permute-start | bytes 3981320 | tf_op jit(solution)/shard_map/ppermute | solution.py:415
  57.0 0.5 collective-permute-done.5.refs_5_
  57.6 1.6 %shard_map.105 = (f32[8,128]{1,0:T(8,128)S(1)}, bf16[192,288]{1,0:T(8,128)(2,1)S(1)}, bf16[4,80,1152]{2,1,0:T(8,128)(2,1)S(1)}, f32[192,288]{1,0:T(8,128)S(1)}, ...) custom-call(s32[1]{0:T(128)} %bitcast.refs_0_.slot_ref, f32[8,128]{1,0:T(8,128)} %get-tuple-element.27.refs_1_, ...), custom_call_target="tpu_custom_call" | custom-call | bytes 1048576 | tf_op jit(solution)/shard_map/pallas_call | solution.py:298
  59.2 3.0 %collective-permute-start.9 = (bf16[576,1152]{1,0:T(8,128)(2,1)S(1)}, bf16[576,1152]{1,0:T(8,128)(2,1)S(1)}, u32[]{:S(2)}, u32[]{:S(2)}) collective-permute-start(bf16[576,1152]{1,0:T(8,128)(2,1)S(1)} %get-tuple-element.43.refs_1_), channel_id=1, source_target_pairs={{0,1},{1,0},{2,3},{3,2},{4,5},{5,4},{6,7},{7,6},{8,9},{9,8},{10,11... | collective-permute-start | bytes 3981320 | tf_op jit(solution)/shard_map/ppermute | solution.py:437
  62.1 0.0 collective-permute-done.6.refs_3_
  62.2 0.0 collective-permute-done.7.refs_4_
  62.2 0.0 copy-start
  62.2 0.9 shard_map.106
  63.1 12.4 %all_to_all.45 = bf16[4,48,1152]{2,1,0:T(8,128)(2,1)S(1)} all-to-all(bf16[4,48,1152]{2,1,0:T(8,128)(2,1)S(1)} %bitcast.24), channel_id=1, replica_groups=mesh['yhi'=2,'z'=16,'x'=4,'ylo'=2,'core'=2] {'x'}, dimensions={0} | all-to-all | bytes 884736 | tf_op jit(solution)/shard_map/all_to_all | solution.py:452
  75.5 0.0 copy-done
  75.5 0.3 shard_map.107
  75.8 10.3 %all_to_all.46 = bf16[4,48,1152]{2,1,0:T(8,128)(2,1)S(1)} all-to-all(bf16[4,48,1152]{2,1,0:T(8,128)(2,1)S(1)} %bitcast.25), channel_id=1, replica_groups=mesh['yhi'=2,'z'=16,'x'=4,'ylo'=2,'core'=2] {'x'}, dimensions={0} | all-to-all | bytes 884736 | tf_op jit(solution)/shard_map/all_to_all | solution.py:456
  86.1 0.0 collective-permute-done.10.refs_3_
  86.1 0.0 collective-permute-done.9.refs_2_
  86.1 1.4 %shard_map.108.refs_2_ = f32[192,1152]{1,0:T(8,128)S(1)} custom-call(bf16[192,1152]{1,0:T(8,128)(2,1)S(1)} %bitcast.19, bf16[576,1152]{1,0:T(8,128)(2,1)S(1)} %get-tuple-element.43.refs_1_, bf16[576,1152]{1,0:T(8,128)(2,1)S(1)} %collective-permute-done.9.refs_2_, bf16[576,1152]{1,0:T(8,128)(2,1)S(1)} %collective-permute-done.10.refs_3_), custom_call_target="tpu_custom_call" | custom-call | bytes 1048576 | tf_op jit(solution)/shard_map/pallas_call | solution.py:298
  87.5 0.0 copy-start.1
  87.5 1.0 collective-permute-done.8.refs_1_
  88.5 0.9 shard_map.109
  89.4 11.5 %all_to_all.47 = bf16[4,48,1152]{2,1,0:T(8,128)(2,1)S(1)} all-to-all(bf16[4,48,1152]{2,1,0:T(8,128)(2,1)S(1)} %bitcast.23), channel_id=1, replica_groups=mesh['yhi'=2,'z'=16,'x'=4,'ylo'=2,'core'=2] {'x'}, dimensions={0} | all-to-all | bytes 884736 | tf_op jit(solution)/shard_map/all_to_all | solution.py:469
  100.9 0.0 copy-done.1
  101.0 0.7 shard_map.110
Async XLA Ops:
  1.7 12.1 %collective-permute-start = (bf16[64,1152]{1,0:T(8,128)(2,1)S(1)}, bf16[64,1152]{1,0:T(8,128)(2,1)S(1)}, u32[]{:S(2)}, u32[]{:S(2)}) collective-permute-start(bf16[64,1152]{1,0:T(8,128)(2,1)S(1)} %shard_map.100), channel_id=1, source_target_pairs={{0,16},{16,32},{32,48},{48,64},{64,80},{80,96},{96,112},{112,128},... | collective-permute-start | bytes 442376 | tf_op jit(solution)/shard_map/ppermute | solution.py:343
  7.3 22.7 %collective-permute-start.2 = (bf16[296,1152]{1,0:T(8,128)(2,1)S(1)}, bf16[296,1152]{1,0:T(8,128)(2,1)S(1)}, u32[]{:S(2)}, u32[]{:S(2)}) collective-permute-start(bf16[296,1152]{1,0:T(8,128)(2,1)S(1)} %shard_map.102.refs_2_), channel_id=1, source_target_pairs={{0,2},{2,0},{1,3},{3,1},{4,6},{6,4},{5,7},{7,5},{8,10},{10,8},{9,1... | collective-permute-start | bytes 2045960 | tf_op jit(solution)/shard_map/ppermute | solution.py:360
  10.8 20.9 %collective-permute-start.3 = (bf16[296,1152]{1,0:T(8,128)(2,1)S(1)}, bf16[296,1152]{1,0:T(8,128)(2,1)S(1)}, u32[]{:S(2)}, u32[]{:S(2)}) collective-permute-start(bf16[296,1152]{1,0:T(8,128)(2,1)S(1)} %shard_map.102.refs_2_), channel_id=1, source_target_pairs={{0,259},{1,258},{258,1},{259,0},{2,257},{3,256},{256,3},{257,2},{4... | collective-permute-start | bytes 2045960 | tf_op jit(solution)/shard_map/ppermute | solution.py:361
  13.8 16.3 %collective-permute-start.1 = (bf16[296,1152]{1,0:T(8,128)(2,1)S(1)}, bf16[296,1152]{1,0:T(8,128)(2,1)S(1)}, u32[]{:S(2)}, u32[]{:S(2)}) collective-permute-start(bf16[296,1152]{1,0:T(8,128)(2,1)S(1)} %shard_map.102.refs_2_), channel_id=1, source_target_pairs={{0,1},{1,0},{2,3},{3,2},{4,5},{5,4},{6,7},{7,6},{8,9},{9,8},{10,11... | collective-permute-start | bytes 2045960 | tf_op jit(solution)/shard_map/ppermute | solution.py:359
  32.9 22.2 %collective-permute-start.4 = (bf16[96,1152]{1,0:T(8,128)(2,1)S(1)}, bf16[96,1152]{1,0:T(8,128)(2,1)S(1)}, u32[]{:S(2)}, u32[]{:S(2)}) collective-permute-start(bf16[96,1152]{1,0:T(8,128)(2,1)S(1)} %get-tuple-element.31.refs_3_), channel_id=1, source_target_pairs={{32,64},{48,80},{64,32},{80,48},{96,128},{112,144},{128,96},{144,1... | collective-permute-start | bytes 663560 | tf_op jit(solution)/shard_map/ppermute | solution.py:412
  42.6 15.0 %collective-permute-start.5 = (bf16[96,1152]{1,0:T(8,128)(2,1)S(1)}, bf16[96,1152]{1,0:T(8,128)(2,1)S(1)}, u32[]{:S(2)}, u32[]{:S(2)}) collective-permute-start(bf16[96,1152]{1,0:T(8,128)(2,1)S(1)} %get-tuple-element.31.refs_3_), channel_id=1, source_target_pairs={{16,32},{32,16},{48,64},{64,48},{80,96},{96,80},{112,128},{128,112... | collective-permute-start | bytes 663560 | tf_op jit(solution)/shard_map/ppermute | solution.py:412
  44.5 17.6 %collective-permute-start.6 = (bf16[96,1152]{1,0:T(8,128)(2,1)S(1)}, bf16[96,1152]{1,0:T(8,128)(2,1)S(1)}, u32[]{:S(2)}, u32[]{:S(2)}) collective-permute-start(bf16[96,1152]{1,0:T(8,128)(2,1)S(1)} %get-tuple-element.31.refs_3_), channel_id=1, source_target_pairs={{0,32},{16,48},{32,0},{48,16},{64,96},{80,112},{96,64},{112,80},{1... | collective-permute-start | bytes 663560 | tf_op jit(solution)/shard_map/ppermute | solution.py:412
  46.5 15.7 %collective-permute-start.7 = (bf16[96,1152]{1,0:T(8,128)(2,1)S(1)}, bf16[96,1152]{1,0:T(8,128)(2,1)S(1)}, u32[]{:S(2)}, u32[]{:S(2)}) collective-permute-start(bf16[96,1152]{1,0:T(8,128)(2,1)S(1)} %get-tuple-element.31.refs_3_), channel_id=1, source_target_pairs={{0,16},{16,0},{32,48},{48,32},{64,80},{80,64},{96,112},{112,96},{1... | collective-permute-start | bytes 663560 | tf_op jit(solution)/shard_map/ppermute | solution.py:412
  51.8 34.2 %collective-permute-start.10 = (bf16[576,1152]{1,0:T(8,128)(2,1)S(1)}, bf16[576,1152]{1,0:T(8,128)(2,1)S(1)}, u32[]{:S(2)}, u32[]{:S(2)}) collective-permute-start(bf16[576,1152]{1,0:T(8,128)(2,1)S(1)} %get-tuple-element.43.refs_1_), channel_id=1, source_target_pairs={{0,2},{2,0},{1,3},{3,1},{4,6},{6,4},{5,7},{7,5},{8,10},{10,8},{9,1... | collective-permute-start | bytes 3981320 | tf_op jit(solution)/shard_map/ppermute | solution.py:414
  55.1 33.4 %collective-permute-start.8 = (bf16[576,1152]{1,0:T(8,128)(2,1)S(1)}, bf16[576,1152]{1,0:T(8,128)(2,1)S(1)}, u32[]{:S(2)}, u32[]{:S(2)}) collective-permute-start(bf16[576,1152]{1,0:T(8,128)(2,1)S(1)} %get-tuple-element.43.refs_1_), channel_id=1, source_target_pairs={{0,259},{1,258},{258,1},{259,0},{2,257},{3,256},{256,3},{257,2},{4... | collective-permute-start | bytes 3981320 | tf_op jit(solution)/shard_map/ppermute | solution.py:415
  59.2 26.9 %collective-permute-start.9 = (bf16[576,1152]{1,0:T(8,128)(2,1)S(1)}, bf16[576,1152]{1,0:T(8,128)(2,1)S(1)}, u32[]{:S(2)}, u32[]{:S(2)}) collective-permute-start(bf16[576,1152]{1,0:T(8,128)(2,1)S(1)} %get-tuple-element.43.refs_1_), channel_id=1, source_target_pairs={{0,1},{1,0},{2,3},{3,2},{4,5},{5,4},{6,7},{7,6},{8,9},{9,8},{10,11... | collective-permute-start | bytes 3981320 | tf_op jit(solution)/shard_map/ppermute | solution.py:437
  62.2 13.4 %copy-start = (bf16[64,1152]{1,0:T(8,128)(2,1)S(1)}, bf16[64,1152]{1,0:T(8,128)(2,1)}, u32[]{:S(2)}) copy-start(bf16[64,1152]{1,0:T(8,128)(2,1)} %get-tuple-element.40.tok_ref) | copy-start | bytes 442372
  87.5 13.5 %copy-start.1 = (bf16[48,1152]{1,0:T(8,128)(2,1)S(1)}, bf16[48,1152]{1,0:T(8,128)(2,1)}, u32[]{:S(2)}) copy-start(bf16[48,1152]{1,0:T(8,128)(2,1)} %fresh_ref.1) | copy-start | bytes 331780
